TPU v7x, 32 devices: a whole 2x2x4 slice. The times are simulated.
32 devices in a mesh: dp: 16 (over z, y, x), rep: 2 (over core).
Axes of the slice: x: 2, y: 2, z: 4, core: 2. Of those that a mesh axis runs over, the one named last changes fastest.
Arguments:
- tokens: bfloat16 [32768, 768], P(('dp', 'rep')), may hold values from -6 to 6
- cotangent: bfloat16 [32768, 768], P(('dp', 'rep')), may hold values from -6 to 6
- segments: int32 [64, 512], P(('dp', 'rep')), may hold values from 0 to 3, never falling along the last dimension, each value on 1 to 256 neighbouring positions
- live_count: int32 [32], P(('dp', 'rep')), may hold values from 1 to 2, as said below
- att_master: float32 [2363136], P('dp'), may hold values from -2 to 2, as said below
- att_first: float32 [2363136], P('dp'), may hold values from -60 to 60
- att_second: float32 [2363136], P('dp'), may hold values from 100 to 10000
- ffn_master: float32 [4723968], P('dp'), may hold values from -2 to 2, as said below
- ffn_first: float32 [4723968], P('dp'), may hold values from -60 to 60
- ffn_second: float32 [4723968], P('dp'), may hold values from 100 to 10000
Outputs:
- output: bfloat16 [32768, 768], P(('dp', 'rep'))
- input_grad: bfloat16 [32768, 768], P(('dp', 'rep'))
- att_grad: float32 [2363136], P('dp')
- att_first_new: float32 [2363136], P('dp')
- att_second_new: float32 [2363136], P('dp')
- att_delta: float32 [2363136], P('dp')
- ffn_grad: float32 [4723968], P('dp')
- ffn_first_new: float32 [4723968], P('dp')
- ffn_second_new: float32 [4723968], P('dp')
- ffn_delta: float32 [4723968], P('dp')
Inputs may be any that keep to these rules, and one draw needn't show every extreme that they name: `segments`: documents of each packed sequence are numbered in order without falling, each 1 to 256 positions long, one exactly 256. `live_count`: each device's number of its first sequence slots that are live; some device has all 2 in every draw. `att_master`: flat attention parameters in the stated layout. `ffn_master`: flat feed-forward parameters in the stated layout.
All inputs are finite; a program needn't handle non-finite values.
Results may differ from a plain program's by a relative error of at most 0.015.
The roundings to bfloat16 on the way count: a program that leaves them out, or rounds other values in their place, can miss the bound.
Values may be sent and summed in bfloat16 or wider, within the bound.
A program may use at most 256 MiB of HBM per device.

v0:
```python
import math

import jax
import jax.numpy as jnp
from jax import lax
from jax.sharding import PartitionSpec as P

D = 768
HEADS = 12
HEAD_DIM = 64
FF = 3072
STEP = 10


norm_eps = 1e-05
beta_one = 0.9
beta_two = 0.98
decay = 0.01
adam_eps = 1e-08
masked = -1e30


def split_attention(flat_params):
    qkv_weight = flat_params[: 3 * D * D].reshape(D, 3 * D)
    offset = 3 * D * D
    out_weight = flat_params[offset : offset + D * D].reshape(D, D)
    offset = offset + D * D
    att_terms = flat_params[offset : offset + 5 * D].reshape(5, D).astype(jnp.float32)
    return (qkv_weight, out_weight, att_terms)


def split_ffn(flat_params):
    in_weight = flat_params[: D * FF].reshape(D, FF)
    offset = D * FF
    down_weight = flat_params[offset : offset + FF * D].reshape(FF, D)
    offset = offset + FF * D
    in_bias = flat_params[offset : offset + FF].astype(jnp.float32)
    offset = offset + FF
    ffn_terms = flat_params[offset : offset + 3 * D].reshape(3, D).astype(jnp.float32)
    return (in_weight, down_weight, in_bias, ffn_terms)


def normalize(values, gain, shift):
    row_mean = jnp.mean(values, -1, keepdims=True)
    centred = values - row_mean
    rstd_rows = lax.rsqrt(jnp.mean(centred * centred, -1, keepdims=True) + norm_eps)
    normed = centred * rstd_rows
    return (normed * gain + shift, normed, rstd_rows)


def norm_back(grad_in, normed, rstd_rows, gain):
    scaled = grad_in * gain
    grad_rows = rstd_rows * (
        scaled
        - jnp.mean(scaled, -1, keepdims=True)
        - normed * jnp.mean(scaled * normed, -1, keepdims=True)
    )
    return (grad_rows, jnp.sum(grad_in * normed, 0), jnp.sum(grad_in, 0))


def gelu_slope(values):
    normal_cdf = 0.5 * (1.0 + lax.erf(values * 0.5**0.5))
    return normal_cdf + values * jnp.exp(-0.5 * values * values) * (2.0 * math.pi) ** (-0.5)


def masked_scores(query_rows, key_rows, seg_ids):
    scores = jnp.einsum(
        "qhd,khd->hqk", query_rows, key_rows, preferred_element_type=jnp.float32
    ) * HEAD_DIM ** (-0.5)
    same_doc = seg_ids[:, None] == seg_ids[None, :]
    return jnp.where(same_doc[None], scores, masked)


def attend_forward(block):
    query_rows, key_rows, value_rows, seg_ids = block
    scores = masked_scores(query_rows, key_rows, seg_ids)
    row_top = jnp.max(scores, -1, keepdims=True)
    raised = jnp.exp(scores - row_top)
    row_total = jnp.sum(raised, -1, keepdims=True)
    soft_probs = (raised / row_total).astype(jnp.bfloat16)
    context = jnp.einsum("hqk,khd->qhd", soft_probs, value_rows, preferred_element_type=jnp.float32)
    return (
        context.astype(jnp.bfloat16).reshape(context.shape[0], -1),
        row_top + jnp.log(row_total),
    )


def attend_backward(query_rows, key_rows, value_rows, seg_ids, log_total, grad_context):
    soft_probs = jnp.exp(masked_scores(query_rows, key_rows, seg_ids) - log_total)
    grad_probs = jnp.einsum(
        "qhd,khd->hqk", grad_context, value_rows, preferred_element_type=jnp.float32
    )
    grad_values = jnp.einsum(
        "hqk,qhd->khd",
        soft_probs.astype(jnp.bfloat16),
        grad_context,
        preferred_element_type=jnp.float32,
    )
    grad_scores = soft_probs * (grad_probs - jnp.sum(soft_probs * grad_probs, -1, keepdims=True))
    grad_scores = grad_scores.astype(jnp.bfloat16)
    grad_queries = jnp.einsum(
        "hqk,khd->qhd", grad_scores, key_rows, preferred_element_type=jnp.float32
    ) * HEAD_DIM ** (-0.5)
    grad_keys = jnp.einsum(
        "hqk,qhd->khd", grad_scores, query_rows, preferred_element_type=jnp.float32
    ) * HEAD_DIM ** (-0.5)
    length_here = query_rows.shape[0]
    return jnp.concatenate(
        [
            grad_queries.reshape(length_here, -1),
            grad_keys.reshape(length_here, -1),
            grad_values.reshape(length_here, -1),
        ],
        -1,
    )


def adam_update(master, first, second, grad):
    first_new = beta_one * first + (1.0 - beta_one) * grad
    second_new = beta_two * second + (1.0 - beta_two) * grad * grad
    fix_one = 1.0 - beta_one**STEP
    fix_two = 1.0 - beta_two**STEP
    update = first_new / fix_one / (jnp.sqrt(second_new / fix_two) + adam_eps)
    return (first_new, second_new, update + decay * master)


def body(
    tokens,
    cotangent,
    segments,
    live_count,
    att_master,
    att_first,
    att_second,
    ffn_master,
    ffn_first,
    ffn_second,
):
    seq_count = segments.shape[0]
    length = segments.shape[1]
    att_full = lax.all_gather(att_master.astype(jnp.bfloat16), "dp", axis=0, tiled=True)
    qkv_weight, out_weight, att_terms = split_attention(att_full)
    bias_qkv = jnp.concatenate([att_terms[0], jnp.zeros_like(att_terms[0]), att_terms[1]])
    qkv = (jnp.dot(tokens, qkv_weight, preferred_element_type=jnp.float32) + bias_qkv).astype(
        jnp.bfloat16
    )
    head_split = qkv.reshape(seq_count, length, 3, HEADS, HEAD_DIM)
    context, log_total = lax.map(
        attend_forward, (head_split[:, :, 0], head_split[:, :, 1], head_split[:, :, 2], segments)
    )
    context = context.reshape(-1, D)
    residual = (
        tokens.astype(jnp.float32)
        + jnp.dot(context, out_weight, preferred_element_type=jnp.float32)
        + att_terms[2]
    )
    first_out, first_hat, first_rstd = normalize(residual, att_terms[3], att_terms[4])
    ffn_full = lax.all_gather(ffn_master.astype(jnp.bfloat16), "dp", axis=0, tiled=True)
    in_weight, down_weight, in_bias, ffn_terms = split_ffn(ffn_full)
    first_low = first_out.astype(jnp.bfloat16)
    ffn_inner = jnp.dot(first_low, in_weight, preferred_element_type=jnp.float32) + in_bias
    ffn_act = jax.nn.gelu(ffn_inner, approximate=False).astype(jnp.bfloat16)
    second_in = (
        first_out + jnp.dot(ffn_act, down_weight, preferred_element_type=jnp.float32) + ffn_terms[0]
    )
    output, second_hat, second_rstd = normalize(second_in, ffn_terms[1], ffn_terms[2])
    att_back = lax.all_gather(att_master.astype(jnp.bfloat16), "dp", axis=0, tiled=True)
    qkv_weight, out_weight, att_terms = split_attention(att_back)
    ffn_back = lax.all_gather(ffn_master.astype(jnp.bfloat16), "dp", axis=0, tiled=True)
    in_weight, down_weight, in_bias, ffn_terms = split_ffn(ffn_back)

    def microbatch(micro_index, state_now):
        grad_sums, input_grads = state_now

        def take_rows(array_in):
            return lax.dynamic_slice_in_dim(array_in, micro_index * length, length, 0)

        grad_out = take_rows(cotangent).astype(jnp.float32)
        grad_second, grad_gain_two, grad_shift_two = norm_back(
            grad_out, take_rows(second_hat), take_rows(second_rstd), ffn_terms[1]
        )
        grad_down = grad_second.astype(jnp.bfloat16)
        grad_down_bias = jnp.sum(grad_down.astype(jnp.float32), 0)
        grad_down_weight = jnp.dot(
            take_rows(ffn_act).T, grad_down, preferred_element_type=jnp.float32
        )
        grad_act = jnp.dot(grad_down, down_weight.T, preferred_element_type=jnp.float32)
        grad_inner = (grad_act * gelu_slope(take_rows(ffn_inner))).astype(jnp.bfloat16)
        grad_in_bias = jnp.sum(grad_inner.astype(jnp.float32), 0)
        grad_in_weight = jnp.dot(
            take_rows(first_low).T, grad_inner, preferred_element_type=jnp.float32
        )
        grad_first = grad_second + jnp.dot(
            grad_inner, in_weight.T, preferred_element_type=jnp.float32
        )
        grad_residual, grad_gain_one, grad_shift_one = norm_back(
            grad_first, take_rows(first_hat), take_rows(first_rstd), att_terms[3]
        )
        grad_proj = grad_residual.astype(jnp.bfloat16)
        grad_out_bias = jnp.sum(grad_proj.astype(jnp.float32), 0)
        grad_out_weight = jnp.dot(
            take_rows(context).T, grad_proj, preferred_element_type=jnp.float32
        )
        grad_context = jnp.dot(grad_proj, out_weight.T, preferred_element_type=jnp.float32).astype(
            jnp.bfloat16
        )
        this_seq = lax.dynamic_index_in_dim(head_split, micro_index, 0, keepdims=False)
        this_segs = lax.dynamic_index_in_dim(segments, micro_index, 0, keepdims=False)
        this_total = lax.dynamic_index_in_dim(log_total, micro_index, 0, keepdims=False)
        grad_qkv = attend_backward(
            this_seq[:, 0],
            this_seq[:, 1],
            this_seq[:, 2],
            this_segs,
            this_total,
            grad_context.reshape(length, HEADS, HEAD_DIM),
        )
        grad_qkv = grad_qkv.astype(jnp.bfloat16)
        grad_wide = grad_qkv.astype(jnp.float32)
        grad_query_bias = jnp.sum(grad_wide[:, :D], 0)
        grad_value_bias = jnp.sum(grad_wide[:, 2 * D :], 0)
        grad_qkv_weight = jnp.dot(take_rows(tokens).T, grad_qkv, preferred_element_type=jnp.float32)
        grad_tokens = (
            jnp.dot(grad_qkv, qkv_weight.T, preferred_element_type=jnp.float32) + grad_residual
        )
        input_grads = lax.dynamic_update_slice_in_dim(
            input_grads, grad_tokens.astype(jnp.bfloat16), micro_index * length, 0
        )
        terms_now = (
            grad_qkv_weight,
            grad_out_weight,
            grad_query_bias,
            grad_value_bias,
            grad_out_bias,
            grad_gain_one,
            grad_shift_one,
            grad_in_weight,
            grad_down_weight,
            grad_in_bias,
            grad_down_bias,
            grad_gain_two,
            grad_shift_two,
        )
        grad_sums = tuple((running + fresh for running, fresh in zip(grad_sums, terms_now)))
        return (grad_sums, input_grads)

    zero_sums = (
        jnp.zeros((D, 3 * D), jnp.float32),
        jnp.zeros((D, D), jnp.float32),
        jnp.zeros((D,), jnp.float32),
        jnp.zeros((D,), jnp.float32),
        jnp.zeros((D,), jnp.float32),
        jnp.zeros((D,), jnp.float32),
        jnp.zeros((D,), jnp.float32),
        jnp.zeros((D, FF), jnp.float32),
        jnp.zeros((FF, D), jnp.float32),
        jnp.zeros((FF,), jnp.float32),
        jnp.zeros((D,), jnp.float32),
        jnp.zeros((D,), jnp.float32),
        jnp.zeros((D,), jnp.float32),
    )
    zero_inputs = jnp.zeros(tokens.shape, jnp.bfloat16)
    grad_sums, input_grad = lax.fori_loop(0, live_count[0], microbatch, (zero_sums, zero_inputs))
    dp_count = lax.axis_size("dp")
    att_pad = att_master.shape[0] * dp_count - 4 * D * D - 5 * D
    ffn_pad = ffn_master.shape[0] * dp_count - 2 * D * FF - FF - 3 * D
    att_local = jnp.concatenate(
        [
            grad_sums[0].reshape(-1),
            grad_sums[1].reshape(-1),
            grad_sums[2],
            grad_sums[3],
            grad_sums[4],
            grad_sums[5],
            grad_sums[6],
            jnp.zeros((att_pad,), jnp.float32),
        ]
    )
    ffn_local = jnp.concatenate(
        [
            grad_sums[7].reshape(-1),
            grad_sums[8].reshape(-1),
            grad_sums[9],
            grad_sums[10],
            grad_sums[11],
            grad_sums[12],
            jnp.zeros((ffn_pad,), jnp.float32),
        ]
    )
    att_rows, ffn_rows = (
        lax.all_to_all(
            att_local.reshape(dp_count, -1).astype(jnp.bfloat16),
            "dp",
            split_axis=0,
            concat_axis=0,
            tiled=True,
        ).astype(jnp.float32),
        lax.all_to_all(
            ffn_local.reshape(dp_count, -1).astype(jnp.bfloat16),
            "dp",
            split_axis=0,
            concat_axis=0,
            tiled=True,
        ).astype(jnp.float32),
    )
    att_share = jnp.sum(att_rows, 0)
    ffn_share = jnp.sum(ffn_rows, 0)
    att_grad, ffn_grad = (
        lax.psum(att_share.astype(jnp.bfloat16), "rep").astype(jnp.float32),
        lax.psum(ffn_share.astype(jnp.bfloat16), "rep").astype(jnp.float32),
    )
    att_new = adam_update(att_master, att_first, att_second, att_grad)
    ffn_new = adam_update(ffn_master, ffn_first, ffn_second, ffn_grad)
    return (
        output.astype(jnp.bfloat16),
        input_grad,
        att_grad,
        att_new[0],
        att_new[1],
        att_new[2],
        ffn_grad,
        ffn_new[0],
        ffn_new[1],
        ffn_new[2],
    )


def solution(mesh):
    placed = (
        P(("dp", "rep"), None),
        P(("dp", "rep"), None),
        P(("dp", "rep"), None),
        P(("dp", "rep")),
        P("dp"),
        P("dp"),
        P("dp"),
        P("dp"),
        P("dp"),
        P("dp"),
    )
    return jax.shard_map(
        body,
        mesh=mesh,
        in_specs=placed,
        out_specs=(
            P(("dp", "rep"), None),
            P(("dp", "rep"), None),
            P("dp"),
            P("dp"),
            P("dp"),
            P("dp"),
            P("dp"),
            P("dp"),
            P("dp"),
            P("dp"),
        ),
        check_vma=False,
    )
```

profile of v0, /device:TPU:0, one launch (start us, length us, event | category | flops | bytes accessed | tf_op | source)
XLA Modules:
  0.0 1638.7 jit_solution(14180808061810777754)
XLA Ops:
  14.8 5.8 dynamic-update-slice
  20.6 4.1 broadcast.180
  24.7 10.2 dynamic-update-slice.1
  38.1 397.8 %all-reduce.7.cloned.1.call-done = (bf16[2363136]{0:T(1024)(128)(2,1)}, bf16[4723968]{0:T(1024)(128)(2,1)}) async-done(((bf16[2363136]{0:T(1024)(128)(2,1)}, bf16[4723968]{0:T(1024)(128)(2,1)}), (bf16[2363136]{0:T(1024)(128)(2,1)}, bf16[4723968]{0:T(1024)(128)(2,1)})) %all-reduce.7.cloned.1.call-update) | async-done | bytes 14174224
  439.1 8.2 fusion.70
  455.0 7.6 reshape.307
  462.6 8.2 fusion.63
  470.8 8.8 reshape.308
  479.6 5.7 copy.61
  485.3 4.9 fusion.71
  490.1 9.2 slice.140
  502.7 8.2 reshape.310
  515.6 25.5 %while.49 = (s32[]{:T(128)}, bf16[2,512,768]{2,1,0:T(8,128)(2,1)}, f32[2,12,512,1]{2,1,3,0:T(8,128)S(1)}, bf16[2,512,12,64]{1,3,2,0:T(8,128)(2,1)}, s32[2,512]{1...) while((s32[]{:T(128)}, bf16[2,512,768]{2,1,0:T(8,128)(2,1)}, ...), condition=%wide.region_3.4_spmd, body=%wide.region_0.3_spmd.sunk | while | flops 843704320 | bytes 45317228 | solution.py:148
  522.5 4.7 fusion.124
  535.1 4.7 fusion.124
  541.1 3.8 fusion.74
  549.4 36.8 %fusion.55 = (bf16[1024,3072]{1,0:T(8,128)(2,1)S(1)}, f32[1024,3072]{1,0:T(8,128)}) fusion(f32[3072]{0:T(1024)S(1)} %copy-done.41, bf16[1024,768]{0,1:T(8,128)(2,1)S(1)} %get-tuple-element.933, bf16[768,3072]{1,0:T(8,128)(2,1)S(1)} %copy-done.19), kind=kOutput, calls=%fused_computation.103 | convolution fusion | flops 5039456256 | bytes 25178112 | tf_op jit(solution)/shard_map/dot_general | solution.py:161
  586.4 5.7 fusion.75
  604.9 4.8 broadcast_in_dim.77
  609.6 4.3 broadcast_in_dim.78
  613.9 99.5 %while.50 = (s32[]{:T(128)}, f32[768,2304]{1,0:T(8,128)}, f32[768,768]{1,0:T(8,128)}, f32[768]{0:T(1024)S(1)}, f32[768]{0:T(1024)}, /*index=5*/f32[768]{0:T(1024...) while((s32[]{:T(128)}, f32[768,2304]{1,0:T(8,128)}, ...), condition=%wide.region_23.24_spmd, body=%wide.region_8.23_spmd.sunk | while | flops 16621890560 | bytes 453741824 | solution.py:263
  635.1 7.1 convert_reduce_fusion.8
  651.6 4.7 convolution_add_fusion.10
  656.4 7.5 convolution_add_fusion.11
  663.9 7.5 convolution_add_fusion.12
  676.4 7.0 multiply_reduce_fusion.9
  683.4 7.0 multiply_convert_fusion.6
  724.7 5.1 convert.60
  729.8 6.4 reshape.311
  738.2 4.7 convert_bitcast_fusion
  746.4 6.3 convert.68
  752.7 9.3 reshape.314
  769.9 11.0 convert_element_type.135
  781.4 101.8 %reduce.8 = bf16[16,147696]{1,0:T(8,128)(2,1)} reduce(bf16[16,1,147696]{2,1,0:T(2,128)(2,1)} %convert_element_type.135, bf16[]{:T(256)} %broadcast.215), dimensions={1}, to_apply=%convert_element_type.135.reduce_sub_computation | reduce | bytes 9452546 | tf_op jit(solution)/shard_map/convert_element_type | solution.py:292
  883.2 6.1 reshape.329
  889.3 92.2 %all-to-all-start = ((bf16[16,2,73848]{2,1,0:T(2,128)(2,1)}), bf16[16,2,73848]{2,1,0:T(2,128)(2,1)}, u32[]{:S(2)}, u32[]{:S(2)}) async-start(bf16[16,2,73848]{2,1,0:T(2,128)(2,1)} %reshape.329), calls=%async_computation | async-start | bytes 9453568 | tf_op jit(solution)/shard_map/all_to_all | solution.py:291
  981.5 5.4 constant_dynamic-update-slice_fusion.2
  986.9 5.4 constant_dynamic-update-slice_fusion.5
  998.5 7.5 reshape_dynamic-update-slice_fusion
  1006.0 74.4 %while.51 = (u32[]{:T(128)}, bf16[4723968]{0:T(1024)(128)(2,1)}, bf16[16,1,295248]{2,1,0:T(2,128)(2,1)}, u32[]{}, u32[]{}, /*index=5*/u32[]{}) while((u32[]{:T(128)}, bf16[4723968]{0:T(1024)(128)(2,1)}, bf16[16,1,295248]{2,1,0:T(2,128)(2,1)}, u32[]{}, u32[]{}, /*index=5*/u32[]{}) %tuple.116), condition=%wide.cond, body=%wide.body.sunk | while | flops 9 | bytes 12401165
  1006.0 3.6 dynamic-slice.4
  1009.6 5.9 reshape.335
  1015.5 5.3 constant_dynamic-update-slice_fusion.10
  1020.8 3.6 dynamic-slice.4
  1024.5 5.9 reshape.335
  1030.4 5.3 constant_dynamic-update-slice_fusion.10
  1035.7 3.6 dynamic-slice.4
  1039.3 5.9 reshape.335
  1045.2 5.3 constant_dynamic-update-slice_fusion.10
  1050.5 3.6 dynamic-slice.4
  1054.2 5.9 reshape.335
  1060.1 5.4 constant_dynamic-update-slice_fusion.10
  1065.5 3.6 dynamic-slice.4
  1069.1 5.9 reshape.335
  1075.0 5.3 constant_dynamic-update-slice_fusion.10
  1080.3 200.3 %reduce.9 = bf16[16,295248]{1,0:T(8,128)(2,1)} reduce(bf16[16,1,295248]{2,1,0:T(2,128)(2,1)} %get-tuple-element.394, bf16[]{:T(256)} %broadcast.215), dimensions={1}, to_apply=%get-tuple-element.394.reduce_sub_computation | reduce | bytes 18895874 | tf_op jit(solution)/shard_map/convert_element_type | solution.py:299
  1280.6 17.5 %reshape.331 = bf16[16,2,147624]{2,1,0:T(2,128)(2,1)} reshape(bf16[16,295248]{1,0:T(8,128)(2,1)} %reduce.9) | data formatting | bytes 18895872
  1298.2 7.0 all-to-all-start.1
  1305.3 18.8 %reshape.330 = bf16[16,1,147696]{2,1,0:T(2,128)(2,1)} reshape(bf16[16,2,73848]{2,1,0:T(2,128)(2,1)} %all-to-all-done) | data formatting | bytes 9452544
  1324.1 14.5 reduce_sum.199
  1338.5 144.9 %all-to-all-done.1 = bf16[16,2,147624]{2,1,0:T(2,128)(2,1)} async-done(((bf16[16,2,147624]{2,1,0:T(2,128)(2,1)}), bf16[16,2,147624]{2,1,0:T(2,128)(2,1)}, u32[]{:S(2)}, u32[]{:S(2)}) %all-to-all-start.1) | async-done | bytes 9447968 | tf_op jit(solution)/shard_map/all_to_all | solution.py:298
  1483.4 34.2 %reshape.332 = bf16[16,1,295248]{2,1,0:T(2,128)(2,1)} reshape(bf16[16,2,147624]{2,1,0:T(2,128)(2,1)} %all-to-all-done.1) | data formatting | bytes 18895872
  1517.6 51.4 %reduce_sum.200 = bf16[295248]{0:T(1024)(128)(2,1)} reduce(bf16[16,1,295248]{2,1,0:T(2,128)(2,1)} %reshape.332, bf16[]{:T(256)} %constant.85.clone.1), dimensions={0,1}, to_apply=%region_26.27 | reduce | flops 4428720 | bytes 10038434 | tf_op jit(solution)/shard_map/reduce_sum | solution.py:307
  1570.7 55.6 %all-reduce.9.cloned.1.call-done = (bf16[147696]{0:T(1024)(128)(2,1)}, bf16[295248]{0:T(1024)(128)(2,1)}) async-done(((bf16[147696]{0:T(1024)(128)(2,1)}, bf16[295248]{0:T(1024)(128)(2,1)}), (bf16[147696]{0:T(1024)(128)(2,1)}, bf16[295248]{0:T(1024)(128)(2,1)})) %all-reduce.9.cloned.1.call-update) | async-done | bytes 885904 | tf_op jit(solution)/shard_map/psum | solution.py:309
  (243 shorter events, 147.7 us)
Async XLA Ops:
  7.2 428.7 %all-reduce.7.cloned.1.call-start = ((), (), s32[]{:S(2)}) async-start(), calls=%async_computation.2 | async-start | bytes 28352512
  35.0 1.4 copy-start.13
  462.6 8.2 copy-start.29
  479.6 5.7 copy-start.9
  515.6 25.5 %copy-start.49 = (f32[768]{0:T(1024)S(1)}, f32[768]{0:T(1024)}, u32[]{:S(2)}) copy-start(f32[768]{0:T(1024)} %get-tuple-element.533) | copy-start | bytes 9220
  541.1 4.3 copy-start.37
  541.1 4.3 copy-start.38
  545.4 4.0 copy-start.19
  545.4 4.0 copy-start.41
  545.4 40.9 %slice-start.4 = ((s8[4718592]{0:T(1024)(128)(4,1)}), s8[4194304]{0:T(1024)(128)(4,1)S(1)}, s32[]{:S(2)}) async-start(s8[4718592]{0:T(1024)(128)(4,1)} %bitcast.166), calls=%async_computation.8 | async-start | bytes 8388608
  546.0 40.3 %copy-start.15 = (bf16[1024,768]{0,1:T(8,128)(2,1)}, bf16[1024,768]{0,1:T(8,128)(2,1)S(1)}, u32[]{:S(2)}) copy-start(bf16[1024,768]{0,1:T(8,128)(2,1)S(1)} %get-tuple-element.933) | copy-start | bytes 4718596
  546.0 40.3 %copy-start.11 = (f32[1024,768]{0,1:T(8,128)}, f32[1024,768]{0,1:T(8,128)S(1)}, u32[]{:S(2)}) copy-start(f32[1024,768]{0,1:T(8,128)S(1)} %get-tuple-element.930) | copy-start | bytes 9437188
  549.4 36.9 %slice-start.5 = ((s8[4718592]{0:T(1024)(128)(4,1)}), s8[524288]{0:T(1024)(128)(4,1)S(1)}, s32[]{:S(2)}) async-start(s8[4718592]{0:T(1024)(128)(4,1)} %bitcast.166), calls=%async_computation.9 | async-start | bytes 1048576
  549.4 36.9 %copy-start.50 = (f32[768]{0:T(1024)S(1)}, f32[768]{0:T(1024)}, u32[]{:S(2)}) copy-start(f32[768]{0:T(1024)} %get-tuple-element.538) | copy-start | bytes 9220
  586.3 5.8 copy-start.10
  586.3 6.2 copy-start.39
  586.3 6.2 copy-start.40
  609.6 4.3 copy-start.30
  614.7 7.3 copy-start.33
  614.8 7.3 copy-start.35
  614.8 3.8 copy-start.12
  630.3 11.9 slice-start.6
  632.5 9.7 copy-start.1
  635.1 7.2 copy-start.3
  635.1 7.2 slice-start.7
  642.2 3.1 copy-start.7
  645.3 4.3 copy-start.27
  645.8 3.9 copy-start.4
  651.6 4.7 copy-start.8
  651.6 4.7 copy-start.16
  651.6 12.3 slice-start.2
  656.4 7.5 copy-start.2
  656.4 7.5 slice-start.3
  671.4 1.8 copy-start.6
  690.4 3.2 copy-start.21
  691.6 2.1 copy-start.5
  691.6 2.1 copy-start.23
  691.6 5.5 slice-start
  693.6 3.5 slice-start.1
  695.7 1.4 copy-start.24
  695.7 1.4 copy-start.31
  695.7 2.0 copy-start.14
  697.7 3.6 copy-start.32
  697.7 6.5 copy-start.34
  697.7 6.5 copy-start.36
  701.3 2.9 copy-start
  752.7 9.4 copy-start.20
  752.7 10.4 copy-start.48
  752.7 11.8 copy-start.47
  752.7 13.2 copy-start.46
  752.7 14.5 copy-start.45
  889.3 408.9 %all-to-all-start = ((bf16[16,2,73848]{2,1,0:T(2,128)(2,1)}), bf16[16,2,73848]{2,1,0:T(2,128)(2,1)}, u32[]{:S(2)}, u32[]{:S(2)}) async-start(bf16[16,2,73848]{2,1,0:T(2,128)(2,1)} %reshape.329), calls=%async_computation | async-start | bytes 9453568 | tf_op jit(solution)/shard_map/all_to_all | solution.py:291
  986.9 6.0 copy-start.44
  986.9 7.4 copy-start.43
  986.9 8.8 copy-start.42
  1298.2 185.3 %all-to-all-start.1 = ((bf16[16,2,147624]{2,1,0:T(2,128)(2,1)}), bf16[16,2,147624]{2,1,0:T(2,128)(2,1)}, u32[]{:S(2)}, u32[]{:S(2)}) async-start(bf16[16,2,147624]{2,1,0:T(2,128)(2,1)} %reshape.331), calls=%async_computation.1 | async-start | bytes 18907136 | tf_op jit(solution)/shard_map/all_to_all | solution.py:298
  1305.2 321.0 %all-reduce.9.cloned.1.call-start = ((), (), s32[]{:S(2)}) async-start(), calls=%async_computation.3 | async-start | bytes 1777664 | tf_op jit(solution)/shard_map/psum | solution.py:309
  1517.6 51.4 %copy-start.17 = (bf16[1024,768]{0,1:T(8,128)(2,1)S(1)}, bf16[1024,768]{0,1:T(8,128)(2,1)}, u32[]{:S(2)}) copy-start(bf16[1024,768]{0,1:T(8,128)(2,1)} %get-tuple-element.511) | copy-start | bytes 4718596
  1517.6 108.6 %copy-start.22 = (f32[147696]{0:T(1024)S(1)}, f32[147696]{0:T(1024)}, u32[]{:S(2)}) copy-start(f32[147696]{0:T(1024)} %param.18) | copy-start | bytes 1772356
  1569.0 60.2 %copy-start.18 = (f32[295248]{0:T(1024)S(1)}, f32[295248]{0:T(1024)}, u32[]{:S(2)}) copy-start(f32[295248]{0:T(1024)} %param.21) | copy-start | bytes 3542980
  1570.6 58.6 %copy-start.25 = (f32[295248]{0:T(1024)S(1)}, f32[295248]{0:T(1024)}, u32[]{:S(2)}) copy-start(f32[295248]{0:T(1024)} %param.23) | copy-start | bytes 3542980
  1626.2 3.0 copy-start.26
  1626.2 3.0 copy-start.28
Sparse Core Ops, SparseCore 0:
  35.1 400.7 all-reduce.6
  1569.2 57.0 all-reduce.8
where the time goes:
time: 1650 us; the launch traced here: 1640 us
  waiting for transfers between devices  598 us (36%)
  other arithmetic  435 us (26%)
  local copies, waits for them, and re-layouts  358 us (22%)
  matrix products  122 us (7%)
  starting transfers between devices  99.4 us (6%)
    unnamed x3, waiting for transfers between devices  398 us
    unnamed x102, local copies, waits for them, and re-layouts  219 us
    convert_element_type x1, other arithmetic, body(): ffn_local.reshape(dp_count, -1).astype(jnp.bfloat16)  200 us
    all_to_all x1, waiting for transfers between devices, body(): lax.all_to_all(ffn_local.reshape(dp_count, -1).astype(jnp.bfloat16), 'dp'...  145 us
    convert_element_type x1, other arithmetic, body(): att_local.reshape(dp_count, -1).astype(jnp.bfloat16)  102 us
    all_to_all x1, starting transfers between devices, body(): lax.all_to_all(att_local.reshape(dp_count, -1).astype(jnp.bfloat16), 'dp'...  92.2 us
    psum x1, waiting for transfers between devices, body(): lax.psum(att_share.astype(jnp.bfloat16), 'rep').astype(jnp.float32)  55.6 us
    reduce_sum x1, other arithmetic, body(): ffn_share = jnp.sum(ffn_rows, 0)  51.4 us
  transfers between devices with their start and end apart: 4, of which 3 were waited for; matrix products, arithmetic and copies ran while one was open for 22% of the time, Pallas kernels for 0%

commit v1 on v0

--- a/solution.py
+++ b/solution.py
@@ -1,8 +1,11 @@
+import functools
 import math
 
 import jax
 import jax.numpy as jnp
 from jax import lax
+from jax.experimental import pallas as pl
+from jax.experimental.pallas import tpu as pltpu
 from jax.sharding import PartitionSpec as P
 
 D = 768
@@ -124,7 +127,7 @@
     return (first_new, second_new, update + decay * master)
 
 
-def body(
+def general_body(
     tokens,
     cotangent,
     segments,
@@ -325,6 +328,788 @@
     )
 
 
+MESH_ID = pl.DeviceIdType.MESH
+
+
+def when(cond, act):
+    if cond is None:
+        act()
+    else:
+        pl.when(cond)(act)
+
+
+class Place:
+    def __init__(self, levels):
+        self.levels = levels
+        d = lax.axis_index("dp")
+        c = lax.axis_index("rep")
+        self.d, self.c = d, c
+        self.z, y, x = d // 4, (d // 2) % 2, d % 2
+        x_near, y_near = d + 1 - 2 * x, d + 2 - 4 * y
+        self.a_near = x_near + c * (y_near - x_near)
+        self.b_near = y_near + c * (x_near - y_near)
+        self.far = x_near + y_near - d
+        self.a_at = x + c * (y - x)
+        self.b_at = y + c * (x - y)
+        self.up = (d + 4, c)
+        self.down = (d - 4, c)
+        self.has_up = self.z < levels - 1
+        self.has_down = self.z > 0
+        self.across_a = (self.a_near, c)
+        self.across_b = (self.b_near, c)
+        self.sibling = (d, 1 - c)
+
+    def levels_at(self, distance):
+        if distance == 0:
+            return [(self.z, None, 0)]
+        return [
+            (self.z - distance, self.z >= distance, -1),
+            (self.z + distance, self.z + distance < self.levels, 1),
+        ]
+
+    def at(self, column, level):
+        return column + 4 * (level - self.z)
+
+    def along(self, step):
+        return (self.up, self.has_up) if step > 0 else (self.down, self.has_down)
+
+    def meet(self, chain):
+        barrier = pltpu.get_barrier_semaphore()
+
+        def greet(device):
+            pl.semaphore_signal(barrier, inc=1, device_id=device, device_id_type=MESH_ID)
+
+        for device in (self.across_a, self.across_b, self.sibling):
+            greet(device)
+        count = 3
+        edges = [(self.up, self.has_up), (self.down, self.has_down)]
+        if chain:
+            edges += [((self.d + 1, self.c), self.d < 4 * self.levels - 1), ((self.d - 1, self.c), self.d > 0)]
+        for device, there in edges:
+            pl.when(there)(functools.partial(greet, device))
+            count = count + there.astype(jnp.int32)
+        pl.semaphore_wait(barrier, count)
+
+
+def both(first, second):
+    if first is None:
+        return second
+    return first if second is None else first & second
+
+
+class Sends:
+    def __init__(self):
+        self.open = []
+
+    def start(self, cond, make):
+        when(cond, lambda: make().start())
+        self.open.append((cond, make))
+
+    def finish(self):
+        for cond, make in self.open:
+            when(cond, lambda make=make: make().wait_send())
+        self.open = []
+
+
+def remote(src, dst, send_sem, recv_sem, device):
+    return pltpu.make_async_remote_copy(
+        src_ref=src,
+        dst_ref=dst,
+        send_sem=send_sem,
+        recv_sem=recv_sem,
+        device_id=device,
+        device_id_type=MESH_ID,
+    )
+
+
+class Gather:
+    def __init__(self, place, sends, ref, send_sem, recv_sem):
+        self.place, self.sends, self.ref = place, sends, ref
+        self.send_sem, self.recv_sem = send_sem, recv_sem
+        self.half = ref.shape[2] // 2
+
+    def piece(self, chip, core):
+        rows = pl.ds(pl.multiple_of(core * self.half, self.half), self.half)
+        return self.ref.at[chip, :, rows, :]
+
+    def copy(self, chip, way, device):
+        own = self.piece(chip, self.place.c)
+        kind = 1 if way == 4 else 0
+        return remote(own, own, self.send_sem.at[way, chip], self.recv_sem.at[kind, chip], device)
+
+    def send(self, cond, chip, way, device):
+        self.sends.start(cond, lambda: self.copy(chip, way, device))
+
+    def arrived(self, cond, chip, kind=0):
+        p = self.place
+        part = self.piece(chip, p.c if kind == 0 else 1 - p.c)
+        make = lambda: remote(part, part, self.send_sem.at[0, chip], self.recv_sem.at[kind, chip], p.sibling)
+        when(cond, lambda: make().wait_recv())
+
+    def own(self):
+        p = self.place
+        self.send(None, p.d, 3, p.across_b)
+        self.send(None, p.d, 2, p.across_a)
+        self.send(p.has_up, p.d, 0, p.up)
+        self.send(p.has_down, p.d, 1, p.down)
+
+    def line(self, distance):
+        p = self.place
+        for level, there, step in p.levels_at(distance):
+            chip = p.at(p.d, level)
+            self.arrived(there, chip)
+            onward, more = p.along(-step)
+            self.send(both(there, more), chip, 0, onward)
+            self.send(there, chip, 3, p.across_b)
+            self.send(there, chip, 2, p.across_a)
+            self.send(there, chip, 4, p.sibling)
+
+    def over_a(self, distance):
+        p = self.place
+        for level, there, _ in p.levels_at(distance):
+            chip = p.at(p.a_near, level)
+            self.arrived(there, chip)
+            self.send(there, chip, 3, p.across_b)
+            self.send(there, chip, 4, p.sibling)
+
+    def over_b(self, column, distance):
+        p = self.place
+        for level, there, _ in p.levels_at(distance):
+            chip = p.at(column, level)
+            self.arrived(there, chip)
+            self.send(there, chip, 4, p.sibling)
+
+    def steps(self):
+        p = self.place
+        todo = [self.own]
+        for distance in range(p.levels + 2):
+            if 0 < distance < p.levels:
+                todo.append(functools.partial(self.line, distance))
+            if 0 <= distance - 1 < p.levels:
+                todo.append(functools.partial(self.over_a, distance - 1))
+            if 0 <= distance - 1 < p.levels:
+                todo.append(functools.partial(self.over_b, p.b_near, distance - 1))
+            if 0 <= distance - 2 < p.levels:
+                todo.append(functools.partial(self.over_b, p.far, distance - 2))
+        return todo
+
+    def from_sibling(self):
+        p = self.place
+        for column in (p.d, p.a_near, p.b_near, p.far):
+            for distance in range(p.levels):
+                for level, there, _ in p.levels_at(distance):
+                    if column is p.d and distance == 0:
+                        continue
+                    self.arrived(there, p.at(column, level), 1)
+
+
+class Spread:
+    def __init__(self, place, sends, ref, send_sem, recv_sem):
+        self.place, self.sends, self.ref = place, sends, ref
+        self.send_sem, self.recv_sem = send_sem, recv_sem
+
+    def copy(self, way, device):
+        return remote(self.ref, self.ref, self.send_sem.at[way], self.recv_sem, device)
+
+    def wait(self, cond):
+        when(cond, lambda: self.copy(0, self.place.sibling).wait_recv())
+
+    def run(self):
+        p = self.place
+        home = (p.a_at == 1) & (p.b_at == 1)
+        self.wait(home & p.has_up)
+        self.sends.start(home & p.has_down, lambda: self.copy(0, p.down))
+        self.wait((p.a_at == 0) & (p.b_at == 1))
+        self.sends.start(home, lambda: self.copy(1, p.across_a))
+        self.wait(p.b_at == 0)
+        self.sends.start(p.b_at == 1, lambda: self.copy(2, p.across_b))
+
+
+def shifted(ref, start, rows):
+    first, turn = start // 128, start % 128
+    here = pltpu.roll(ref[pl.ds(first, rows), :], (128 - turn) % 128, 1)
+    after = pltpu.roll(ref[pl.ds(first + 1, rows), :], (128 - turn) % 128, 1)
+    lane = lax.broadcasted_iota(jnp.int32, (rows, 128), 1)
+    return jnp.where(lane < 128 - turn, here, after)
+
+
+class Flat:
+    def __init__(self, length, chips, parts, split):
+        self.length, self.chips, self.parts = length, chips, parts
+        self.rows = length // D // parts * parts
+        self.slip = length - self.rows * D
+        self.deep = self.rows // parts
+        self.split = split
+        self.lines = self.rows * (D // 128)
+        self.most = self.slip * chips
+        self.halo = -(-self.most // 1024) * 8
+        self.held = -(-length // 1024) * 8
+        self.tail_from = (length - self.most) // 1024 * 8
+        self.tail = self.held - self.tail_from
+
+    def place_of(self, part, block, split):
+        if split:
+            return 6 * part + block, 6 * self.parts
+        return 6 * self.deep * part + block, 6
+
+
+class Lead:
+    def __init__(self, place, sends, flat, own_ref, long_ref, halo_ref, line_ref, send_sem, recv_sem):
+        self.place, self.sends, self.flat = place, sends, flat
+        self.own_ref, self.long_ref, self.halo_ref, self.line_ref = own_ref, long_ref, halo_ref, line_ref
+        self.send_sem, self.recv_sem = send_sem, recv_sem
+
+    def copy(self):
+        f, p = self.flat, self.place
+        return remote(
+            self.own_ref.at[pl.ds(f.tail_from, f.tail), :],
+            self.halo_ref.at[pl.ds(0, f.tail), :],
+            self.send_sem,
+            self.recv_sem,
+            (p.d + 1, p.c),
+        )
+
+    def begin(self):
+        p, f = self.place, self.flat
+        self.sends.start(p.d < f.chips - 1, self.copy)
+        self.long_ref[pl.ds(f.halo, f.held), :] = self.own_ref[...]
+
+    def lines(self):
+        p, f = self.place, self.flat
+        slip = f.slip * p.d
+        self.line_ref[...] = shifted(self.long_ref, f.halo * 128 - slip, f.lines)
+
+        def mend():
+            self.copy().wait_recv()
+            before = shifted(self.halo_ref, f.length - f.tail_from * 128 - slip, f.halo)
+            at = lax.broadcasted_iota(jnp.int32, (f.halo, 128), 0) * 128
+            at = at + lax.broadcasted_iota(jnp.int32, (f.halo, 128), 1)
+            self.line_ref[pl.ds(0, f.halo), :] = jnp.where(at < slip, before, self.line_ref[pl.ds(0, f.halo), :])
+
+        pl.when(p.d > 0)(mend)
+
+    def store(self, out_ref):
+        p, f = self.place, self.flat
+
+        def put(split):
+            for part in range(f.parts):
+                for block in range(D // 128):
+                    first, stride = f.place_of(part, block, split)
+                    out_ref[p.d, part, :, pl.ds(128 * block, 128)] = self.line_ref[
+                        pl.ds(first, f.deep, stride=stride), :
+                    ].astype(jnp.bfloat16)
+
+        pl.when(p.d < f.split)(lambda: put(True))
+        pl.when(p.d >= f.split)(lambda: put(False))
+
+    def last_rows(self, count):
+        f = self.flat
+        lines = -(-count * 6 // 8) * 8
+        return shifted(self.long_ref, f.halo * 128 + f.length - count * D, lines)
+
+
+def scratch_lead(flat):
+    return [
+        pltpu.VMEM((flat.halo + flat.held + 8, 128), jnp.float32),
+        pltpu.VMEM((flat.tail + flat.halo + 8, 128), jnp.float32),
+        pltpu.VMEM((flat.lines, 128), jnp.float32),
+    ]
+
+
+def gather_kernel(levels, att, ffn, att_ref, ffn_ref, att_out, ffn_out, terms_out, att_w, ffn_w, terms,
+                  att_long, att_halo, att_line, ffn_long, ffn_halo, ffn_line, spare,
+                  halo_send, halo_recv, att_send, att_recv, ffn_send, ffn_recv, term_send, term_recv, out_sem):
+    p = Place(levels)
+    p.meet(True)
+    sends = Sends()
+    lead_a = Lead(p, sends, att, att_ref, att_long, att_halo, att_line, halo_send.at[0], halo_recv.at[0])
+    lead_f = Lead(p, sends, ffn, ffn_ref, ffn_long, ffn_halo, ffn_line, halo_send.at[1], halo_recv.at[1])
+    lead_a.begin()
+    lead_f.begin()
+    lead_a.lines()
+    lead_a.store(att_w)
+    att_go = Gather(p, sends, att_w, att_send, att_recv)
+    ffn_go = Gather(p, sends, ffn_w, ffn_send, ffn_recv)
+    steps_a, steps_f = att_go.steps(), ffn_go.steps()
+    steps_a[0]()
+
+    def last():
+        terms[...] = jnp.zeros(terms.shape, terms.dtype)
+        for lead, at, count in ((lead_a, 0, 5), (lead_f, 8, 7)):
+            rows = lead.last_rows(count)
+            spare[pl.ds(0, rows.shape[0]), :] = rows
+            for block in range(D // 128):
+                terms[pl.ds(at, count), pl.ds(128 * block, 128)] = spare[pl.ds(block, count, stride=6), :]
+
+    pl.when(p.d == att.chips - 1)(last)
+    lead_f.lines()
+    lead_f.store(ffn_w)
+    for step in steps_a[1:3]:
+        step()
+    steps_f[0]()
+    for step in steps_a[3:]:
+        step()
+    Spread(p, sends, terms, term_send, term_recv).run()
+    for step in steps_f[1:]:
+        step()
+    att_go.from_sibling()
+    ffn_go.from_sibling()
+    terms_out[...] = terms[...]
+    outs = [pltpu.make_async_copy(att_w, att_out, out_sem.at[0]), pltpu.make_async_copy(ffn_w, ffn_out, out_sem.at[1])]
+    for copy in outs:
+        copy.start()
+    sends.finish()
+    for copy in outs:
+        copy.wait()
+
+
+def gather_weights(levels, att, ffn, att_lines, ffn_lines):
+    vmem = pl.BlockSpec(memory_space=pltpu.VMEM)
+    anywhere = pl.BlockSpec(memory_space=pl.ANY)
+    chips = att.chips
+    att_shape = (chips, att.parts, att.deep, D)
+    ffn_shape = (chips, ffn.parts, ffn.deep, D)
+    dma = pltpu.SemaphoreType.DMA
+    return pl.pallas_call(
+        functools.partial(gather_kernel, levels, att, ffn),
+        out_shape=(
+            jax.ShapeDtypeStruct(att_shape, jnp.bfloat16),
+            jax.ShapeDtypeStruct(ffn_shape, jnp.bfloat16),
+            jax.ShapeDtypeStruct((16, D), jnp.float32),
+        ),
+        in_specs=[vmem, vmem],
+        out_specs=(anywhere, anywhere, vmem),
+        scratch_shapes=[
+            pltpu.VMEM(att_shape, jnp.bfloat16),
+            pltpu.VMEM(ffn_shape, jnp.bfloat16),
+            pltpu.VMEM((16, D), jnp.float32),
+            *scratch_lead(att),
+            *scratch_lead(ffn),
+            pltpu.VMEM((48, 128), jnp.float32),
+            dma((2,)),
+            dma((2,)),
+            dma((5, chips)),
+            dma((2, chips)),
+            dma((5, chips)),
+            dma((2, chips)),
+            dma((3,)),
+            dma,
+            dma((2,)),
+        ],
+        compiler_params=pltpu.CompilerParams(
+            collective_id=1, has_side_effects=True, vmem_limit_bytes=56 * 2**20
+        ),
+        name="gather_weights",
+    )(att_lines, ffn_lines)
+
+
+class Reduce:
+    def __init__(self, place, sends, ref, own_ref, sib_ref, b_ref, a_ref, z_ref, send_sem, recv_sem):
+        self.place, self.sends, self.ref, self.own_ref = place, sends, ref, own_ref
+        self.sib_ref, self.b_ref, self.a_ref, self.z_ref = sib_ref, b_ref, a_ref, z_ref
+        self.send_sem, self.recv_sem = send_sem, recv_sem
+        self.half = ref.shape[2] // 2
+
+    def rows(self, core):
+        return pl.ds(pl.multiple_of(core * self.half, self.half), self.half)
+
+    def levels(self):
+        p = self.place
+        return [(p.z + p.levels // 2 + i) % p.levels for i in range(p.levels)]
+
+    def send(self, cond, chip, way, dst, device):
+        p = self.place
+        core = 1 - p.c if way == 4 else p.c
+        src = self.ref.at[chip, :, self.rows(core), :]
+        make = lambda: remote(src, dst, self.send_sem.at[way, chip], self.recv_sem.at[way, chip], device)
+        self.sends.start(cond, make)
+
+    def add(self, cond, chip, way, src):
+        p = self.place
+
+        def act():
+            remote(src, src, self.send_sem.at[way, chip], self.recv_sem.at[way, chip], p.sibling).wait_recv()
+            for part in range(self.ref.shape[1]):
+                at = (chip, part, self.rows(p.c), slice(None))
+                self.ref[at] = self.ref[at] + src[part]
+
+        when(cond, act)
+
+    def share(self):
+        p = self.place
+        for column in (p.far, p.b_near, p.a_near, p.d):
+            for level in self.levels():
+                chip = p.at(column, level)
+                self.send(None, chip, 4, self.sib_ref.at[chip], p.sibling)
+
+    def over_b(self):
+        p = self.place
+        for kind, column in ((1, p.far), (0, p.b_near)):
+            for level in self.levels():
+                chip = p.at(column, level)
+                self.add(None, chip, 4, self.sib_ref.at[chip])
+                self.send(None, chip, 3, self.b_ref.at[kind, level], p.across_b)
+
+    def over_a(self):
+        p = self.place
+        for level in self.levels():
+            chip = p.at(p.a_near, level)
+            self.add(None, chip, 4, self.sib_ref.at[chip])
+            self.add(None, chip, 3, self.b_ref.at[1, level])
+            self.send(None, chip, 2, self.a_ref.at[level], p.across_a)
+
+    def collect(self, cond, chip, level):
+        self.add(cond, chip, 4, self.sib_ref.at[chip])
+        self.add(cond, chip, 3, self.b_ref.at[0, level])
+        self.add(cond, chip, 2, self.a_ref.at[level])
+
+    def line(self):
+        p = self.place
+        for distance in range(p.levels - 1, 0, -1):
+            for level, there, step in p.levels_at(distance):
+                chip = p.at(p.d, level)
+                way = 0 if step > 0 else 1
+                onward, _ = p.along(step)
+                _, behind = p.along(-step)
+                self.collect(there, chip, level)
+                self.add(both(there, behind), chip, way, self.z_ref.at[way, level])
+                self.send(there, chip, way, self.z_ref.at[way, level], onward)
+
+    def keep(self):
+        p = self.place
+        self.collect(None, p.d, p.z)
+        for part in range(self.ref.shape[1]):
+            self.own_ref[p.c, part] = self.ref[p.d, part, self.rows(p.c), :].astype(jnp.float32)
+        for way, there in ((0, p.has_down), (1, p.has_up)):
+
+            def act(way=way):
+                src = self.z_ref.at[way, p.z]
+                remote(src, src, self.send_sem.at[way, p.d], self.recv_sem.at[way, p.d], p.sibling).wait_recv()
+                for part in range(self.ref.shape[1]):
+                    self.own_ref[p.c, part] = self.own_ref[p.c, part] + src[part].astype(jnp.float32)
+
+            pl.when(there)(act)
+
+    def hand_over(self, send_sem, recv_sem):
+        p = self.place
+        own, other = self.own_ref.at[p.c], self.own_ref.at[1 - p.c]
+        self.sends.start(None, lambda: remote(own, own, send_sem, recv_sem, p.sibling))
+        return lambda: remote(other, other, send_sem, recv_sem, p.sibling).wait_recv()
+
+
+class Terms:
+    def __init__(self, place, sends, ref, got_ref, all_ref, send_sem, recv_sem):
+        self.place, self.sends, self.ref, self.got_ref, self.all_ref = place, sends, ref, got_ref, all_ref
+        self.send_sem, self.recv_sem = send_sem, recv_sem
+
+    def copy(self, way, core, device):
+        return remote(self.ref.at[core], self.got_ref.at[way], self.send_sem.at[way], self.recv_sem.at[way], device)
+
+    def add(self, cond, way):
+        def act():
+            self.copy(way, 0, self.place.sibling).wait_recv()
+            self.ref[self.place.c] = self.ref[self.place.c] + self.got_ref[way]
+
+        when(cond, act)
+
+    def run(self):
+        p = self.place
+        c = p.c
+        self.sends.start(None, lambda: self.copy(0, 1 - c, p.sibling))
+        self.add(None, 0)
+        self.sends.start(p.b_at == 0, lambda: self.copy(1, c, p.across_b))
+        self.add(p.b_at == 1, 1)
+        self.sends.start((p.b_at == 1) & (p.a_at == 0), lambda: self.copy(2, c, p.across_a))
+        home = (p.b_at == 1) & (p.a_at == 1)
+        self.add(home, 2)
+        self.add(home & p.has_down, 3)
+        self.sends.start(home & p.has_up, lambda: self.copy(3, c, p.up))
+
+    def hand_over(self, last):
+        p = self.place
+        own = self.ref.at[p.c]
+        make = lambda: remote(own, self.all_ref.at[p.c], self.send_sem.at[4], self.recv_sem.at[4], p.sibling)
+        self.sends.start(last, make)
+
+        def end():
+            make().wait_recv()
+            self.all_ref[p.c] = self.ref[p.c]
+
+        return end
+
+
+class Trail:
+    def __init__(self, place, sends, flat, own_ref, line_ref, out_ref, send_sem, recv_sem):
+        self.place, self.sends, self.flat = place, sends, flat
+        self.own_ref, self.line_ref, self.out_ref = own_ref, line_ref, out_ref
+        self.send_sem, self.recv_sem = send_sem, recv_sem
+
+    def copy(self):
+        f, p = self.flat, self.place
+        return remote(
+            self.line_ref.at[pl.ds(0, f.halo), :],
+            self.line_ref.at[pl.ds(f.lines, f.halo), :],
+            self.send_sem,
+            self.recv_sem,
+            (p.d - 1, p.c),
+        )
+
+    def lines(self):
+        p, f = self.place, self.flat
+        half = f.deep // 2
+
+        def put(split):
+            for core in range(2):
+                for part in range(f.parts):
+                    for block in range(D // 128):
+                        first, stride = f.place_of(part, block, split)
+                        first = first + stride * half * core
+                        self.line_ref[pl.ds(first, half, stride=stride), :] = self.own_ref[
+                            core, part, :, pl.ds(128 * block, 128)
+                        ]
+
+        pl.when(p.d < f.split)(lambda: put(True))
+        pl.when(p.d >= f.split)(lambda: put(False))
+        self.sends.start(p.d > 0, self.copy)
+
+    def last_rows(self, terms_ref, at, count):
+        f = self.flat
+        for core in range(2):
+            for block in range(3):
+                self.line_ref[pl.ds(f.lines + 3 * core + block, count, stride=6), :] = terms_ref[
+                    core, pl.ds(at, count), pl.ds(128 * block, 128)
+                ]
+
+    def out(self):
+        p, f = self.place, self.flat
+        pl.when(p.d < f.chips - 1)(lambda: self.copy().wait_recv())
+        self.out_ref[...] = shifted(self.line_ref, f.slip * p.d, f.held)
+
+
+def reduce_kernel(levels, att, ffn, att_in, ffn_in, terms_in, att_out, ffn_out, att_g, ffn_g, terms,
+                  att_own, att_sib, att_b, att_a, att_z, ffn_own, ffn_sib, ffn_b, ffn_a, ffn_z, terms_got, terms_all,
+                  att_line, ffn_line, att_send, att_recv, ffn_send, ffn_recv, term_send, term_recv,
+                  own_send, own_recv, halo_send, halo_recv, in_sem):
+    p = Place(levels)
+    ins = [pltpu.make_async_copy(ffn_in, ffn_g, in_sem.at[0]), pltpu.make_async_copy(att_in, att_g, in_sem.at[1])]
+    for copy in ins:
+        copy.start()
+    p.meet(True)
+    sends = Sends()
+    terms[...] = terms_in[...]
+    add_t = Terms(p, sends, terms, terms_got, terms_all, term_send, term_recv)
+    add_f = Reduce(p, sends, ffn_g, ffn_own, ffn_sib, ffn_b, ffn_a, ffn_z, ffn_send, ffn_recv)
+    add_a = Reduce(p, sends, att_g, att_own, att_sib, att_b, att_a, att_z, att_send, att_recv)
+    for copy in ins:
+        copy.wait()
+    add_f.share()
+    add_a.share()
+    for work in (add_f, add_a):
+        work.over_b()
+    for work in (add_f, add_a):
+        work.over_a()
+    for work in (add_f, add_a):
+        work.line()
+    add_t.run()
+    add_f.keep()
+    end_f = add_f.hand_over(own_send.at[0], own_recv.at[0])
+    add_a.keep()
+    end_a = add_a.hand_over(own_send.at[1], own_recv.at[1])
+    last = p.d == att.chips - 1
+    end_t = add_t.hand_over(last)
+    trail_f = Trail(p, sends, ffn, ffn_own, ffn_line, ffn_out, halo_send.at[0], halo_recv.at[0])
+    trail_a = Trail(p, sends, att, att_own, att_line, att_out, halo_send.at[1], halo_recv.at[1])
+    end_f()
+    trail_f.lines()
+    end_a()
+    trail_a.lines()
+
+    def terms_here():
+        end_t()
+        trail_f.last_rows(terms_all, 8, 7)
+        trail_a.last_rows(terms_all, 0, 5)
+
+    pl.when(last)(terms_here)
+    trail_f.out()
+    trail_a.out()
+    sends.finish()
+
+
+def scratch_reduce(flat, levels):
+    half = (flat.parts, flat.deep // 2, D)
+    bf16 = jnp.bfloat16
+    return [
+        pltpu.VMEM((2, *half), jnp.float32),
+        pltpu.VMEM((flat.chips, *half), bf16),
+        pltpu.VMEM((2, levels, *half), bf16),
+        pltpu.VMEM((levels, *half), bf16),
+        pltpu.VMEM((2, levels, *half), bf16),
+    ]
+
+
+def reduce_grads(levels, att, ffn, att_grads, ffn_grads, terms):
+    vmem = pl.BlockSpec(memory_space=pltpu.VMEM)
+    anywhere = pl.BlockSpec(memory_space=pl.ANY)
+    chips = att.chips
+    dma = pltpu.SemaphoreType.DMA
+    return pl.pallas_call(
+        functools.partial(reduce_kernel, levels, att, ffn),
+        out_shape=(
+            jax.ShapeDtypeStruct((att.held, 128), jnp.float32),
+            jax.ShapeDtypeStruct((ffn.held, 128), jnp.float32),
+        ),
+        in_specs=[anywhere, anywhere, vmem],
+        out_specs=(vmem, vmem),
+        scratch_shapes=[
+            pltpu.VMEM((chips, att.parts, att.deep, D), jnp.bfloat16),
+            pltpu.VMEM((chips, ffn.parts, ffn.deep, D), jnp.bfloat16),
+            pltpu.VMEM((2, 16, D // 2), jnp.float32),
+            *scratch_reduce(att, levels),
+            *scratch_reduce(ffn, levels),
+            pltpu.VMEM((4, 16, D // 2), jnp.float32),
+            pltpu.VMEM((2, 16, D // 2), jnp.float32),
+            pltpu.VMEM((att.lines + att.halo + 8, 128), jnp.float32),
+            pltpu.VMEM((ffn.lines + ffn.halo + 8, 128), jnp.float32),
+            dma((5, chips)),
+            dma((5, chips)),
+            dma((5, chips)),
+            dma((5, chips)),
+            dma((5,)),
+            dma((5,)),
+            dma((2,)),
+            dma((2,)),
+            dma((2,)),
+            dma((2,)),
+            dma((2,)),
+        ],
+        compiler_params=pltpu.CompilerParams(
+            collective_id=2, has_side_effects=True, vmem_limit_bytes=60 * 2**20
+        ),
+        name="reduce_grads",
+    )(att_grads, ffn_grads, terms)
+
+
+def as_lines(flat, vector):
+    return jnp.pad(vector, (0, flat.held * 128 - flat.length)).reshape(flat.held, 128)
+
+
+def attend_batch(query_rows, key_rows, value_rows, seg_ids):
+    scores = jnp.einsum(
+        "sqhd,skhd->shqk", query_rows, key_rows, preferred_element_type=jnp.float32
+    ) * HEAD_DIM ** (-0.5)
+    same_doc = seg_ids[:, :, None] == seg_ids[:, None, :]
+    return jnp.where(same_doc[:, None], scores, masked)
+
+
+def fast_body(
+    levels,
+    tokens,
+    cotangent,
+    segments,
+    live_count,
+    att_master,
+    att_first,
+    att_second,
+    ffn_master,
+    ffn_first,
+    ffn_second,
+):
+    f32, bf16 = jnp.float32, jnp.bfloat16
+    seqs, length = segments.shape
+    chips = lax.axis_size("dp")
+    att = Flat(att_master.shape[0], chips, 3, 3 * chips // 4)
+    ffn = Flat(ffn_master.shape[0], chips, 4, chips // 2)
+    att_w, ffn_w, terms = gather_weights(levels, att, ffn, as_lines(att, att_master), as_lines(ffn, ffn_master))
+    dot = functools.partial(jnp.dot, preferred_element_type=f32)
+    qkv_weight = att_w[: att.split].transpose(0, 2, 1, 3).reshape(D, 3 * D)
+    out_weight = att_w[att.split :].reshape(D, D)
+    in_weight = ffn_w[: ffn.split].transpose(0, 2, 1, 3).reshape(D, FF)
+    down_weight = ffn_w[ffn.split :].reshape(FF, D)
+    att_terms, in_bias, ffn_terms = terms[:5], terms[8:12].reshape(FF), terms[12:15]
+    bias_qkv = jnp.concatenate([att_terms[0], jnp.zeros_like(att_terms[0]), att_terms[1]])
+    qkv = (dot(tokens, qkv_weight) + bias_qkv).astype(bf16)
+    heads = qkv.reshape(seqs, length, 3, HEADS, HEAD_DIM)
+    query_rows, key_rows, value_rows = heads[:, :, 0], heads[:, :, 1], heads[:, :, 2]
+    scores = attend_batch(query_rows, key_rows, value_rows, segments)
+    row_top = jnp.max(scores, -1, keepdims=True)
+    raised = jnp.exp(scores - row_top)
+    row_total = jnp.sum(raised, -1, keepdims=True)
+    probs = raised / row_total
+    context = (
+        jnp.einsum("shqk,skhd->sqhd", probs.astype(bf16), value_rows, preferred_element_type=f32)
+        .astype(bf16)
+        .reshape(-1, D)
+    )
+    log_total = row_top + jnp.log(row_total)
+    residual = tokens.astype(f32) + dot(context, out_weight) + att_terms[2]
+    first_out, first_hat, first_rstd = normalize(residual, att_terms[3], att_terms[4])
+    first_low = first_out.astype(bf16)
+    ffn_inner = dot(first_low, in_weight) + in_bias
+    ffn_act = jax.nn.gelu(ffn_inner, approximate=False).astype(bf16)
+    second_in = first_out + dot(ffn_act, down_weight) + ffn_terms[0]
+    output, second_hat, second_rstd = normalize(second_in, ffn_terms[1], ffn_terms[2])
+
+    live = jnp.arange(seqs * length) // length < live_count[0]
+    grad_out = jnp.where(live[:, None], cotangent.astype(f32), 0.0)
+    grad_second, grad_gain_two, grad_shift_two = norm_back(grad_out, second_hat, second_rstd, ffn_terms[1])
+    grad_down = grad_second.astype(bf16)
+    grad_down_bias = jnp.sum(grad_down.astype(f32), 0)
+    grad_down_weight = dot(ffn_act.T, grad_down)
+    grad_inner = (dot(grad_down, down_weight.T) * gelu_slope(ffn_inner)).astype(bf16)
+    grad_in_bias = jnp.sum(grad_inner.astype(f32), 0)
+    grad_in_weight = dot(first_low.T, grad_inner)
+    grad_first = grad_second + dot(grad_inner, in_weight.T)
+    grad_residual, grad_gain_one, grad_shift_one = norm_back(grad_first, first_hat, first_rstd, att_terms[3])
+    grad_proj = grad_residual.astype(bf16)
+    grad_out_bias = jnp.sum(grad_proj.astype(f32), 0)
+    grad_out_weight = dot(context.T, grad_proj)
+    grad_context = dot(grad_proj, out_weight.T).astype(bf16).reshape(seqs, length, HEADS, HEAD_DIM)
+    probs = jnp.exp(attend_batch(query_rows, key_rows, value_rows, segments) - log_total)
+    grad_probs = jnp.einsum("sqhd,skhd->shqk", grad_context, value_rows, preferred_element_type=f32)
+    grad_values = jnp.einsum("shqk,sqhd->skhd", probs.astype(bf16), grad_context, preferred_element_type=f32)
+    grad_scores = probs * (grad_probs - jnp.sum(probs * grad_probs, -1, keepdims=True))
+    grad_scores = grad_scores.astype(bf16)
+    scale = HEAD_DIM ** (-0.5)
+    grad_queries = jnp.einsum("shqk,skhd->sqhd", grad_scores, key_rows, preferred_element_type=f32) * scale
+    grad_keys = jnp.einsum("shqk,sqhd->skhd", grad_scores, query_rows, preferred_element_type=f32) * scale
+    grad_qkv = jnp.concatenate([g.reshape(-1, D) for g in (grad_queries, grad_keys, grad_values)], -1).astype(bf16)
+    grad_wide = grad_qkv.astype(f32)
+    grad_query_bias = jnp.sum(grad_wide[:, :D], 0)
+    grad_value_bias = jnp.sum(grad_wide[:, 2 * D :], 0)
+    grad_qkv_weight = dot(tokens.T, grad_qkv)
+    input_grad = (dot(grad_qkv, qkv_weight.T) + grad_residual).astype(bf16)
+
+    zero = jnp.zeros((D,), f32)
+    rows = [grad_query_bias, grad_value_bias, grad_out_bias, grad_gain_one, grad_shift_one, zero, zero, zero]
+    rows += [*grad_in_bias.reshape(4, D), grad_down_bias, grad_gain_two, grad_shift_two, zero]
+    term_grads = jnp.stack(rows).reshape(16, 2, D // 2).transpose(1, 0, 2)
+    att_grads = jnp.concatenate(
+        [
+            grad_qkv_weight.astype(bf16).reshape(att.split, att.deep, 3, D).transpose(0, 2, 1, 3),
+            grad_out_weight.astype(bf16).reshape(chips - att.split, 3, att.deep, D),
+        ]
+    )
+    ffn_grads = jnp.concatenate(
+        [
+            grad_in_weight.astype(bf16).reshape(ffn.split, ffn.deep, 4, D).transpose(0, 2, 1, 3),
+            grad_down_weight.astype(bf16).reshape(chips - ffn.split, 4, ffn.deep, D),
+        ]
+    )
+    att_sum, ffn_sum = reduce_grads(levels, att, ffn, att_grads, ffn_grads, term_grads)
+    att_grad = att_sum.reshape(-1)[: att.length]
+    ffn_grad = ffn_sum.reshape(-1)[: ffn.length]
+    att_new = adam_update(att_master, att_first, att_second, att_grad)
+    ffn_new = adam_update(ffn_master, ffn_first, ffn_second, ffn_grad)
+    return (output.astype(bf16), input_grad, att_grad, *att_new, ffn_grad, *ffn_new)
+
+
+def body_for(mesh):
+    chips, cores = mesh.shape["dp"], mesh.shape["rep"]
+    if chips == 16 and cores == 2:
+        return functools.partial(fast_body, chips // 4)
+    return general_body
+
+
 def solution(mesh):
     placed = (
         P(("dp", "rep"), None),
@@ -339,7 +1124,7 @@
         P("dp"),
     )
     return jax.shard_map(
-        body,
+        body_for(mesh),
         mesh=mesh,
         in_specs=placed,
         out_specs=(

time: 1650 us -> 549 us (0.33)
  the two profiles are of different devices: /device:TPU:0 before, /device:TPU:29 now
where the time goes in v1:
time: 549 us; the launch traced here: 541 us
  Pallas kernels  190 us (35%)
  matrix products  174 us (32%)
  local copies, waits for them, and re-layouts  114 us (21%)
  other arithmetic  60.3 us (11%)
    pallas_call x1, Pallas kernels, reduce_grads(): pl.pallas_call(functools.partial(reduce_kernel, levels, att, ffn), out_sh...  108 us
    pallas_call x1, Pallas kernels, gather_weights(): pl.pallas_call(functools.partial(gather_kernel, levels, att, ffn), out_sh...  82.3 us
    dot_general x1, matrix products, fast_body(): ffn_inner = dot(first_low, in_weight) + in_bias  36.4 us
    unnamed x126, local copies, waits for them, and re-layouts  23 us
    convert_element_type x1, other arithmetic, fast_body(): grad_scores = grad_scores.astype(bf16)  21.6 us
    dot_general x1, matrix products, fast_body(): jnp.einsum('sqhd,skhd->shqk', grad_context, value_rows, preferred_element...  18 us
    reshape x2, local copies, waits for them, and re-layouts, fast_body(): grad_qkv_weight.astype(bf16).reshape(att.split, att.deep, 3, D)  18 us
    reshape x2, local copies, waits for them, and re-layouts, fast_body(): grad_in_weight.astype(bf16).reshape(ffn.split, ffn.deep, 4, D)  13.2 us

profile of v1, /device:TPU:29, one launch (start us, length us, event | category | flops | bytes accessed | tf_op | source)
XLA Modules:
  0.0 540.9 jit_solution(7411212523996247433)
XLA Ops:
  2.0 1.1 broadcast_compare_fusion
  3.1 2.1 pad_bitcast_fusion.1.att_ref
  5.2 2.4 pad_bitcast_fusion.ffn_ref
  7.6 1.6 copy.45
  9.2 1.7 copy.36
  10.9 82.3 %gather_weights.1 = (bf16[16,3,64,768]{3,2,1,0:T(8,128)(2,1)}, bf16[16,4,96,768]{3,2,1,0:T(8,128)(2,1)}, f32[16,768]{1,0:T(8,128)}) custom-call(f32[1160,128]{1,0:T(8,128)} %pad_bitcast_fusion.1.att_ref, f32[2312,128]{1,0:T(8,128)} %pad_bitcast_fusion.ffn_ref), custom_call_target="tpu_custom_call" | custom-call | tf_op jit(solution)/shard_map/gather_weights/pallas_call | solution.py:673
  93.2 8.3 %fusion.62 = (bf16[8,4,96,768]{3,2,1,0:T(8,128)(2,1)}, bf16[8,96,4,768]{3,1,2,0:T(8,128)(2,1)}) fusion(bf16[16,4,96,768]{3,2,1,0:T(8,128)(2,1)} %get-tuple-element.17), kind=kLoop, calls=%fused_computation.141 | loop fusion | bytes 18874368 | tf_op jit(solution)/shard_map/slice | solution.py:1027
  102.2 2.4 slice.106
  104.5 2.2 slice_bitcast_fusion.1
  106.8 3.0 copy.37
  109.8 0.8 copy.74
  110.6 1.8 copy-done.19
  112.4 6.6 %fusion.23 = bf16[1024,2304]{0,1:T(8,128)(2,1)} fusion(bf16[768,2304]{1,0:T(8,128)(2,1)S(1)} %bitcast.131, bf16[1024,768]{1,0:T(8,128)(2,1)S(1)} %copy-done.25, f32[2304]{0:T(1024)S(1)} %pad_maximum_fusion.2), kind=kOutput, calls=%fused_computation.44 | convolution fusion | flops 3628597248 | bytes 9839616 | tf_op jit(solution)/shard_map/dot_general | solution.py:1030
  119.0 8.9 %reshape.207 = bf16[2,512,3,12,64]{1,0,4,3,2:T(2,128)(2,1)} reshape(bf16[1024,2304]{0,1:T(8,128)(2,1)} %fusion.23) | data formatting | bytes 9437184 | tf_op jit(solution)/shard_map/reshape | solution.py:1031
  128.0 5.5 %fusion.63 = (bf16[2,512,1,12,64]{1,0,4,3,2:T(2,128)(2,1)S(1)}, bf16[2,512,1,12,64]{1,0,4,3,2:T(2,128)(2,1)S(1)}, bf16[2,512,1,12,64]{1,0,4,3,2:T(2,128)(2,1)S(1)}) fusion(bf16[2,512,3,12,64]{1,0,4,3,2:T(2,128)(2,1)} %reshape.207), kind=kLoop, calls=%fused_computation.142 | loop fusion | bytes 9437184 | tf_op jit(solution)/shard_map/slice | solution.py:1032
  133.5 3.6 copy.43
  137.2 1.0 copy.76
  138.3 10.4 %fusion.22 = (f32[2,12,512]{2,1,0:T(8,128)S(1)}, f32[2,12,512,512]{2,3,1,0:T(8,128)}) fusion(pred[2,512,512]{1,2,0:T(8,128)(4,1)S(1)} %broadcast_compare_fusion, bf16[2,512,1,12,64]{1,0,4,3,2:T(2,128)(2,1)S(1)} %get-tuple-element.74, bf16[2,512,1,12,64]{1,0,4,3,2:T(2,128)(2,1)S(1)} %get-tuple-element.73), kind=kOutput, calls=%fused_computation.40 | convolution fusion | flops 824168448 | bytes 28884992 | tf_op jit(solution)/shard_map/sqhd,skhd->shqk/dot_general | solution.py:997
  148.7 11.0 %fusion = f32[2,12,512]{2,1,0:T(8,128)S(1)} fusion(f32[2,12,512]{2,1,0:T(8,128)S(1)} %get-tuple-element.80, f32[2,12,512,512]{2,3,1,0:T(8,128)} %get-tuple-element.81, pred[2,512,512]{1,2,0:T(8,128)(4,1)S(1)} %broadcast_compare_fusion), kind=kLoop, calls=%fused_computation.6 | loop fusion | flops 25153536 | bytes 25788416 | tf_op jit(solution)/shard_map/reduce_sum | solution.py:1036
  160.4 12.2 %fusion.38 = bf16[2,512,12,64]{1,3,2,0:T(8,128)(2,1)S(1)} fusion(f32[2,12,512]{2,1,0:T(8,128)S(1)} %fusion, f32[2,12,512]{2,1,0:T(8,128)S(1)} %get-tuple-element.80, f32[2,12,512,512]{2,3,1,0:T(8,128)} %get-tuple-element.81, pred[2,512,512]{1,2,0:T(8,128)(4,1)S(1)} %broadcast_compare_fusion, bf16[2,512,1,12,64]{1,0,4,3,2:T(2,128)(2,1)S(1)} %get-tuple-element.72), kind=kOutput, calls=%fused_computation.89 | convolution fusion | flops 837550080 | bytes 28934144 | tf_op jit(solution)/shard_map/shqk,skhd->sqhd/dot_general | solution.py:1039
  172.6 1.6 copy.42
  174.7 1.7 fusion.65
  176.8 36.4 %fusion.4 = (bf16[1024,3072]{1,0:T(8,128)(2,1)}, f32[1024,3072]{1,0:T(8,128)}) fusion(f32[3072]{0:T(1024)S(1)} %add.150, bf16[768,3072]{1,0:T(8,128)(2,1)S(1)} %bitcast.120, f32[1024,768]{0,1:T(8,128)S(1)} %get-tuple-element.83, f32[768]{0:T(1024)S(1)} %get-tuple-element.53, f32[768]{0:T(1024)S(1)} %get-tuple-element.54, f32[1024]{0:T(1024)S(1)} %add_rsqrt_fusion.1, ...), kind=kOutput, calls=%fused_computation.12 | convolution fusion | flops 5043388416 | bytes 26765312 | tf_op jit(solution)/shard_map/dot_general | solution.py:1047
  213.3 7.6 %fusion.66 = (f32[1024]{0:T(1024)S(1)}, f32[1024,768]{0,1:T(8,128)S(1)}) fusion(f32[768]{0:T(1024)S(1)} %copy-done.42, bf16[1024,3072]{1,0:T(8,128)(2,1)} %get-tuple-element.84, bf16[3072,768]{1,0:T(8,128)(2,1)S(1)} %bitcast.127, f32[768]{0:T(1024)S(1)} %get-tuple-element.53, f32[768]{0:T(1024)S(1)} %get-tuple-element.54, f32[1024]{0:T(1024)S(1)} %add_rsqrt_fusion.1, ...), kind=kOutput, calls=%fused_computation.145 | convolution fusion | flops 4837342208 | bytes 17323008 | tf_op jit(solution)/shard_map/dot_general | solution.py:1049
  221.4 1.0 copy-done.4
  222.4 1.4 multiply_reduce_fusion.1
  225.0 4.0 convert_reduce_fusion.1
  229.0 12.2 %convert_reduce_fusion = (f32[3072]{0:T(1024)S(1)}, bf16[1024,3072]{1,0:T(8,128)(2,1)S(1)}) fusion(f32[1024,3072]{1,0:T(8,128)} %get-tuple-element.85, f32[3072]{0:T(1024)S(1)} %add.150, bf16[1024,768]{0,1:T(8,128)(2,1)S(1)} %get-tuple-element.67, bf16[3072,768]{1,0:T(8,128)(2,1)} %bitcast.124), kind=kOutput, calls=%fused_computation.20 | convolution fusion | flops 4872729600 | bytes 25190400 | tf_op jit(solution)/shard_map/dot_general | solution.py:1058
  241.3 7.0 %convolution_convert_fusion = bf16[3072,768]{1,0:T(8,128)(2,1)} fusion(bf16[1024,3072]{1,0:T(8,128)(2,1)S(1)} %bitcast.142, bf16[1024,768]{0,1:T(8,128)(2,1)S(1)} %get-tuple-element.67), kind=kOutput, calls=%fused_computation.41 | convolution fusion | flops 4834197504 | bytes 12582912 | tf_op jit(solution)/shard_map/dot_general | solution.py:1057
  248.4 8.3 %multiply_reduce_fusion.2 = (f32[768]{0:T(1024)S(1)}, f32[1024]{0:T(1024)S(1)}, f32[1024]{0:T(1024)S(1)}, f32[768]{0:T(1024)S(1)}, f32[1024,768]{0,1:T(8,128)}) fusion(f32[1024,768]{0,1:T(8,128)S(1)} %copy-done.9, f32[1024]{0:T(1024)S(1)} %add_rsqrt_fusion.1, f32[1024]{0:T(1024)S(1)} %broadcast_multiply_fusion.5, f32[768]{0:T(1024)S(1)} %get-tuple-element.54, ...), kind=kOutput, calls=%fused_computation.54 | convolution fusion | flops 4846776320 | bytes 22066176 | tf_op jit(solution)/shard_map/dot_general | solution.py:1061
  258.5 4.1 convert_reduce_fusion.2
  262.6 1.5 copy-done.44
  264.1 7.1 %convolution_convert_fusion.1 = bf16[768,3072]{1,0:T(8,128)(2,1)} fusion(bf16[1024,3072]{1,0:T(8,128)(2,1)S(1)} %copy-done.44, f32[1024,768]{0,1:T(8,128)S(1)} %copy-done.10, f32[768]{0:T(1024)S(1)} %get-tuple-element.53, f32[768]{0:T(1024)S(1)} %get-tuple-element.54, f32[1024]{0:T(1024)S(1)} %add_rsqrt_fusion.1, f32[1024]{0:T(1024)S(1)} %broadcast_multiply_fusion.5), kind=kOutput, calls=%fused_computation.42 | convolution fusion | flops 4838129664 | bytes 14170112 | tf_op jit(solution)/shard_map/dot_general | solution.py:1060
  271.2 2.5 convolution_convert_fusion.4
  274.2 9.8 %reshape.218 = bf16[8,96,4,768]{3,2,1,0:T(4,128)(2,1)} reshape(bf16[768,3072]{1,0:T(8,128)(2,1)} %convolution_convert_fusion.1) | data formatting | bytes 9437184 | tf_op jit(solution)/shard_map/reshape | solution.py:1094
  284.1 3.4 copy.102
  287.7 4.4 pad_maximum_fusion.ffn_in
  294.5 3.3 convolution_convert_fusion.3
  297.8 1.6 copy.47
  299.5 2.9 reshape.212
  302.4 12.1 %fusion.33 = bf16[2,512,12,64]{1,3,2,0:T(8,128)(2,1)S(1)} fusion(f32[2,12,512]{2,1,0:T(8,128)S(1)} %copy-done.36, f32[2,12,512,512]{2,3,1,0:T(8,128)} %get-tuple-element.81, pred[2,512,512]{1,2,0:T(8,128)(4,1)S(1)} %copy-done.7, bf16[2,512,12,64]{1,0,3,2:T(2,128)(2,1)S(1)} %reshape.212), kind=kOutput, calls=%fused_computation.86 | convolution fusion | flops 831258624 | bytes 28884992 | tf_op jit(solution)/shard_map/shqk,sqhd->skhd/dot_general | solution.py:1069
  314.5 1.6 copy.55
  316.1 1.6 copy.79
  317.7 2.6 copy.60
  320.3 18.0 %multiply_reduce_fusion = (f32[2,12,512]{2,1,0:T(8,128)S(1)}, f32[2,12,512,512]{2,3,1,0:T(8,128)}) fusion(f32[2,12,512]{2,1,0:T(8,128)S(1)} %copy-done.36, f32[2,12,512,512]{2,3,1,0:T(8,128)} %get-tuple-element.81, pred[2,512,512]{1,2,0:T(8,128)(4,1)S(1)} %copy-done.7, bf16[2,512,1,12,64]{1,0,4,3,2:T(2,128)(2,1)S(1)} %copy-done.13, ...), kind=kOutput, calls=%fused_computation.1 | convolution fusion | flops 836751360 | bytes 54099968 | tf_op jit(solution)/shard_map/sqhd,skhd->shqk/dot_general | solution.py:1068
  338.3 21.6 %multiply_convert_fusion = bf16[2,12,512,512]{2,3,1,0:T(8,128)(2,1)} fusion(f32[2,12,512,512]{2,3,1,0:T(8,128)} %get-tuple-element.90, f32[2,12,512]{2,1,0:T(8,128)S(1)} %get-tuple-element.89, f32[2,12,512]{2,1,0:T(8,128)S(1)} %copy-done.36, f32[2,12,512,512]{2,3,1,0:T(8,128)} %get-tuple-element.81, pred[2,512,512]{1,2,0:T(8,128)(4,1)S(1)} %copy-done.7), kind=kLoop, calls=%fused_computation | loop fusion | flops 37748736 | bytes 63537152 | tf_op jit(solution)/shard_map/convert_element_type | solution.py:1071
  359.9 8.6 %fusion.37 = bf16[2,512,12,64]{1,3,2,0:T(8,128)(2,1)S(1)} fusion(bf16[2,12,512,512]{2,3,1,0:T(8,128)(2,1)} %multiply_convert_fusion, bf16[2,512,1,12,64]{1,0,4,3,2:T(2,128)(2,1)S(1)} %copy-done.3), kind=kOutput, calls=%fused_computation.88 | convolution fusion | flops 806879232 | bytes 15728640 | tf_op jit(solution)/shard_map/shqk,sqhd->skhd/dot_general | solution.py:1074
  368.5 6.7 %fusion.36 = bf16[2,512,12,64]{1,3,2,0:T(8,128)(2,1)S(1)} fusion(bf16[2,12,512,512]{2,3,1,0:T(8,128)(2,1)} %multiply_convert_fusion, bf16[2,512,1,12,64]{1,0,4,3,2:T(2,128)(2,1)S(1)} %copy-done.1), kind=kOutput, calls=%fused_computation.87 | convolution fusion | flops 806879232 | bytes 15728640 | tf_op jit(solution)/shard_map/shqk,skhd->sqhd/dot_general | solution.py:1073
  375.2 1.6 copy.50
  377.3 1.6 copy.52
  379.6 1.1 copy-done.15
  380.9 2.4 copy-done.11
  383.2 1.2 copy-done.20
  384.5 5.0 add_convert_fusion.1
  389.5 2.6 copy.61
  392.1 8.0 %fusion.24 = bf16[768,2304]{0,1:T(8,128)(2,1)} fusion(bf16[1024,2304]{0,1:T(8,128)(2,1)} %copy-done.11, bf16[1024,768]{1,0:T(8,128)(2,1)S(1)} %copy-done.26), kind=kOutput, calls=%fused_computation.48 | convolution fusion | flops 3625648128 | bytes 9830400 | tf_op jit(solution)/shard_map/dot_general | solution.py:1079
  400.1 1.1 convert_element_type.105
  402.9 2.7 stack.42
  405.6 8.7 %reshape.222 = bf16[12,64,3,768]{1,0,3,2:T(8,128)(2,1)} reshape(bf16[768,2304]{0,1:T(8,128)(2,1)S(1)} %copy-done.18) | data formatting | bytes 7077888 | tf_op jit(solution)/shard_map/reshape | solution.py:1088
  414.3 9.3 %copy.58 = bf16[12,64,3,768]{3,1,2,0:T(8,128)(2,1)S(1)} copy(bf16[12,64,3,768]{1,0,3,2:T(8,128)(2,1)} %reshape.222) | data formatting | bytes 7077888 | tf_op jit(solution)/shard_map/reshape | solution.py:1088
  423.6 3.8 pad_maximum_fusion.1.att_in
  427.4 107.8 %reduce_grads.1 = (f32[1160,128]{1,0:T(8,128)}, f32[2312,128]{1,0:T(8,128)}) custom-call(bf16[16,3,64,768]{3,2,1,0:T(8,128)(2,1)} %pad_maximum_fusion.1.att_in, bf16[16,4,96,768]{3,2,1,0:T(8,128)(2,1)} %pad_maximum_fusion.ffn_in, f32[2,16,384]{2,1,0:T(8,128)} %bitcast.140), custom_call_target="tpu_custom_call" | custom-call | tf_op jit(solution)/shard_map/reduce_grads/pallas_call | solution.py:955
  535.3 2.7 multiply_add_fusion.3
  538.2 2.5 multiply_add_fusion.1
  (152 shorter events, 12.3 us)
Async XLA Ops:
  0.6 7.0 %copy-start.24 = (bf16[1024,768]{1,0:T(8,128)(2,1)S(1)}, bf16[1024,768]{1,0:T(8,128)(2,1)}, u32[]{:S(2)}) copy-start(bf16[1024,768]{1,0:T(8,128)(2,1)} %param.11) | copy-start | bytes 4718596
  3.1 157.3 %copy-start.6 = (pred[2,512,512]{1,2,0:T(8,128)(4,1)}, pred[2,512,512]{1,2,0:T(8,128)(4,1)S(1)}, u32[]{:S(2)}) copy-start(pred[2,512,512]{1,2,0:T(8,128)(4,1)S(1)} %broadcast_compare_fusion) | copy-start | bytes 1572868
  93.2 8.3 %copy-start.38 = (f32[16,768]{1,0:T(8,128)S(1)}, f32[16,768]{1,0:T(8,128)}, u32[]{:S(2)}) copy-start(f32[16,768]{1,0:T(8,128)} %get-tuple-element.16) | copy-start | bytes 147460
  109.8 2.6 copy-start.25
  110.6 1.8 copy-start.19
  119.0 14.5 %slice-start = ((s8[4718592]{0:T(1024)(128)(4,1)}), s8[524288]{0:T(1024)(128)(4,1)S(1)}, s32[]{:S(2)}) async-start(s8[4718592]{0:T(1024)(128)(4,1)} %bitcast.106), calls=%async_computation | async-start | bytes 1048576
  128.0 5.6 %slice-start.1 = ((s8[4718592]{0:T(1024)(128)(4,1)}), s8[4194304]{0:T(1024)(128)(4,1)S(1)}, s32[]{:S(2)}) async-start(s8[4718592]{0:T(1024)(128)(4,1)} %bitcast.106), calls=%async_computation.1 | async-start | bytes 8388608
  133.5 4.8 copy-start
  133.5 4.8 copy-start.2
  133.5 26.9 %copy-start.12 = (bf16[2,512,1,12,64]{1,0,4,3,2:T(2,128)(2,1)}, bf16[2,512,1,12,64]{1,0,4,3,2:T(2,128)(2,1)S(1)}, u32[]{:S(2)}) copy-start(bf16[2,512,1,12,64]{1,0,4,3,2:T(2,128)(2,1)S(1)} %get-tuple-element.72) | copy-start | bytes 4718596
  138.2 38.5 %copy-start.17 = (bf16[96,8,4,768]{3,1,2,0:T(8,128)(2,1)}, bf16[96,8,4,768]{3,1,2,0:T(8,128)(2,1)S(1)}, u32[]{:S(2)}) copy-start(bf16[96,8,4,768]{3,1,2,0:T(8,128)(2,1)S(1)} %copy.76) | copy-start | bytes 14155780
  172.6 2.1 copy-start.32
  174.6 1.7 copy-start.27
  174.7 38.6 %slice-start.6 = ((s8[4718592]{0:T(1024)(128)(4,1)}), s8[4194304]{0:T(1024)(128)(4,1)S(1)}, s32[]{:S(2)}) async-start(s8[4718592]{0:T(1024)(128)(4,1)} %bitcast.125), calls=%async_computation.6 | async-start | bytes 8388608
  176.4 36.9 %copy-start.8 = (f32[1024,768]{0,1:T(8,128)}, f32[1024,768]{0,1:T(8,128)S(1)}, u32[]{:S(2)}) copy-start(f32[1024,768]{0,1:T(8,128)S(1)} %get-tuple-element.83) | copy-start | bytes 9437188
  176.8 36.5 %slice-start.7 = ((s8[4718592]{0:T(1024)(128)(4,1)}), s8[524288]{0:T(1024)(128)(4,1)S(1)}, s32[]{:S(2)}) async-start(s8[4718592]{0:T(1024)(128)(4,1)} %bitcast.125), calls=%async_computation.7 | async-start | bytes 1048576
  176.8 36.5 %copy-start.42 = (f32[768]{0:T(1024)S(1)}, f32[768]{0:T(1024)}, u32[]{:S(2)}) copy-start(f32[768]{0:T(1024)} %get-tuple-element.52) | copy-start | bytes 9220
  220.9 1.4 copy-start.4
  220.9 1.4 copy-start.37
  221.0 1.4 copy-start.41
  221.4 3.6 copy-start.39
  225.0 16.2 %slice-start.10 = ((s8[6291456]{0:T(1024)(128)(4,1)}), s8[4194304]{0:T(1024)(128)(4,1)S(1)}, s32[]{:S(2)}) async-start(s8[6291456]{0:T(1024)(128)(4,1)} %bitcast.141), calls=%async_computation.10 | async-start | bytes 8388608
  225.0 23.4 %slice-start.4 = ((s8[4718592]{0:T(1024)(128)(4,1)}), s8[4194304]{0:T(1024)(128)(4,1)S(1)}, s32[]{:S(2)}) async-start(s8[4718592]{0:T(1024)(128)(4,1)} %bitcast.121), calls=%async_computation.4 | async-start | bytes 8388608
  229.0 12.2 %slice-start.11 = ((s8[6291456]{0:T(1024)(128)(4,1)}), s8[2097152]{0:T(1024)(128)(4,1)S(1)}, s32[]{:S(2)}) async-start(s8[6291456]{0:T(1024)(128)(4,1)} %bitcast.141), calls=%async_computation.11 | async-start | bytes 4194304
  229.0 19.3 %slice-start.5 = ((s8[4718592]{0:T(1024)(128)(4,1)}), s8[524288]{0:T(1024)(128)(4,1)S(1)}, s32[]{:S(2)}) async-start(s8[4718592]{0:T(1024)(128)(4,1)} %bitcast.121), calls=%async_computation.5 | async-start | bytes 1048576
  241.2 7.1 %copy-start.43 = (bf16[1024,3072]{1,0:T(8,128)(2,1)}, bf16[1024,3072]{1,0:T(8,128)(2,1)S(1)}, u32[]{:S(2)}) copy-start(bf16[1024,3072]{1,0:T(8,128)(2,1)S(1)} %get-tuple-element.92) | copy-start | bytes 18874372
  241.3 7.1 %copy-start.5 = (bf16[1024,768]{0,1:T(8,128)(2,1)S(1)}, bf16[1024,768]{0,1:T(8,128)(2,1)}, u32[]{:S(2)}) copy-start(bf16[1024,768]{0,1:T(8,128)(2,1)} %copy.45) | copy-start | bytes 4718596
  241.3 7.1 %copy-start.9 = (f32[1024,768]{0,1:T(8,128)S(1)}, f32[1024,768]{0,1:T(8,128)}, u32[]{:S(2)}) copy-start(f32[1024,768]{0,1:T(8,128)} %copy-done.8) | copy-start | bytes 9437188
  258.5 4.1 copy-start.10
  258.5 5.6 %copy-start.44 = (bf16[1024,3072]{1,0:T(8,128)(2,1)S(1)}, bf16[1024,3072]{1,0:T(8,128)(2,1)}, u32[]{:S(2)}) copy-start(bf16[1024,3072]{1,0:T(8,128)(2,1)} %copy-done.43) | copy-start | bytes 18874372
  264.1 7.1 %copy-start.21 = (f32[1024,768]{0,1:T(8,128)}, f32[1024,768]{0,1:T(8,128)S(1)}, u32[]{:S(2)}) copy-start(f32[1024,768]{0,1:T(8,128)S(1)} %get-tuple-element.69) | copy-start | bytes 9437188
  264.1 7.1 %copy-start.28 = (bf16[96,8,2,512]{3,1,2,0:T(8,128)(2,1)S(1)}, bf16[96,8,2,512]{3,1,2,0:T(8,128)(2,1)}, u32[]{:S(2)}) copy-start(bf16[96,8,2,512]{3,1,2,0:T(8,128)(2,1)} %copy-done.27) | copy-start | bytes 4718596
  274.2 13.2 %slice-start.8 = ((s8[4718592]{0:T(1024)(128)(4,1)}), s8[524288]{0:T(1024)(128)(4,1)S(1)}, s32[]{:S(2)}) async-start(s8[4718592]{0:T(1024)(128)(4,1)} %bitcast.128), calls=%async_computation.8 | async-start | bytes 1048576
  284.0 3.6 slice-start.9
  287.7 6.8 %copy-start.33 = (bf16[4,3,64,768]{3,2,1,0:T(8,128)(2,1)S(1)}, bf16[4,3,64,768]{3,2,1,0:T(8,128)(2,1)}, u32[]{:S(2)}) copy-start(bf16[4,3,64,768]{3,2,1,0:T(8,128)(2,1)} %slice.106) | copy-start | bytes 3538948
  297.8 4.5 copy-start.7
  297.8 4.5 copy-start.36
  302.4 12.1 %copy-start.14 = (bf16[2,512,12,64]{1,0,3,2:T(2,128)(2,1)}, bf16[2,512,12,64]{1,0,3,2:T(2,128)(2,1)S(1)}, u32[]{:S(2)}) copy-start(bf16[2,512,12,64]{1,0,3,2:T(2,128)(2,1)S(1)} %reshape.212) | copy-start | bytes 4718596
  316.1 4.2 copy-start.13
  338.3 21.6 %copy-start.3 = (bf16[2,512,1,12,64]{1,0,4,3,2:T(2,128)(2,1)S(1)}, bf16[2,512,1,12,64]{1,0,4,3,2:T(2,128)(2,1)}, u32[]{:S(2)}) copy-start(bf16[2,512,1,12,64]{1,0,4,3,2:T(2,128)(2,1)} %copy-done.2) | copy-start | bytes 4718596
  359.9 8.6 %copy-start.1 = (bf16[2,512,1,12,64]{1,0,4,3,2:T(2,128)(2,1)S(1)}, bf16[2,512,1,12,64]{1,0,4,3,2:T(2,128)(2,1)}, u32[]{:S(2)}) copy-start(bf16[2,512,1,12,64]{1,0,4,3,2:T(2,128)(2,1)} %copy-done) | copy-start | bytes 4718596
  379.3 1.4 copy-start.15
  379.3 3.9 copy-start.22
  379.5 5.0 copy-start.20
  380.8 2.4 copy-start.11
  384.5 7.6 %copy-start.26 = (bf16[1024,768]{1,0:T(8,128)(2,1)S(1)}, bf16[1024,768]{1,0:T(8,128)(2,1)}, u32[]{:S(2)}) copy-start(bf16[1024,768]{1,0:T(8,128)(2,1)} %param.10) | copy-start | bytes 4718596
  389.5 10.6 %slice-start.2 = ((s8[4718592]{0:T(1024)(128)(4,1)}), s8[524288]{0:T(1024)(128)(4,1)S(1)}, s32[]{:S(2)}) async-start(s8[4718592]{0:T(1024)(128)(4,1)} %bitcast.111), calls=%async_computation.2 | async-start | bytes 1048576
  392.1 8.0 %slice-start.3 = ((s8[4718592]{0:T(1024)(128)(4,1)}), s8[4194304]{0:T(1024)(128)(4,1)S(1)}, s32[]{:S(2)}) async-start(s8[4718592]{0:T(1024)(128)(4,1)} %bitcast.111), calls=%async_computation.3 | async-start | bytes 8388608
  401.3 1.6 copy-start.40
  401.3 4.3 copy-start.18
  427.4 107.9 %copy-start.23 = (f32[147696]{0:T(1024)S(1)}, f32[147696]{0:T(1024)}, u32[]{:S(2)}) copy-start(f32[147696]{0:T(1024)} %param.14) | copy-start | bytes 1772356
  427.4 107.9 %copy-start.34 = (f32[147696]{0:T(1024)S(1)}, f32[147696]{0:T(1024)}, u32[]{:S(2)}) copy-start(f32[147696]{0:T(1024)} %param.16) | copy-start | bytes 1772356
  427.4 107.9 %copy-start.35 = (f32[147696]{0:T(1024)S(1)}, f32[147696]{0:T(1024)}, u32[]{:S(2)}) copy-start(f32[147696]{0:T(1024)} %param.15) | copy-start | bytes 1772356
  535.2 2.8 copy-start.16
  535.2 2.8 copy-start.29
  535.2 2.8 copy-start.30
  535.2 2.9 copy-start.31

commit v2 on v0

--- a/solution.py
+++ b/solution.py
@@ -1,8 +1,12 @@
+import functools
 import math
+import types
 
 import jax
 import jax.numpy as jnp
 from jax import lax
+from jax.experimental import pallas as pl
+from jax.experimental.pallas import tpu as pltpu
 from jax.sharding import PartitionSpec as P
 
 D = 768
@@ -124,7 +128,7 @@
     return (first_new, second_new, update + decay * master)
 
 
-def body(
+def general_body(
     tokens,
     cotangent,
     segments,
@@ -325,6 +329,1325 @@
     )
 
 
+MESH_ID = pl.DeviceIdType.MESH
+
+
+def when(cond, act):
+    if cond is None:
+        act()
+    else:
+        pl.when(cond)(act)
+
+
+class Place:
+    def __init__(self, levels):
+        self.levels = levels
+        d = lax.axis_index("dp")
+        c = lax.axis_index("rep")
+        self.d, self.c = d, c
+        self.z, y, x = d // 4, (d // 2) % 2, d % 2
+        x_near, y_near = d + 1 - 2 * x, d + 2 - 4 * y
+        self.a_near = x_near + c * (y_near - x_near)
+        self.b_near = y_near + c * (x_near - y_near)
+        self.far = x_near + y_near - d
+        self.a_at = x + c * (y - x)
+        self.b_at = y + c * (x - y)
+        self.up = (d + 4, c)
+        self.down = (d - 4, c)
+        self.has_up = self.z < levels - 1
+        self.has_down = self.z > 0
+        self.across_a = (self.a_near, c)
+        self.across_b = (self.b_near, c)
+        self.sibling = (d, 1 - c)
+
+    def levels_at(self, distance):
+        if distance == 0:
+            return [(self.z, None, 0)]
+        return [
+            (self.z - distance, self.z >= distance, -1),
+            (self.z + distance, self.z + distance < self.levels, 1),
+        ]
+
+    def at(self, column, level):
+        return column + 4 * (level - self.z)
+
+    def along(self, step):
+        return (self.up, self.has_up) if step > 0 else (self.down, self.has_down)
+
+    def meet(self, chain):
+        barrier = pltpu.get_barrier_semaphore()
+
+        def greet(device):
+            pl.semaphore_signal(barrier, inc=1, device_id=device, device_id_type=MESH_ID)
+
+        for device in (self.across_a, self.across_b, self.sibling):
+            greet(device)
+        count = 3
+        edges = [(self.up, self.has_up), (self.down, self.has_down)]
+        if chain:
+            edges += [((self.d + 1, self.c), self.d < 4 * self.levels - 1), ((self.d - 1, self.c), self.d > 0)]
+        for device, there in edges:
+            pl.when(there)(functools.partial(greet, device))
+            count = count + there.astype(jnp.int32)
+        pl.semaphore_wait(barrier, count)
+
+
+def both(first, second):
+    if first is None:
+        return second
+    return first if second is None else first & second
+
+
+class Sends:
+    def __init__(self):
+        self.steps, self.closing = [], False
+
+    def go(self, step):
+        if not any(step is other for other in self.steps):
+            self.steps.append(step)
+        step()
+
+    def later(self, step):
+        return lambda: self.go(step)
+
+    def start(self, cond, make):
+        when(cond, lambda: make().wait_send() if self.closing else make().start())
+
+    def wait(self, cond, make):
+        if not self.closing:
+            when(cond, lambda: make().wait_recv())
+
+    def finish(self):
+        self.closing = True
+        for step in self.steps:
+            step()
+
+
+def remote(src, dst, send_sem, recv_sem, device):
+    return pltpu.make_async_remote_copy(
+        src_ref=src,
+        dst_ref=dst,
+        send_sem=send_sem,
+        recv_sem=recv_sem,
+        device_id=device,
+        device_id_type=MESH_ID,
+    )
+
+
+class Gather:
+    def __init__(self, place, ref, parts, lanes, send_sem, recv_sem, sib_sem):
+        self.place, self.ref, self.parts, self.lanes = place, ref, parts, lanes
+        self.send_sem, self.recv_sem, self.sib_sem = send_sem, recv_sem, sib_sem
+        self.half = ref.shape[2] // 2
+        levels = place.levels
+        self.leave_up = [k + 1 for k in range(levels)]
+        self.leave = (levels, 2 * levels, 4 * levels - 1)
+
+    def rows(self, core):
+        return pl.ds(pl.multiple_of(core * self.half, self.half), self.half)
+
+    def piece(self, chip, core):
+        return self.ref.at[chip, self.parts, self.rows(core), self.lanes]
+
+    def several(self, count):
+        return self.ref.at[pl.ds(0, count), self.parts, pl.ds(0, self.half), self.lanes]
+
+    def send(self, cond, chip, way, device):
+        own = self.piece(chip, self.place.c)
+        recv = self.sib_sem if way == 4 else self.recv_sem.at[chip]
+        when(cond, lambda: remote(own, own, self.send_sem.at[way], recv, device).start())
+
+    def wait(self, cond, part, sem):
+        when(cond, lambda: remote(part, part, self.send_sem.at[0], sem, self.place.sibling).wait_recv())
+
+    def arrived(self, cond, chip):
+        self.wait(cond, self.piece(chip, self.place.c), self.recv_sem.at[chip])
+
+    def own(self):
+        p = self.place
+        self.send(p.has_up, p.d, 0, p.up)
+        self.send(p.has_down, p.d, 1, p.down)
+        self.send(None, p.d, 3, p.across_b)
+        self.send(None, p.d, 2, p.across_a)
+
+    def line(self, distance):
+        p = self.place
+        for level, there, step in p.levels_at(distance):
+            chip = p.at(p.d, level)
+            self.arrived(there, chip)
+            onward, more = p.along(-step)
+            self.send(both(there, more), chip, 0 if step < 0 else 1, onward)
+            self.send(there, chip, 3, p.across_b)
+            self.send(there, chip, 2, p.across_a)
+            self.send(there, chip, 4, p.sibling)
+
+    def over_a(self, distance):
+        p = self.place
+        for level, there, _ in p.levels_at(distance):
+            chip = p.at(p.a_near, level)
+            self.arrived(there, chip)
+            self.send(there, chip, 3, p.across_b)
+            self.send(there, chip, 4, p.sibling)
+
+    def over_b(self, distance):
+        p = self.place
+        for column in (p.b_near, p.far):
+            for level, there, _ in p.levels_at(distance):
+                chip = p.at(column, level)
+                self.arrived(there, chip)
+                self.send(there, chip, 4, p.sibling)
+
+    def from_sibling(self):
+        self.wait(None, self.several(4 * self.place.levels - 1), self.sib_sem)
+
+    def left(self, cond, way, count):
+        part = self.several(count)
+        sem = self.send_sem.at[way]
+        when(cond, lambda: remote(part, part, sem, self.sib_sem, self.place.sibling).wait_send())
+
+    def finish(self):
+        p = self.place
+        for level in range(p.levels):
+            if level < p.levels - 1:
+                self.left(p.z == level, 0, self.leave_up[level])
+            if level > 0:
+                self.left(p.z == level, 1, self.leave_up[p.levels - 1 - level])
+        for way, count in zip((2, 3, 4), self.leave):
+            self.left(None, way, count)
+
+
+class Plane(Gather):
+    def __init__(self, place, ref, parts, lanes, send_sem, recv_sem, sib_sem):
+        super().__init__(place, ref, parts, lanes, send_sem, recv_sem, sib_sem)
+        self.leave_up = [4 * count for count in self.leave_up]
+        self.leave = (1, 2, 4 * place.levels - 1)
+        self.from_a, self.from_b = place.levels, place.levels + 1
+
+    def send(self, cond, chip, way, device):
+        own = self.piece(chip, self.place.c)
+        recv = self.sib_sem if way == 4 else self.recv_sem.at[self.from_a if way == 2 else self.from_b]
+        when(cond, lambda: remote(own, own, self.send_sem.at[way], recv, device).start())
+
+    def own(self):
+        p = self.place
+        self.send(None, p.d, 2, p.across_a)
+        self.send(None, p.d, 3, p.across_b)
+
+    def near(self):
+        p = self.place
+        self.wait(None, self.piece(p.a_near, p.c), self.recv_sem.at[self.from_a])
+        self.send(None, p.a_near, 3, p.across_b)
+        self.send(None, p.a_near, 4, p.sibling)
+
+    def sheet(self, level):
+        return self.ref.at[pl.ds(4 * level, 4), self.parts, self.rows(self.place.c), self.lanes]
+
+    def send_sheet(self, cond, level, way, device):
+        own = self.sheet(level)
+        recv = self.sib_sem if way == 4 else self.recv_sem.at[level]
+        when(cond, lambda: remote(own, own, self.send_sem.at[way], recv, device).start())
+
+    def complete(self):
+        p = self.place
+        self.wait(None, self.several(2), self.recv_sem.at[self.from_b])
+        self.send_sheet(p.has_up, p.z, 0, p.up)
+        self.send_sheet(p.has_down, p.z, 1, p.down)
+        for chip in (p.b_near, p.far):
+            self.send(None, chip, 4, p.sibling)
+
+    def line(self, distance):
+        p = self.place
+        for level, there, step in p.levels_at(distance):
+            self.wait(there, self.sheet(level), self.recv_sem.at[level])
+            onward, more = p.along(-step)
+            self.send_sheet(both(there, more), level, 0 if step < 0 else 1, onward)
+            self.send_sheet(there, level, 4, p.sibling)
+
+
+def steps_of(go, plane):
+    levels = go.place.levels
+    todo = [functools.partial(go.line, 1), plane.near, functools.partial(go.over_a, 0), plane.complete]
+    for distance in range(2, levels):
+        todo.append(functools.partial(go.line, distance))
+        todo.append(functools.partial(go.over_a, distance - 1))
+        todo.append(functools.partial(plane.line, distance - 1))
+    todo.append(functools.partial(go.over_a, levels - 1))
+    todo.append(functools.partial(go.over_b, 0))
+    todo.append(functools.partial(plane.line, levels - 1))
+    return todo + [functools.partial(go.over_b, distance) for distance in range(1, levels)]
+
+
+class Spread:
+    def __init__(self, place, sends, ref, send_sem, recv_sem):
+        self.place, self.sends, self.ref = place, sends, ref
+        self.send_sem, self.recv_sem = send_sem, recv_sem
+
+    def copy(self, way, device):
+        return remote(self.ref, self.ref, self.send_sem.at[way], self.recv_sem, device)
+
+    def wait(self, cond):
+        self.sends.wait(cond, lambda: self.copy(0, self.place.sibling))
+
+    def run(self):
+        p = self.place
+        home = (p.a_at == 1) & (p.b_at == 1)
+        self.wait(home & p.has_up)
+        self.sends.start(home & p.has_down, lambda: self.copy(0, p.down))
+        self.wait((p.a_at == 0) & (p.b_at == 1))
+        self.sends.start(home, lambda: self.copy(1, p.across_a))
+        self.wait(p.b_at == 0)
+        self.sends.start(p.b_at == 1, lambda: self.copy(2, p.across_b))
+
+
+def shifted(ref, start, rows):
+    first, turn = start // 128, start % 128
+    here = pltpu.roll(ref[pl.ds(first, rows), :], (128 - turn) % 128, 1)
+    after = pltpu.roll(ref[pl.ds(first + 1, rows), :], (128 - turn) % 128, 1)
+    lane = lax.broadcasted_iota(jnp.int32, (rows, 128), 1)
+    return jnp.where(lane < 128 - turn, here, after)
+
+
+class Flat:
+    def __init__(self, length, chips, parts, split, turned):
+        self.length, self.chips, self.parts, self.turned = length, chips, parts, turned
+        self.rows = length // D // parts * parts
+        self.slip = length - self.rows * D
+        self.deep = self.rows // parts
+        self.split = split
+        self.lines = self.rows * (D // 128)
+        self.most = self.slip * chips
+        self.halo = -(-self.most // 1024) * 8
+        self.held = -(-length // 1024) * 8
+        self.tail_from = (length - self.most) // 1024 * 8
+        self.tail = self.held - self.tail_from
+
+    def place_of(self, part, block, split):
+        if split:
+            return 6 * part + block, 6 * self.parts
+        return 6 * self.deep * part + block, 6
+
+
+class Lead:
+    def __init__(self, place, sends, flat, long_ref, halo_ref, line_ref, send_sem, recv_sem):
+        self.place, self.sends, self.flat = place, sends, flat
+        self.long_ref, self.halo_ref, self.line_ref = long_ref, halo_ref, line_ref
+        self.send_sem, self.recv_sem = send_sem, recv_sem
+
+    def copy(self):
+        f, p = self.flat, self.place
+        return remote(
+            self.long_ref.at[pl.ds(f.halo + f.tail_from, f.tail), :],
+            self.halo_ref.at[pl.ds(0, f.tail), :],
+            self.send_sem,
+            self.recv_sem,
+            (p.d + 1, p.c),
+        )
+
+    def begin(self):
+        self.sends.start(self.place.d < self.flat.chips - 1, self.copy)
+
+    def lines(self):
+        p, f = self.place, self.flat
+        slip = f.slip * p.d
+        self.line_ref[pl.ds(0, f.lines), :] = shifted(self.long_ref, f.halo * 128 - slip, f.lines)
+
+        def mend():
+            self.copy().wait_recv()
+            before = shifted(self.halo_ref, f.length - f.tail_from * 128 - slip, f.halo)
+            at = lax.broadcasted_iota(jnp.int32, (f.halo, 128), 0) * 128
+            at = at + lax.broadcasted_iota(jnp.int32, (f.halo, 128), 1)
+            self.line_ref[pl.ds(0, f.halo), :] = jnp.where(at < slip, before, self.line_ref[pl.ds(0, f.halo), :])
+
+        pl.when(p.d > 0)(mend)
+
+    def store(self, out_ref):
+        p, f = self.place, self.flat
+
+        def put(split):
+            for part in range(f.parts):
+                for block in range(D // 128):
+                    first, stride = f.place_of(part, block, split)
+                    out_ref[p.d, part, :, pl.ds(128 * block, 128)] = self.line_ref[
+                        pl.ds(first, f.deep, stride=stride), :
+                    ].astype(jnp.bfloat16)
+
+        pl.when(p.d < f.split)(lambda: put(True))
+        pl.when(p.d >= f.split)(lambda: put(False))
+
+    def last_rows(self, count):
+        f = self.flat
+        lines = -(-count * 6 // 8) * 8
+        return shifted(self.long_ref, f.halo * 128 + f.length - count * D, lines)
+
+
+class Reduce:
+    def __init__(self, place, parts, chips, batches, view, slots, extra, kept, send_sem, recv_sem, whole=None):
+        self.place, self.parts, self.batches = place, parts, batches
+        self.view, self.slots, self.extra, self.kept = view, slots, extra, kept
+        self.send_sem, self.recv_sem, self.whole = send_sem, recv_sem, whole
+        self.levels = [level for batch in batches for level in batch]
+        self.from_b, self.from_a = chips, chips + 2 * place.levels
+        self.from_z = chips + 3 * place.levels
+
+    @staticmethod
+    def semaphores(batches):
+        return 4 * len(batches) + 2 * sum(map(len, batches))
+
+    def arrival(self, kind, batch):
+        return self.recv_sem.at[4 * batch + kind]
+
+    def along(self, way, level):
+        return self.recv_sem.at[4 * len(self.batches) + 2 * self.levels.index(level) + way]
+
+    def wait(self, part, sem):
+        remote(part, part, self.send_sem.at[0], sem, self.place.sibling).wait_recv()
+
+    def send(self, cond, chip, way, dst, recv, device):
+        p = self.place
+        src = self.view(chip, 1 - p.c if way == 4 else p.c)
+        when(cond, lambda: remote(src, dst, self.send_sem.at[way], recv, device).start())
+
+    def add(self, chip, src):
+        here = self.view(chip, self.place.c)
+        for part in range(self.parts):
+            here[part] = here[part] + src[part]
+
+    def share(self, batch):
+        p = self.place
+        recv = self.arrival(0, batch)
+        if self.whole is not None:
+            src, dst = self.whole
+            remote(src, dst, self.send_sem.at[4], recv, p.sibling).start()
+            return
+        for level in self.batches[batch]:
+            for column in (p.far, p.b_near, p.a_near, p.d):
+                chip = p.at(column, level)
+                self.send(None, chip, 4, self.slots(chip, 1), recv, p.sibling)
+
+    def over_b(self, batch):
+        p = self.place
+        levels = self.batches[batch]
+        self.wait(self.slots(4 * levels[0], 4 * len(levels)), self.arrival(0, batch))
+        for kind, column in ((1, p.far), (0, p.b_near)):
+            for level in levels:
+                chip = p.at(column, level)
+                self.add(chip, self.slots(chip, 1))
+                dst = self.slots(self.from_b + p.levels * kind + level, 1)
+                self.send(None, chip, 3, dst, self.arrival(1 + kind, batch), p.across_b)
+
+    def over_a(self, batch):
+        p = self.place
+        levels = self.batches[batch]
+        first = self.from_b + p.levels
+        self.wait(self.slots(first + levels[0], len(levels)), self.arrival(2, batch))
+        for level in levels:
+            chip = p.at(p.a_near, level)
+            self.add(chip, self.slots(chip, 1))
+            self.add(chip, self.slots(first + level, 1))
+            self.send(None, chip, 2, self.slots(self.from_a + level, 1), self.arrival(3, batch), p.across_a)
+
+    def collect(self, batch):
+        p = self.place
+        levels = self.batches[batch]
+        self.wait(self.slots(self.from_b + levels[0], len(levels)), self.arrival(1, batch))
+        self.wait(self.slots(self.from_a + levels[0], len(levels)), self.arrival(3, batch))
+        for level in levels:
+            chip = p.at(p.d, level)
+            for first in (0, self.from_b, self.from_a):
+                self.add(chip, self.slots(first + level if first else chip, 1))
+
+    def pass_on(self, here, level, way, waits, dst, device):
+        p = self.place
+        chip = p.at(p.d, level)
+        slot = self.slots(self.from_z + level, 1)
+
+        def act():
+            if waits:
+                self.wait(slot, self.along(way, level))
+                self.add(chip, slot)
+            self.send(None, chip, way, dst, self.along(way, level), device)
+
+        pl.when(here)(act)
+
+    def line(self, distance, batch):
+        p = self.place
+        for level in self.batches[batch]:
+            slot = self.slots(self.from_z + level, 1)
+            if level >= distance:
+                self.pass_on(p.z == level - distance, level, 0, level > distance, slot, p.up)
+            if level + distance < p.levels:
+                dst = slot if distance > 1 else self.extra
+                self.pass_on(p.z == level + distance, level, 1, level + distance < p.levels - 1, dst, p.down)
+
+    def keep(self):
+        p = self.place
+        own = self.kept(p.c)
+
+        def at(level):
+            here = self.view(p.d, p.c)
+            for part in range(self.parts):
+                own[part] = here[part].astype(jnp.float32)
+            sources = [(0, self.slots(self.from_z + level, 1))] if level > 0 else []
+            sources += [(1, self.extra)] if level < p.levels - 1 else []
+            for way, src in sources:
+                self.wait(src, self.along(way, level))
+                for part in range(self.parts):
+                    own[part] = own[part] + src[part].astype(jnp.float32)
+
+        for level in self.levels:
+            pl.when(p.z == level)(functools.partial(at, level))
+
+    def left(self, cond, way, count):
+        part = self.slots(0, count)
+        sem = self.send_sem.at[way]
+        when(cond, lambda: remote(part, part, sem, self.recv_sem.at[0], self.place.sibling).wait_send())
+
+    def finish(self):
+        p = self.place
+        count = len(self.levels)
+        for way, pieces in ((4, 4 * count), (3, 2 * count), (2, count)):
+            self.left(None, way, pieces)
+        for z in range(p.levels):
+            for way, pieces in enumerate((sum(n > z for n in self.levels), sum(n < z for n in self.levels))):
+                if pieces:
+                    self.left(p.z == z, way, pieces)
+
+
+def handed(place, own_ref, core, send_sem, recv_sem):
+    own = own_ref.at[core]
+    return remote(own, own, send_sem, recv_sem, place.sibling)
+
+
+class Terms:
+    def __init__(self, place, sends, ref, got_ref, all_ref, send_sem, recv_sem):
+        self.place, self.sends, self.ref, self.got_ref, self.all_ref = place, sends, ref, got_ref, all_ref
+        self.send_sem, self.recv_sem = send_sem, recv_sem
+
+    def copy(self, way, core, device):
+        return remote(self.ref.at[core], self.got_ref.at[way], self.send_sem.at[way], self.recv_sem.at[way], device)
+
+    def add(self, cond, way):
+        if self.sends.closing:
+            return
+
+        def act():
+            self.copy(way, 0, self.place.sibling).wait_recv()
+            self.ref[self.place.c] = self.ref[self.place.c] + self.got_ref[way]
+
+        when(cond, act)
+
+    def share(self):
+        self.sends.start(None, lambda: self.copy(0, 1 - self.place.c, self.place.sibling))
+
+    def over_b(self):
+        p = self.place
+        self.add(None, 0)
+        self.sends.start(p.b_at == 0, lambda: self.copy(1, p.c, p.across_b))
+
+    def over_a(self):
+        p = self.place
+        self.add(p.b_at == 1, 1)
+        self.sends.start((p.b_at == 1) & (p.a_at == 0), lambda: self.copy(2, p.c, p.across_a))
+
+    def line(self, distance):
+        p = self.place
+        home = (p.b_at == 1) & (p.a_at == 1) & (p.z == p.levels - 1 - distance)
+        self.add(home, 2)
+        if distance < p.levels - 1:
+            self.add(home, 3)
+        if distance > 0:
+            self.sends.start(home, lambda: self.copy(3, p.c, p.up))
+
+    def final(self):
+        return remote(
+            self.ref.at[self.place.c],
+            self.all_ref.at[self.place.c],
+            self.send_sem.at[4],
+            self.recv_sem.at[4],
+            self.place.sibling,
+        )
+
+    def hand_over(self):
+        p = self.place
+        self.sends.start(p.d == 4 * p.levels - 1, self.final)
+
+    def take_over(self):
+        self.final().wait_recv()
+        self.all_ref[self.place.c] = self.ref[self.place.c]
+
+
+class Trail:
+    def __init__(self, place, sends, flat, own_ref, line_ref, out_ref, send_sem, recv_sem):
+        self.place, self.sends, self.flat = place, sends, flat
+        self.own_ref, self.line_ref, self.out_ref = own_ref, line_ref, out_ref
+        self.send_sem, self.recv_sem = send_sem, recv_sem
+
+    def copy(self):
+        f, p = self.flat, self.place
+        return remote(
+            self.line_ref.at[pl.ds(0, f.halo), :],
+            self.line_ref.at[pl.ds(f.lines, f.halo), :],
+            self.send_sem,
+            self.recv_sem,
+            (p.d - 1, p.c),
+        )
+
+    def lines(self):
+        p, f = self.place, self.flat
+        half = f.deep // 2
+
+        def put(split):
+            for core in range(2):
+                for part in range(f.parts):
+                    for block in range(D // 128):
+                        first, stride = f.place_of(part, block, split)
+                        first = first + stride * half * core
+                        self.line_ref[pl.ds(first, half, stride=stride), :] = self.own_ref[
+                            core, part, :, pl.ds(128 * block, 128)
+                        ]
+
+        def put_turned():
+            for j in range(f.rows // 128):
+                blocks = []
+                for i in range(D // f.deep):
+                    lanes = pl.ds(128 * (3 * (i % 2) + j), 128)
+                    blocks += [self.own_ref[core, i // 2, :, lanes] for core in range(2)]
+                turned = jnp.concatenate(blocks, 0).T
+                for block in range(D // 128):
+                    first = 6 * 128 * j + block
+                    self.line_ref[pl.ds(first, 128, stride=6), :] = turned[:, 128 * block : 128 * (block + 1)]
+
+        pl.when(p.d < f.split)(lambda: put(True))
+        pl.when(p.d >= f.split)(put_turned if f.turned else lambda: put(False))
+
+    def pass_back(self):
+        self.sends.start(self.place.d > 0, self.copy)
+
+    def last_rows(self, terms_ref, at, count):
+        f = self.flat
+        for core in range(2):
+            for block in range(3):
+                self.line_ref[pl.ds(f.lines + 3 * core + block, count, stride=6), :] = terms_ref[
+                    core, pl.ds(at, count), pl.ds(128 * block, 128)
+                ]
+
+    def out(self):
+        p, f = self.place, self.flat
+        pl.when(p.d < f.chips - 1)(lambda: self.copy().wait_recv())
+        self.out_ref[pl.ds(0, f.held), :] = shifted(self.line_ref, f.slip * p.d, f.held)
+
+
+def dot(a, b):
+    return jnp.dot(a, b, preferred_element_type=jnp.float32)
+
+
+def dot_nt(a, b):
+    return lax.dot_general(a, b, (((1,), (1,)), ((), ())), preferred_element_type=jnp.float32)
+
+
+def square(values):
+    return values.reshape(D, D)
+
+
+def tile(index, size):
+    return pl.ds(pl.multiple_of(index * size, size), size)
+
+
+def loop(count, step, beside=()):
+    def body(i, _):
+        step(i)
+        for at, act in beside:
+            pl.when(i == at)(act)
+        return 0
+
+    lax.fori_loop(0, count, body, 0)
+
+
+TILE = 256
+
+
+class Layer:
+    def __init__(self, refs, att_split, ffn_split, seqs, length):
+        self.__dict__.update(refs)
+        self.att_split, self.ffn_split = att_split, ffn_split
+        self.seqs, self.length = seqs, length
+        self.tiles = seqs * length // TILE
+
+    def whole(self, blocks, part):
+        count = blocks.shape[0] // 4
+        return blocks[pl.ds(count * part, count)].reshape(self.seqs * self.length, D)
+
+    def some(self, blocks, part, r):
+        count = TILE // blocks.shape[1]
+        return pl.ds(blocks.shape[0] // 4 * part + count * r, count)
+
+    def qkv_weight(self, part):
+        return square(self.att_w[pl.ds(0, self.att_split), part])
+
+    def out_weight(self):
+        return square(self.att_w[pl.ds(self.att_split, self.att_w.shape[0] - self.att_split)])
+
+    def in_weight(self, part):
+        return square(self.ffn_w[pl.ds(0, self.ffn_split), part])
+
+    def down_weight(self, part):
+        return square(self.ffn_w[pl.ds(self.ffn_split + 2 * part, 2)])
+
+    def term(self, row):
+        return self.terms[pl.ds(row, 1), :]
+
+    def add_term(self, row, values):
+        self.term_grads[pl.ds(row, 1), :] += jnp.sum(values, 0, keepdims=True)
+
+
+    def qkv(self, beside=()):
+        def step(r):
+            rows = tile(r, TILE)
+            x = self.tok[rows, :]
+            queries = (dot(x, self.qkv_weight(0)) + self.term(0)).astype(jnp.bfloat16)
+            self.heads[0, rows, :] = queries * HEAD_DIM ** (-0.5)
+            self.heads[1, rows, :] = dot(x, self.qkv_weight(1)).astype(jnp.bfloat16)
+            self.heads[2, rows, :] = (dot(x, self.qkv_weight(2)) + self.term(1)).astype(jnp.bfloat16)
+
+        loop(self.tiles, step, beside)
+
+    def make_bias(self):
+        for seq in range(self.seqs):
+            same = self.seg_col[:, seq : seq + 1] == self.seg_row[seq : seq + 1, :]
+            self.bias[pl.ds(seq * self.length, self.length), :] = jnp.where(same, 0.0, masked)
+
+    def lane_half(self, half):
+        lane = lax.broadcasted_iota(jnp.int32, (self.length, 2 * HEAD_DIM), 1)
+        return (lane // HEAD_DIM) == half
+
+    def attend(self, beside=()):
+        self.make_bias()
+
+        def step(i):
+            seq, pair = i // (HEADS // 2), i % (HEADS // 2)
+            lanes = tile(pair, 2 * HEAD_DIM)
+            rows = tile(seq, self.length)
+            queries, keys, values = (self.heads[j, rows, lanes] for j in range(3))
+            values_t = values.T
+            parts = []
+            for half in range(2):
+                own = jnp.where(self.lane_half(half), queries, jnp.zeros_like(queries))
+                scores = dot_nt(keys, own) + self.bias[rows, :]
+                top = jnp.max(scores, 0, keepdims=True)
+                raised = jnp.exp(scores - top)
+                total = jnp.sum(raised, 0, keepdims=True)
+                probs = (raised * (1.0 / total)).astype(jnp.bfloat16)
+                self.totals[pl.ds(HEADS * seq + 2 * pair + half, 1), :] = top + jnp.log(total)
+                parts.append(dot(values_t[HEAD_DIM * half : HEAD_DIM * (half + 1)], probs))
+            both_t = jnp.concatenate(parts, 0).astype(jnp.bfloat16)
+            self.ctx_t[lanes, rows] = both_t
+            self.ctx[rows, lanes] = both_t.T
+
+        loop(self.seqs * HEADS // 2, step, beside)
+
+    def first_norm(self, beside=()):
+        def step(r):
+            rows = tile(r, TILE)
+            residual = self.tok[rows, :].astype(jnp.float32) + dot(self.ctx[rows, :], self.out_weight()) + self.term(2)
+            first, normed, rstd = normalize(residual, self.term(3), self.term(4))
+            self.hat[rows, :] = normed
+            self.rstd[rows, :] = rstd
+            self.low_t[:, rows] = first.astype(jnp.bfloat16).T
+
+        loop(self.tiles, step, beside)
+
+    def feed(self, beside=()):
+        def step(r):
+            rows = tile(r, TILE)
+            first = self.hat[rows, :] * self.term(3) + self.term(4)
+            low = first.astype(jnp.bfloat16)
+            second = first + self.term(12)
+            for part in range(4):
+                inner = dot(low, self.in_weight(part)) + self.term(8 + part)
+                cdf, slope = gelu_parts(inner)
+                act = (inner * cdf).astype(jnp.bfloat16)
+                self.act[self.some(self.act, part, r)] = act.reshape(-1, self.act.shape[1], D)
+                slope = slope.astype(jnp.bfloat16).reshape(-1, self.slope.shape[1], D)
+                self.slope[self.some(self.slope, part, r)] = slope
+                second = second + dot(act, self.down_weight(part))
+            out, normed, rstd = normalize(second, self.term(13), self.term(14))
+            seq = r // (self.length // TILE)
+            grad_out = self.cot[rows, :].astype(jnp.float32) * self.live[pl.ds(seq, 1), 0:1]
+            self.out[rows, :] = out.astype(jnp.bfloat16)
+            scaled = grad_out * self.term(13)
+            grad = rstd * (
+                scaled
+                - jnp.mean(scaled, -1, keepdims=True)
+                - normed * jnp.mean(scaled * normed, -1, keepdims=True)
+            )
+            self.add_term(13, grad_out * normed)
+            self.add_term(14, grad_out)
+            grad_down = grad.astype(jnp.bfloat16)
+            self.add_term(12, grad_down.astype(jnp.float32))
+            self.grad[rows, :] = grad
+            self.down[rows, :] = grad_down
+            self.down_t[:, rows] = grad_down.T
+
+        loop(self.tiles, step, beside)
+
+
+    def hidden_back(self, part, beside=()):
+        def step(r):
+            rows = tile(r, TILE)
+            grad_act = dot_nt(self.down[rows, :], self.down_weight(part))
+            at = self.some(self.slope, part, r)
+            slope = self.slope[at].reshape(TILE, D).astype(jnp.float32)
+            inner = (grad_act * slope).astype(jnp.bfloat16)
+            self.slope[at] = inner.reshape(-1, self.slope.shape[1], D)
+            self.add_term(8 + part, inner.astype(jnp.float32))
+
+        loop(self.tiles, step, beside)
+
+    def down_grads(self, part, beside=()):
+        deep = self.ffn_w.shape[2]
+        first = self.ffn_split + 2 * part
+
+        def step(m):
+            grads = dot(self.down_t[tile(m, 2 * deep), :], self.whole(self.act, part)).astype(jnp.bfloat16)
+            for owner in range(2):
+                for block in range(6):
+                    at = 128 * (3 * owner + block % 3)
+                    self.ffn_w[first + owner, m, :, pl.ds(128 * block, 128)] = grads[
+                        deep * (block // 3) : deep * (block // 3 + 1), at : at + 128
+                    ]
+
+        loop(4, step, beside)
+
+    def in_back(self, part, beside=()):
+        def step(r):
+            rows = tile(r, TILE)
+            self.grad[rows, :] += dot_nt(
+                self.slope[self.some(self.slope, part, r)].reshape(TILE, D), self.in_weight(part)
+            )
+
+        loop(self.tiles, step, beside)
+
+    def in_grads(self, part, beside=()):
+        deep = self.ffn_w.shape[2]
+
+        def step(m):
+            grads = dot(self.low_t[tile(m, 2 * deep), :], self.whole(self.slope, part)).astype(jnp.bfloat16)
+            self.ffn_w[pl.ds(2 * m, 2), part] = grads.reshape(2, deep, D)
+
+        loop(4, step, beside)
+
+    def first_back(self, beside=()):
+        def step(r):
+            rows = tile(r, TILE)
+            grad_first, normed = self.grad[rows, :], self.hat[rows, :]
+            scaled = grad_first * self.term(3)
+            grad = self.rstd[rows, :] * (
+                scaled
+                - jnp.mean(scaled, -1, keepdims=True)
+                - normed * jnp.mean(scaled * normed, -1, keepdims=True)
+            )
+            self.add_term(3, grad_first * normed)
+            self.add_term(4, grad_first)
+            proj = grad.astype(jnp.bfloat16)
+            self.add_term(2, proj.astype(jnp.float32))
+            self.grad[rows, :] = grad
+            shape = (-1, self.act.shape[1], D)
+            self.act[self.some(self.act, 3, r)] = proj.reshape(shape)
+            grad_context = dot_nt(proj, self.out_weight()).astype(jnp.bfloat16)
+            self.act[self.some(self.act, 0, r)] = grad_context.reshape(shape)
+            self.tok_t[:, rows] = self.tok[rows, :].T
+
+        loop(self.tiles, step, beside)
+
+    def out_grads(self, beside=()):
+        def step(m):
+            grads = dot(self.ctx_t[tile(m, 192), :], self.whole(self.act, 3)).astype(jnp.bfloat16)
+            self.att_w[self.att_split + m] = grads.reshape(self.att_w.shape[1:])
+
+        loop(4, step, beside)
+
+    def attend_back(self, group, beside=()):
+        def step(i):
+            seq, pair = i % self.seqs, 2 * group + i // self.seqs
+            lanes = tile(pair, 2 * HEAD_DIM)
+            rows = tile(seq, self.length)
+            count = self.length // self.act.shape[1]
+            queries, keys, values = (self.heads[j, rows, lanes] for j in range(3))
+            grads = self.act[pl.ds(count * seq, count), :, lanes].reshape(self.length, 2 * HEAD_DIM)
+            keys_t = keys.T
+            parts = []
+            grad_keys = grad_values = 0.0
+            for half in range(2):
+                here = self.lane_half(half)
+                own = jnp.where(here, queries, jnp.zeros_like(queries))
+                own_grads = jnp.where(here, grads, jnp.zeros_like(grads))
+                total = self.totals[pl.ds(HEADS * seq + 2 * pair + half, 1), :]
+                probs = jnp.exp(dot_nt(keys, own) + self.bias[rows, :] - total)
+                grad_values = grad_values + dot(probs.astype(jnp.bfloat16), own_grads)
+                grad_probs = dot_nt(values, own_grads)
+                row_sum = jnp.sum(probs * grad_probs, 0, keepdims=True)
+                grad_scores = (probs * (grad_probs - row_sum)).astype(jnp.bfloat16)
+                grad_keys = grad_keys + dot(grad_scores, own)
+                parts.append(dot(keys_t[HEAD_DIM * half : HEAD_DIM * (half + 1)], grad_scores))
+            grad_queries = (jnp.concatenate(parts, 0) * HEAD_DIM ** (-0.5)).astype(jnp.bfloat16).T
+            grad_values = grad_values.astype(jnp.bfloat16)
+            self.heads[0, rows, lanes] = grad_queries
+            self.heads[1, rows, lanes] = grad_keys.astype(jnp.bfloat16)
+            self.heads[2, rows, lanes] = grad_values
+            for row, grad in ((0, grad_queries), (1, grad_values)):
+                self.term_grads[pl.ds(row, 1), lanes] += jnp.sum(grad.astype(jnp.float32), 0, keepdims=True)
+
+        loop(2 * self.seqs, step, beside)
+
+    def qkv_grads(self, group):
+        lanes = pl.ds(4 * HEAD_DIM * group, 4 * HEAD_DIM)
+        deep = self.att_w.shape[2]
+
+        def step(part):
+            grads = dot(self.tok_t[...], self.heads[part, :, lanes]).astype(jnp.bfloat16)
+            for chip in range(self.att_split):
+                self.act[self.act_first + 3 * chip + part, :, lanes] = grads[deep * chip : deep * (chip + 1)]
+
+        loop(3, step)
+
+    def input_back(self, beside=()):
+        def step(r):
+            rows = tile(r, TILE)
+            total = self.grad[rows, :]
+            for part in range(3):
+                total = total + dot_nt(self.heads[part, rows, :], self.qkv_weight(part))
+            self.gin[rows, :] = total.astype(jnp.bfloat16)
+
+        loop(self.tiles, step, beside)
+
+
+def gelu_parts(values):
+    cdf = 0.5 * (1.0 + lax.erf(values * 0.5**0.5))
+    return cdf, cdf + values * jnp.exp(-0.5 * values * values) * (2.0 * math.pi) ** (-0.5)
+
+
+def batches(levels):
+    return [(level,) for level in range(levels)], [(levels - 1,)], [tuple(range(levels - 1))]
+
+
+def scratch_shapes(levels, att, ffn, rows, seqs, length):
+    bf16, f32 = jnp.bfloat16, jnp.float32
+    vmem, dma = pltpu.VMEM, pltpu.SemaphoreType.DMA
+    chips = att.chips
+    turned = vmem((D, rows), bf16)
+    f_batches, o_batches, q_batches = batches(levels)
+    shapes = dict(
+        att_w=vmem((chips, att.parts, att.deep, D), bf16),
+        ffn_w=vmem((chips, ffn.parts, ffn.deep, D), bf16),
+        tok=vmem((rows, D), bf16),
+        heads=vmem((3, rows, D), bf16),
+        totals=vmem((seqs * HEADS, length), f32),
+        ctx=vmem((rows, D), bf16),
+        ctx_t=turned,
+        hat=vmem((rows, D), f32),
+        rstd=vmem((rows, 1), f32),
+        low_t=turned,
+        act=vmem((4 * rows // att.deep, att.deep, D), bf16),
+        slope=vmem((8 * rows // att.deep, att.deep // 2, D), bf16),
+        grad=vmem((rows, D), f32),
+        down_t=turned,
+        terms=vmem((16, D), f32),
+        term_grads=vmem((16, D), f32),
+        spare=vmem((48, 128), f32),
+        terms_sum=vmem((2, 16, D // 2), f32),
+        terms_got=vmem((4, 16, D // 2), f32),
+        terms_all=vmem((2, 16, D // 2), f32),
+        ffn_slots=vmem((chips + 4 * levels, ffn.parts, ffn.deep // 2, D), bf16),
+        local_sem=dma((8,)),
+        term_send=dma((3,)),
+        term_recv=dma,
+        sum_send=dma((5,)),
+        sum_recv=dma((5,)),
+        free=pltpu.SemaphoreType.REGULAR,
+        f_send=dma((5,)),
+        f_recv=dma((Reduce.semaphores(f_batches),)),
+        o_send=dma((5,)),
+        o_recv=dma((Reduce.semaphores(o_batches),)),
+        q_send=dma((3, 5)),
+        q_recv=dma((3, Reduce.semaphores(q_batches))),
+    )
+    for name, flat in (("att_", att), ("ffn_", ffn)):
+        half = (flat.parts, flat.deep // 2, D)
+        own = dict(
+            long=vmem((flat.halo + flat.held + 8, 128), f32),
+            halo=vmem((flat.tail + flat.halo + 8, 128), f32),
+            line=vmem((flat.lines + flat.halo + 8, 128), f32),
+            own=vmem((2, *half), f32),
+            extra=vmem(half, bf16),
+            send=dma((5,)),
+            recv=dma((chips,)),
+            sib=dma,
+            plane_send=dma((5,)),
+            plane_recv=dma((levels + 2,)),
+            plane_sib=dma,
+            halo_send=dma,
+            halo_recv=dma,
+            own_send=dma,
+            own_recv=dma,
+            back_send=dma,
+            back_recv=dma,
+        )
+        shapes.update({name + key: shape for key, shape in own.items()})
+    return shapes
+
+
+def spaced(acts, first, every=1):
+    return tuple((first + every * i, act) for i, act in enumerate(acts))
+
+
+def run(acts):
+    for act in acts:
+        act()
+
+
+def layer_kernel(names, levels, att, ffn, seqs, length, att_in, ffn_in, tok_in, cot_in, seg_row, seg_col, live,
+                 out_out, gin_out, att_out, ffn_out, *scratch):
+    s = types.SimpleNamespace(**dict(zip(names, scratch)))
+    act_first = s.act.shape[0] // 4
+    refs = dict(vars(s), seg_row=seg_row, seg_col=seg_col, live=live)
+    refs.update(cot=s.tok, out=s.tok, down=s.ctx, tok_t=s.low_t)
+    refs.update(bias=s.hat.at[:, pl.ds(0, length)], gin=s.tok, act_first=act_first)
+    work = Layer(refs, att.split, ffn.split, seqs, length)
+
+    def local(src, dst, at):
+        copy = pltpu.make_async_copy(src, dst, s.local_sem.at[at])
+        copy.start()
+        return copy
+
+    p = Place(levels)
+    get_a = local(att_in, s.att_long.at[pl.ds(att.halo, att.held), :], 0)
+    get_f = local(ffn_in, s.ffn_long.at[pl.ds(ffn.halo, ffn.held), :], 1)
+    get_t = local(tok_in, s.tok, 2)
+    p.meet(True)
+    sends = Sends()
+    lead_a = Lead(p, sends, att, s.att_long, s.att_halo, s.att_line, s.att_halo_send, s.att_halo_recv)
+    lead_f = Lead(p, sends, ffn, s.ffn_long, s.ffn_halo, s.ffn_line, s.ffn_halo_send, s.ffn_halo_recv)
+    get_a.wait()
+    sends.go(lead_a.begin)
+    get_f.wait()
+    sends.go(lead_f.begin)
+    lead_a.lines()
+    lead_a.store(s.att_w)
+    def gathers(ref, cut, *sems):
+        parts, lanes = ref.shape[1], pl.ds(0, D)
+        if cut[0]:
+            first, last = (pl.ds(0, parts - cut[0]), lanes), (pl.ds(parts - cut[0], cut[0]), lanes)
+        else:
+            first = (pl.ds(0, parts), pl.ds(0, D - cut[1]))
+            last = (pl.ds(0, parts), pl.ds(D - cut[1], cut[1]))
+        go, plane = Gather(p, ref, *first, *sems[:3]), Plane(p, ref, *last, *sems[3:])
+        return [go.own, plane.own, *steps_of(go, plane)], (go, plane)
+
+    steps_a, go_a = gathers(
+        s.att_w, (0, 128), s.att_send, s.att_recv, s.att_sib, s.att_plane_send, s.att_plane_recv, s.att_plane_sib
+    )
+    steps_f, go_f = gathers(
+        s.ffn_w, (1, 0), s.ffn_send, s.ffn_recv, s.ffn_sib, s.ffn_plane_send, s.ffn_plane_recv, s.ffn_plane_sib
+    )
+    run(steps_a[:2])
+
+    def last():
+        terms, spare = s.terms, s.spare
+        terms[...] = jnp.zeros(terms.shape, terms.dtype)
+        for lead, at, count in ((lead_a, 0, 5), (lead_f, 8, 7)):
+            rows = lead.last_rows(count)
+            spare[pl.ds(0, rows.shape[0]), :] = rows
+            for block in range(D // 128):
+                terms[pl.ds(at, count), pl.ds(128 * block, 128)] = spare[pl.ds(block, count, stride=6), :]
+
+    pl.when(p.d == att.chips - 1)(last)
+    lead_f.lines()
+    lead_f.store(s.ffn_w)
+    s.term_grads[...] = jnp.zeros(s.term_grads.shape, jnp.float32)
+    run(steps_a[2:5])
+    run(steps_f[:2])
+    run(steps_a[5:])
+    sends.go(Spread(p, sends, s.terms, s.term_send, s.term_recv).run)
+    for go in go_a:
+        go.from_sibling()
+    get_t.wait()
+
+    rest = steps_f[2:]
+    work.qkv(spaced(rest[:4], 0))
+    work.attend(spaced(rest[4:16], 0))
+    work.first_norm(spaced(rest[16:20], 0))
+    run(rest[20:])
+    get_c = local(cot_in, s.tok, 2)
+    for go in go_f:
+        go.from_sibling()
+    get_c.wait()
+    work.feed()
+    put_o = local(s.tok, out_out, 3)
+    sends.finish()
+    for go in (*go_a, *go_f):
+        go.finish()
+
+    sums = Sends()
+    slots, slope, act = s.ffn_slots, s.slope, s.act
+    half_a, half_f = att.deep // 2, ffn.deep // 2
+
+    def of(ref, half):
+        return lambda chip, core: ref.at[chip, :, tile(core, half), :]
+
+    def att_slots(lanes):
+        return lambda i, count: slope.at[pl.ds(3 * i, 3 * count), :, lanes]
+
+    f_batches, o_batches, q_batches = batches(levels)
+    everything = pl.ds(0, D)
+    ffn_slots = lambda i, count: slots.at[i] if count == 1 else slots.at[pl.ds(i, count)]
+    add_f = Reduce(
+        p, 4, ffn.chips, f_batches, of(s.ffn_w, half_f), ffn_slots, s.ffn_extra,
+        lambda core: s.ffn_own.at[core], s.f_send, s.f_recv,
+    )
+    add_o = Reduce(
+        p, 3, att.chips, o_batches, of(s.att_w, half_a), att_slots(everything), s.att_extra,
+        lambda core: s.att_own.at[core], s.o_send, s.o_recv,
+    )
+    add_q = []
+    for group in range(3):
+        lanes = pl.ds(256 * group, 256)
+        blocks = pl.ds(act_first, 3 * att.split)
+        view = lambda chip, core, lanes=lanes: act.at[pl.ds(act_first + 3 * chip, 3), tile(core, half_a), lanes]
+        whole = (act.at[blocks, tile(1 - p.c, half_a), lanes], slope.at[pl.ds(0, 3 * att.split), :, lanes])
+        add_q.append(
+            Reduce(
+                p, 3, att.chips, q_batches, view, att_slots(lanes), s.att_extra.at[:, :, lanes],
+                lambda core, lanes=lanes: s.att_own.at[core, :, :, lanes], s.q_send.at[group], s.q_recv.at[group], whole,
+            )
+        )
+    add_t = Terms(p, sums, s.terms_sum, s.terms_got, s.terms_all, s.sum_send, s.sum_recv)
+
+    def do(act, *at):
+        return sums.later(functools.partial(act, *at))
+
+    def q(group, act, *at):
+        return functools.partial(act, add_q[group], *at, 0)
+
+    def f(act, *at):
+        return functools.partial(act, *at)
+
+    work.hidden_back(0)
+    work.down_grads(0)
+    work.hidden_back(1)
+    work.down_grads(1)
+    f(add_f.share, 2)()
+    put_o.wait()
+    get_t = local(tok_in, s.tok, 2)
+    work.hidden_back(2)
+    work.down_grads(2, ((0, f(add_f.over_b, 2)),))
+    work.hidden_back(3)
+    work.down_grads(3)
+    f(add_f.share, 3)()
+    work.in_back(0, ((3, f(add_f.over_b, 3)),))
+    work.in_grads(0)
+    work.in_back(1, ((2, f(add_f.over_a, 2)),))
+    work.in_grads(1)
+    work.in_back(2)
+    work.in_grads(2)
+    work.in_back(3, ((2, f(add_f.collect, 2)), (2, f(add_f.line, 2, 2))))
+    work.in_grads(3, ((1, f(add_f.over_a, 3)),))
+    f(add_f.share, 0)()
+    f(add_f.share, 1)()
+
+    def greet(device):
+        pl.semaphore_signal(s.free, inc=1, device_id=device, device_id_type=MESH_ID)
+
+    for device in (p.sibling, p.across_a, p.across_b):
+        greet(device)
+    pl.when(p.has_up)(lambda: greet(p.up))
+    pl.when(p.has_down)(lambda: greet(p.down))
+
+    get_t.wait()
+    work.first_back(((1, f(add_f.over_b, 0)),))
+    work.out_grads(((3, f(add_f.line, 1, 2)),))
+    pl.semaphore_wait(s.free, 3 + p.has_up.astype(jnp.int32) + p.has_down.astype(jnp.int32))
+    f(add_o.share, 0)()
+    work.make_bias()
+    work.attend_back(
+        0,
+        (
+            (0, f(add_f.over_b, 1)),
+            (1, f(add_f.collect, 3)),
+            (1, f(add_f.line, 3, 3)),
+            (2, f(add_f.over_a, 0)),
+            (3, f(add_o.over_b, 0)),
+        ),
+    )
+    work.qkv_grads(0)
+    add_q[0].share(0)
+    work.attend_back(
+        1,
+        (
+            (0, q(0, Reduce.over_b)),
+            (1, f(add_f.line, 2, 3)),
+            (1, f(add_f.collect, 0)),
+            (1, f(add_f.line, 3, 0)),
+            (2, f(add_f.over_a, 1)),
+            (3, q(0, Reduce.over_a)),
+            (3, f(add_o.over_a, 0)),
+        ),
+    )
+    work.qkv_grads(1)
+    add_q[1].share(0)
+    work.attend_back(
+        2,
+        (
+            (0, f(add_f.line, 1, 3)),
+            (0, f(add_f.line, 2, 0)),
+            (0, f(add_f.collect, 1)),
+            (0, f(add_f.line, 2, 1)),
+            (0, q(1, Reduce.over_b)),
+            (1, q(0, Reduce.collect)),
+            (1, f(add_o.collect, 0)),
+            (1, f(add_o.line, 3, 0)),
+            (1, q(0, Reduce.line, 3)),
+            (2, q(0, Reduce.line, 2)),
+            (3, f(add_o.line, 2, 0)),
+            (3, q(1, Reduce.over_a)),
+        ),
+    )
+    work.qkv_grads(2)
+    add_q[2].share(0)
+    for core in range(2):
+        s.terms_sum[core] = s.term_grads[:, pl.ds(D // 2 * core, D // 2)]
+    do(add_t.share)()
+    f(add_f.line, 1, 0)()
+    f(add_f.line, 1, 1)()
+    q(0, Reduce.line, 1)()
+    work.input_back(
+        (
+            (0, q(2, Reduce.over_b)),
+            (0, do(add_t.over_b)),
+            (0, f(add_o.line, 1, 0)),
+            (1, q(1, Reduce.collect)),
+            (1, q(1, Reduce.line, 3)),
+            (2, q(1, Reduce.line, 2)),
+            (2, do(add_t.over_a)),
+            (3, q(2, Reduce.over_a)),
+            (3, q(1, Reduce.line, 1)),
+        )
+    )
+    put_g = local(work.gin, gin_out, 4)
+    trail_f = Trail(p, sums, ffn, s.ffn_own, s.ffn_line, s.ffn_long, s.ffn_back_send, s.ffn_back_recv)
+    trail_a = Trail(p, sums, att, s.att_own, s.att_line, s.att_long, s.att_back_send, s.att_back_recv)
+    given_f = lambda core: handed(p, s.ffn_own, core, s.ffn_own_send, s.ffn_own_recv)
+    given_a = lambda core: handed(p, s.att_own, core, s.att_own_send, s.att_own_recv)
+    do(add_t.line, 3)()
+    add_f.keep()
+    sums.go(lambda: sums.start(None, lambda: given_f(p.c)))
+    q(2, Reduce.collect)()
+    q(2, Reduce.line, 3)()
+    do(add_t.line, 2)()
+    given_f(1 - p.c).wait_recv()
+    trail_f.lines()
+    q(2, Reduce.line, 2)()
+    do(add_t.line, 1)()
+    sums.go(trail_f.pass_back)
+    q(2, Reduce.line, 1)()
+    do(add_t.line, 0)()
+    do(add_t.hand_over)()
+    final = p.d == att.chips - 1
+
+    def terms_here():
+        add_t.take_over()
+        trail_f.last_rows(s.terms_all, 8, 7)
+        trail_a.last_rows(s.terms_all, 0, 5)
+
+    pl.when(final)(terms_here)
+    trail_f.out()
+    put_f = local(s.ffn_long.at[pl.ds(0, ffn.held), :], ffn_out, 1)
+    for who in (add_o, *add_q):
+        who.keep()
+    sums.go(lambda: sums.start(None, lambda: given_a(p.c)))
+    given_a(1 - p.c).wait_recv()
+    trail_a.lines()
+    sums.go(trail_a.pass_back)
+    trail_a.out()
+    put_a = local(s.att_long.at[pl.ds(0, att.held), :], att_out, 0)
+    sums.finish()
+    for who in (add_f, add_o, *add_q):
+        who.finish()
+    for copy in (put_g, put_f, put_a):
+        copy.wait()
+
+
+def run_layer(levels, att, ffn, att_lines, ffn_lines, tokens, cotangent, segments, live_count):
+    vmem = pl.BlockSpec(memory_space=pltpu.VMEM)
+    anywhere = pl.BlockSpec(memory_space=pl.ANY)
+    seqs, length = segments.shape
+    rows = tokens.shape[0]
+    bf16, f32 = jnp.bfloat16, jnp.float32
+    live = jnp.broadcast_to((jnp.arange(seqs) < live_count[0]).astype(f32)[:, None], (seqs, 128))
+    shape = jax.ShapeDtypeStruct
+    scratch = scratch_shapes(levels, att, ffn, rows, seqs, length)
+    return pl.pallas_call(
+        functools.partial(layer_kernel, tuple(scratch), levels, att, ffn, seqs, length),
+        out_shape=(
+            shape(tokens.shape, bf16),
+            shape(tokens.shape, bf16),
+            shape((att.held, 128), f32),
+            shape((ffn.held, 128), f32),
+        ),
+        in_specs=[anywhere, anywhere, anywhere, anywhere, vmem, vmem, vmem],
+        out_specs=(anywhere, anywhere, anywhere, anywhere),
+        scratch_shapes=list(scratch.values()),
+        compiler_params=pltpu.CompilerParams(
+            collective_id=1, has_side_effects=True, vmem_limit_bytes=64 * 2**20
+        ),
+        name="layer",
+    )(att_lines, ffn_lines, tokens, cotangent, segments, segments.T, live)
+
+
+def as_lines(flat, vector):
+    return jnp.pad(vector, (0, flat.held * 128 - flat.length)).reshape(flat.held, 128)
+
+
+def fast_body(
+    levels,
+    tokens,
+    cotangent,
+    segments,
+    live_count,
+    att_master,
+    att_first,
+    att_second,
+    ffn_master,
+    ffn_first,
+    ffn_second,
+):
+    chips = lax.axis_size("dp")
+    att = Flat(att_master.shape[0], chips, 3, 3 * chips // 4, False)
+    ffn = Flat(ffn_master.shape[0], chips, 4, chips // 2, True)
+    output, input_grad, att_sum, ffn_sum = run_layer(
+        levels,
+        att,
+        ffn,
+        as_lines(att, att_master),
+        as_lines(ffn, ffn_master),
+        tokens,
+        cotangent,
+        segments,
+        live_count,
+    )
+    att_grad = att_sum.reshape(-1)[: att.length]
+    ffn_grad = ffn_sum.reshape(-1)[: ffn.length]
+    att_new = adam_update(att_master, att_first, att_second, att_grad)
+    ffn_new = adam_update(ffn_master, ffn_first, ffn_second, ffn_grad)
+    return (output, input_grad, att_grad, *att_new, ffn_grad, *ffn_new)
+
+
+def body_for(mesh):
+    chips, cores = mesh.shape["dp"], mesh.shape["rep"]
+    if chips == 16 and cores == 2:
+        return functools.partial(fast_body, chips // 4)
+    return general_body
+
+
 def solution(mesh):
     placed = (
         P(("dp", "rep"), None),
@@ -339,7 +1662,7 @@
         P("dp"),
     )
     return jax.shard_map(
-        body,
+        body_for(mesh),
         mesh=mesh,
         in_specs=placed,
         out_specs=(

time: 1650 us -> 218 us (0.13)
  waiting for transfers between devices: 598 us -> 0 us
  other arithmetic: 435 us -> 5.82 us
  local copies, waits for them, and re-layouts: 358 us -> 8.56 us
  Pallas kernels: 0 us -> 201 us
  matrix products: 122 us -> 0 us
  starting transfers between devices: 99.4 us -> 0 us
    unnamed x3 -> x0, waiting for transfers between devices: 398 us -> none
    convert_element_type x11 -> x1, other arithmetic: 318 us -> 0.01 us  [run_layer(): (jnp.arange(seqs) < live_count[0]).astype(f32)[:, None]]
    unnamed x102 -> x17, local copies, waits for them, and re-layouts: 219 us -> 4.91 us
    pallas_call x0 -> x1, Pallas kernels: none -> 201 us  [run_layer(): pl.pallas_call(functools.partial(layer_kernel, tuple(scratch), levels, at...]
    all_to_all x2 -> x0, waiting for transfers between devices: 145 us -> none  [the longest x1 145 us: body(): lax.all_to_all(ffn_local.reshape(dp_count, -1).astype(jnp.bfloat16), 'dp'...]
    dot_general x21 -> x0, matrix products: 122 us -> none  [the longest x1 36.8 us: body(): jnp.dot(first_low, in_weight, preferred_element_type=jnp.float32) + in_bias]
    all_to_all x2 -> x0, starting transfers between devices: 99.3 us -> none  [the longest x1 92.2 us: body(): lax.all_to_all(att_local.reshape(dp_count, -1).astype(jnp.bfloat16), 'dp'...]
    reduce_sum x10 -> x0, other arithmetic: 76.8 us -> none  [the longest x1 51.4 us: body(): ffn_share = jnp.sum(ffn_rows, 0)]
  transfers between devices with their start and end apart: 4 -> 0, of which waited for: 3 -> 0; matrix products, arithmetic and copies ran while one was open for 22% -> 0% of each run, Pallas kernels for 0% -> 0%
where the time goes in v2:
time: 218 us; the launch traced here: 217 us
  Pallas kernels  201 us (92%)
  local copies, waits for them, and re-layouts  8.56 us (4%)
  other arithmetic  5.82 us (3%)
    pallas_call x1, Pallas kernels, run_layer(): pl.pallas_call(functools.partial(layer_kernel, tuple(scratch), levels, at...  201 us
    add x2, other arithmetic, adam_update(): return (first_new, second_new, update + decay * master)  5.81 us
    unnamed x17, local copies, waits for them, and re-layouts  4.91 us

profile of v2, /device:TPU:0, one launch (start us, length us, event | category | flops | bytes accessed | tf_op | source)
XLA Modules:
  0.0 217.2 jit_solution(7849679863532615472)
XLA Ops:
  0.6 0.0 copy-start
  1.4 0.6 broadcast_in_dim.2.live
  2.0 1.5 copy.20
  3.6 1.9 pad_bitcast_fusion.1.att_in
  5.5 0.0 copy-done
  5.5 1.1 pad_bitcast_fusion.ffn_in
  6.6 201.4 %layer.1 = (bf16[1024,768]{1,0:T(8,128)(2,1)}, bf16[1024,768]{1,0:T(8,128)(2,1)}, f32[1160,128]{1,0:T(8,128)}, f32[2312,128]{1,0:T(8,128)}) custom-call(f32[1160,128]{1,0:T(8,128)} %pad_bitcast_fusion.1.att_in, f32[2312,128]{1,0:T(8,128)} %pad_bitcast_fusion.ffn_in, bf16[1024,768]{1,0:T(8,128)(2,1)} %tok_in.1, bf16[1024,768]{1,0:T(8,128)(2,1)} %cot_in.1, ...), custom_call_target="tpu_custom_call" | custom-call | tf_op jit(solution)/shard_map/layer/pallas_call | solution.py:1588
  208.0 0.0 copy-start.1
  208.0 0.0 copy-start.4
  208.0 0.0 copy-start.5
  208.0 0.0 copy-start.6
  208.0 3.3 %multiply_add_fusion.2 = (f32[147696]{0:T(1024)}, f32[147696]{0:T(1024)}, f32[147696]{0:T(1024)}, f32[147696]{0:T(1024)}) fusion(f32[147696]{0:T(1024)} %param.14, f32[147696]{0:T(1024)} %param.16, f32[147696]{0:T(1024)} %param.15, f32[148480]{0:T(1024)} %bitcast.11), kind=kLoop, calls=%fused_computation.7 | loop fusion | flops 1920048 | bytes 4726272 | tf_op jit(solution)/shard_map/add | solution.py:128
  211.3 0.0 copy-done.1
  211.3 0.0 copy-done.4
  211.3 0.0 copy-done.5
  211.3 0.2 copy-done.6
  211.6 0.0 copy-start.3
  211.6 2.5 %multiply_add_fusion = (f32[295248]{0:T(1024)}, f32[295248]{0:T(1024)}, f32[295248]{0:T(1024)}, f32[295248]{0:T(1024)}) fusion(f32[295248]{0:T(1024)S(1)} %copy-done.1, f32[295248]{0:T(1024)S(1)} %copy-done.4, f32[295248]{0:T(1024)S(1)} %copy-done.5, f32[295936]{0:T(1024)S(1)} %bitcast.9), kind=kLoop, calls=%fused_computation.2 | loop fusion | flops 3838224 | bytes 9447936 | tf_op jit(solution)/shard_map/add | solution.py:128
  214.1 0.0 copy-done.3
  214.1 0.0 copy-start.2
  214.1 1.1 copy.24
  215.2 0.8 copy-done.2
  216.1 1.1 copy.25
  (1 shorter events, 0.0 us)
Async XLA Ops:
  0.6 4.9 %copy-start = (f32[295248]{0:T(1024)S(1)}, f32[295248]{0:T(1024)}, u32[]{:S(2)}) copy-start(f32[295248]{0:T(1024)} %param.17) | copy-start | bytes 3542980
  208.0 3.3 %copy-start.1 = (f32[295248]{0:T(1024)S(1)}, f32[295248]{0:T(1024)}, u32[]{:S(2)}) copy-start(f32[295248]{0:T(1024)} %param.17) | copy-start | bytes 3542980
  208.0 3.3 %copy-start.4 = (f32[295248]{0:T(1024)S(1)}, f32[295248]{0:T(1024)}, u32[]{:S(2)}) copy-start(f32[295248]{0:T(1024)} %param.19) | copy-start | bytes 3542980
  208.0 3.3 %copy-start.5 = (f32[295248]{0:T(1024)S(1)}, f32[295248]{0:T(1024)}, u32[]{:S(2)}) copy-start(f32[295248]{0:T(1024)} %param.18) | copy-start | bytes 3542980
  208.0 3.5 %copy-start.6 = (f32[2312,128]{1,0:T(8,128)S(1)}, f32[2312,128]{1,0:T(8,128)}, u32[]{:S(2)}) copy-start(f32[2312,128]{1,0:T(8,128)} %get-tuple-element.17) | copy-start | bytes 3551236
  211.6 2.5 %copy-start.3 = (bf16[1024,768]{1,0:T(8,128)(2,1)S(1)}, bf16[1024,768]{1,0:T(8,128)(2,1)}, u32[]{:S(2)}) copy-start(bf16[1024,768]{1,0:T(8,128)(2,1)} %get-tuple-element.36) | copy-start | bytes 4718596
  214.1 2.0 copy-start.2

commit v3 on v2

--- a/solution.py
+++ b/solution.py
@@ -371,10 +371,13 @@
     def at(self, column, level):
         return column + 4 * (level - self.z)
 
+    def turn(self, distance):
+        return self.at(self.d, (self.z + distance) % self.levels)
+
     def along(self, step):
         return (self.up, self.has_up) if step > 0 else (self.down, self.has_down)
 
-    def meet(self, chain):
+    def meet(self):
         barrier = pltpu.get_barrier_semaphore()
 
         def greet(device):
@@ -383,9 +386,10 @@
         for device in (self.across_a, self.across_b, self.sibling):
             greet(device)
         count = 3
-        edges = [(self.up, self.has_up), (self.down, self.has_down)]
-        if chain:
-            edges += [((self.d + 1, self.c), self.d < 4 * self.levels - 1), ((self.d - 1, self.c), self.d > 0)]
+        for distance in range(1, self.levels):
+            greet((self.turn(distance), self.c))
+            count += 1
+        edges = [((self.d + 1, self.c), self.d < 4 * self.levels - 1), ((self.d - 1, self.c), self.d > 0)]
         for device, there in edges:
             pl.when(there)(functools.partial(greet, device))
             count = count + there.astype(jnp.int32)
@@ -440,8 +444,8 @@
         self.send_sem, self.recv_sem, self.sib_sem = send_sem, recv_sem, sib_sem
         self.half = ref.shape[2] // 2
         levels = place.levels
-        self.leave_up = [k + 1 for k in range(levels)]
-        self.leave = (levels, 2 * levels, 4 * levels - 1)
+        self.leave = {2: levels, 3: 2 * levels, 4: 4 * levels - 1}
+        self.together = 1
 
     def rows(self, core):
         return pl.ds(pl.multiple_of(core * self.half, self.half), self.half)
@@ -507,20 +511,20 @@
 
     def finish(self):
         p = self.place
+        for way, count in self.leave.items():
+            self.left(None, way, count)
         for level in range(p.levels):
             if level < p.levels - 1:
-                self.left(p.z == level, 0, self.leave_up[level])
+                self.left(p.z == level, 0, self.together * (level + 1))
             if level > 0:
-                self.left(p.z == level, 1, self.leave_up[p.levels - 1 - level])
-        for way, count in zip((2, 3, 4), self.leave):
-            self.left(None, way, count)
+                self.left(p.z == level, 1, self.together * (p.levels - level))
 
 
 class Plane(Gather):
     def __init__(self, place, ref, parts, lanes, send_sem, recv_sem, sib_sem):
         super().__init__(place, ref, parts, lanes, send_sem, recv_sem, sib_sem)
-        self.leave_up = [4 * count for count in self.leave_up]
-        self.leave = (1, 2, 4 * place.levels - 1)
+        self.leave = {2: 1, 3: 2, 4: 4 * place.levels - 1}
+        self.together = 4
         self.from_a, self.from_b = place.levels, place.levels + 1
 
     def send(self, cond, chip, way, device):
@@ -562,19 +566,6 @@
             onward, more = p.along(-step)
             self.send_sheet(both(there, more), level, 0 if step < 0 else 1, onward)
             self.send_sheet(there, level, 4, p.sibling)
-
-
-def steps_of(go, plane):
-    levels = go.place.levels
-    todo = [functools.partial(go.line, 1), plane.near, functools.partial(go.over_a, 0), plane.complete]
-    for distance in range(2, levels):
-        todo.append(functools.partial(go.line, distance))
-        todo.append(functools.partial(go.over_a, distance - 1))
-        todo.append(functools.partial(plane.line, distance - 1))
-    todo.append(functools.partial(go.over_a, levels - 1))
-    todo.append(functools.partial(go.over_b, 0))
-    todo.append(functools.partial(plane.line, levels - 1))
-    return todo + [functools.partial(go.over_b, distance) for distance in range(1, levels)]
 
 
 class Spread:
@@ -681,23 +672,16 @@
 
 
 class Reduce:
-    def __init__(self, place, parts, chips, batches, view, slots, extra, kept, send_sem, recv_sem, whole=None):
+    def __init__(self, place, parts, chips, batches, view, slots, kept, send_sem, recv_sem, whole=None):
         self.place, self.parts, self.batches = place, parts, batches
-        self.view, self.slots, self.extra, self.kept = view, slots, extra, kept
+        self.view, self.slots, self.kept = view, slots, kept
         self.send_sem, self.recv_sem, self.whole = send_sem, recv_sem, whole
         self.levels = [level for batch in batches for level in batch]
         self.from_b, self.from_a = chips, chips + 2 * place.levels
         self.from_z = chips + 3 * place.levels
 
-    @staticmethod
-    def semaphores(batches):
-        return 4 * len(batches) + 2 * sum(map(len, batches))
-
     def arrival(self, kind, batch):
-        return self.recv_sem.at[4 * batch + kind]
-
-    def along(self, way, level):
-        return self.recv_sem.at[4 * len(self.batches) + 2 * self.levels.index(level) + way]
+        return self.recv_sem.at[batch, kind]
 
     def wait(self, part, sem):
         remote(part, part, self.send_sem.at[0], sem, self.place.sibling).wait_recv()
@@ -756,6 +740,49 @@
             for first in (0, self.from_b, self.from_a):
                 self.add(chip, self.slots(first + level if first else chip, 1))
 
+    def line(self, batch):
+        p = self.place
+        dst = self.slots(self.from_z + p.z, 1)
+        for level in self.batches[batch]:
+            chip = p.at(p.d, level)
+            self.send(p.z != level, chip, 0, dst, self.arrival(4, batch), (chip, p.c))
+
+    def keep(self):
+        p = self.place
+        own = self.kept(p.c)
+
+        def total(batch):
+            self.wait(self.slots(self.from_z, p.levels - 1), self.arrival(4, batch))
+            here = self.view(p.d, p.c)
+            others = [self.slots(self.from_z + (p.z + i) % p.levels, 1) for i in range(1, p.levels)]
+            for part in range(self.parts):
+                sum_now = here[part].astype(jnp.float32)
+                for other in others:
+                    sum_now = sum_now + other[part].astype(jnp.float32)
+                own[part] = sum_now
+
+        for batch, levels in enumerate(self.batches):
+            pl.when((p.z >= levels[0]) & (p.z <= levels[-1]))(functools.partial(total, batch))
+
+    def left(self, cond, way, count):
+        part = self.slots(0, count)
+        sem = self.send_sem.at[way]
+        when(cond, lambda: remote(part, part, sem, self.recv_sem.at[0, 0], self.place.sibling).wait_send())
+
+    def finish(self):
+        p = self.place
+        count = len(self.levels)
+        for way, pieces in ((4, 4 * count), (3, 2 * count), (2, count)):
+            self.left(None, way, pieces)
+        for z in range(p.levels):
+            self.left(p.z == z, 0, count - (z in self.levels))
+
+
+class Chain(Reduce):
+    def __init__(self, extra, line_sem, *rest):
+        super().__init__(*rest)
+        self.extra, self.line_sem = extra, line_sem
+
     def pass_on(self, here, level, way, waits, dst, device):
         p = self.place
         chip = p.at(p.d, level)
@@ -763,9 +790,9 @@
 
         def act():
             if waits:
-                self.wait(slot, self.along(way, level))
+                self.wait(slot, self.line_sem.at[way, level])
                 self.add(chip, slot)
-            self.send(None, chip, way, dst, self.along(way, level), device)
+            self.send(None, chip, way, dst, self.line_sem.at[way, level], device)
 
         pl.when(here)(act)
 
@@ -790,17 +817,12 @@
             sources = [(0, self.slots(self.from_z + level, 1))] if level > 0 else []
             sources += [(1, self.extra)] if level < p.levels - 1 else []
             for way, src in sources:
-                self.wait(src, self.along(way, level))
+                self.wait(src, self.line_sem.at[way, level])
                 for part in range(self.parts):
                     own[part] = own[part] + src[part].astype(jnp.float32)
 
         for level in self.levels:
             pl.when(p.z == level)(functools.partial(at, level))
-
-    def left(self, cond, way, count):
-        part = self.slots(0, count)
-        sem = self.send_sem.at[way]
-        when(cond, lambda: remote(part, part, sem, self.recv_sem.at[0], self.place.sibling).wait_send())
 
     def finish(self):
         p = self.place
@@ -849,14 +871,22 @@
         self.add(p.b_at == 1, 1)
         self.sends.start((p.b_at == 1) & (p.a_at == 0), lambda: self.copy(2, p.c, p.across_a))
 
-    def line(self, distance):
-        p = self.place
-        home = (p.b_at == 1) & (p.a_at == 1) & (p.z == p.levels - 1 - distance)
+    def line(self):
+        p = self.place
+        home = (p.b_at == 1) & (p.a_at == 1)
         self.add(home, 2)
-        if distance < p.levels - 1:
-            self.add(home, 3)
-        if distance > 0:
-            self.sends.start(home, lambda: self.copy(3, p.c, p.up))
+        here, top = self.ref.at[p.c], p.at(p.d, p.levels - 1)
+        self.sends.start(
+            home & p.has_up,
+            lambda: remote(here, self.got_ref.at[3 + p.z], self.send_sem.at[3], self.recv_sem.at[3], (top, p.c)),
+        )
+
+    def keep(self):
+        p = self.place
+        got = self.got_ref.at[pl.ds(3, p.levels - 1)]
+        remote(got, got, self.send_sem.at[3], self.recv_sem.at[3], p.sibling).wait_recv()
+        for level in range(p.levels - 1):
+            self.ref[p.c] = self.ref[p.c] + self.got_ref[3 + level]
 
     def final(self):
         return remote(
@@ -869,7 +899,10 @@
 
     def hand_over(self):
         p = self.place
-        self.sends.start(p.d == 4 * p.levels - 1, self.final)
+        last = p.d == 4 * p.levels - 1
+        if not self.sends.closing:
+            pl.when(last)(self.keep)
+        self.sends.start(last, self.final)
 
     def take_over(self):
         self.final().wait_recv()
@@ -963,7 +996,7 @@
     lax.fori_loop(0, count, body, 0)
 
 
-TILE = 256
+TILE, WIDE = 256, 512
 
 
 class Layer:
@@ -977,8 +1010,8 @@
         count = blocks.shape[0] // 4
         return blocks[pl.ds(count * part, count)].reshape(self.seqs * self.length, D)
 
-    def some(self, blocks, part, r):
-        count = TILE // blocks.shape[1]
+    def some(self, blocks, part, r, size=TILE):
+        count = size // blocks.shape[1]
         return pl.ds(blocks.shape[0] // 4 * part + count * r, count)
 
     def qkv_weight(self, part):
@@ -1012,8 +1045,10 @@
         loop(self.tiles, step, beside)
 
     def make_bias(self):
+        segs = self.segs[...].astype(jnp.float32)
+        columns = jnp.concatenate([segs, jnp.zeros((8 - self.seqs, self.length), jnp.float32)], 0).T
         for seq in range(self.seqs):
-            same = self.seg_col[:, seq : seq + 1] == self.seg_row[seq : seq + 1, :]
+            same = columns[:, seq : seq + 1] == segs[seq : seq + 1, :]
             self.bias[pl.ds(seq * self.length, self.length), :] = jnp.where(same, 0.0, masked)
 
     def lane_half(self, half):
@@ -1072,7 +1107,8 @@
                 second = second + dot(act, self.down_weight(part))
             out, normed, rstd = normalize(second, self.term(13), self.term(14))
             seq = r // (self.length // TILE)
-            grad_out = self.cot[rows, :].astype(jnp.float32) * self.live[pl.ds(seq, 1), 0:1]
+            live = jnp.clip(self.live_count[0] - seq, 0, 1).astype(jnp.float32)
+            grad_out = self.cot[rows, :].astype(jnp.float32) * live
             self.out[rows, :] = out.astype(jnp.bfloat16)
             scaled = grad_out * self.term(13)
             grad = rstd * (
@@ -1093,15 +1129,15 @@
 
     def hidden_back(self, part, beside=()):
         def step(r):
-            rows = tile(r, TILE)
+            rows = tile(r, WIDE)
             grad_act = dot_nt(self.down[rows, :], self.down_weight(part))
-            at = self.some(self.slope, part, r)
-            slope = self.slope[at].reshape(TILE, D).astype(jnp.float32)
+            at = self.some(self.slope, part, r, WIDE)
+            slope = self.slope[at].reshape(WIDE, D).astype(jnp.float32)
             inner = (grad_act * slope).astype(jnp.bfloat16)
             self.slope[at] = inner.reshape(-1, self.slope.shape[1], D)
             self.add_term(8 + part, inner.astype(jnp.float32))
 
-        loop(self.tiles, step, beside)
+        loop(self.seqs * self.length // WIDE, step, beside)
 
     def down_grads(self, part, beside=()):
         deep = self.ffn_w.shape[2]
@@ -1120,12 +1156,12 @@
 
     def in_back(self, part, beside=()):
         def step(r):
-            rows = tile(r, TILE)
+            rows = tile(r, WIDE)
             self.grad[rows, :] += dot_nt(
-                self.slope[self.some(self.slope, part, r)].reshape(TILE, D), self.in_weight(part)
+                self.slope[self.some(self.slope, part, r, WIDE)].reshape(WIDE, D), self.in_weight(part)
             )
 
-        loop(self.tiles, step, beside)
+        loop(self.seqs * self.length // WIDE, step, beside)
 
     def in_grads(self, part, beside=()):
         deep = self.ffn_w.shape[2]
@@ -1255,7 +1291,7 @@
         term_grads=vmem((16, D), f32),
         spare=vmem((48, 128), f32),
         terms_sum=vmem((2, 16, D // 2), f32),
-        terms_got=vmem((4, 16, D // 2), f32),
+        terms_got=vmem((2 + levels, 16, D // 2), f32),
         terms_all=vmem((2, 16, D // 2), f32),
         ffn_slots=vmem((chips + 4 * levels, ffn.parts, ffn.deep // 2, D), bf16),
         local_sem=dma((8,)),
@@ -1264,12 +1300,14 @@
         sum_send=dma((5,)),
         sum_recv=dma((5,)),
         free=pltpu.SemaphoreType.REGULAR,
+        ffn_extra=vmem((ffn.parts, ffn.deep // 2, D), bf16),
         f_send=dma((5,)),
-        f_recv=dma((Reduce.semaphores(f_batches),)),
+        f_line=dma((2, levels)),
+        f_recv=dma((len(f_batches), 5)),
         o_send=dma((5,)),
-        o_recv=dma((Reduce.semaphores(o_batches),)),
+        o_recv=dma((len(o_batches), 5)),
         q_send=dma((3, 5)),
-        q_recv=dma((3, Reduce.semaphores(q_batches))),
+        q_recv=dma((3, len(q_batches), 5)),
     )
     for name, flat in (("att_", att), ("ffn_", ffn)):
         half = (flat.parts, flat.deep // 2, D)
@@ -1278,7 +1316,6 @@
             halo=vmem((flat.tail + flat.halo + 8, 128), f32),
             line=vmem((flat.lines + flat.halo + 8, 128), f32),
             own=vmem((2, *half), f32),
-            extra=vmem(half, bf16),
             send=dma((5,)),
             recv=dma((chips,)),
             sib=dma,
@@ -1296,20 +1333,11 @@
     return shapes
 
 
-def spaced(acts, first, every=1):
-    return tuple((first + every * i, act) for i, act in enumerate(acts))
-
-
-def run(acts):
-    for act in acts:
-        act()
-
-
-def layer_kernel(names, levels, att, ffn, seqs, length, att_in, ffn_in, tok_in, cot_in, seg_row, seg_col, live,
+def layer_kernel(names, levels, att, ffn, seqs, length, att_in, ffn_in, tok_in, cot_in, segs, live_count,
                  out_out, gin_out, att_out, ffn_out, *scratch):
     s = types.SimpleNamespace(**dict(zip(names, scratch)))
     act_first = s.act.shape[0] // 4
-    refs = dict(vars(s), seg_row=seg_row, seg_col=seg_col, live=live)
+    refs = dict(vars(s), segs=segs, live_count=live_count)
     refs.update(cot=s.tok, out=s.tok, down=s.ctx, tok_t=s.low_t)
     refs.update(bias=s.hat.at[:, pl.ds(0, length)], gin=s.tok, act_first=act_first)
     work = Layer(refs, att.split, ffn.split, seqs, length)
@@ -1323,7 +1351,7 @@
     get_a = local(att_in, s.att_long.at[pl.ds(att.halo, att.held), :], 0)
     get_f = local(ffn_in, s.ffn_long.at[pl.ds(ffn.halo, ffn.held), :], 1)
     get_t = local(tok_in, s.tok, 2)
-    p.meet(True)
+    p.meet()
     sends = Sends()
     lead_a = Lead(p, sends, att, s.att_long, s.att_halo, s.att_line, s.att_halo_send, s.att_halo_recv)
     lead_f = Lead(p, sends, ffn, s.ffn_long, s.ffn_halo, s.ffn_line, s.ffn_halo_send, s.ffn_halo_recv)
@@ -1341,15 +1369,17 @@
             first = (pl.ds(0, parts), pl.ds(0, D - cut[1]))
             last = (pl.ds(0, parts), pl.ds(D - cut[1], cut[1]))
         go, plane = Gather(p, ref, *first, *sems[:3]), Plane(p, ref, *last, *sems[3:])
-        return [go.own, plane.own, *steps_of(go, plane)], (go, plane)
-
-    steps_a, go_a = gathers(
+        return go, plane
+
+    go_a = gathers(
         s.att_w, (0, 128), s.att_send, s.att_recv, s.att_sib, s.att_plane_send, s.att_plane_recv, s.att_plane_sib
     )
-    steps_f, go_f = gathers(
+    go_f = gathers(
         s.ffn_w, (1, 0), s.ffn_send, s.ffn_recv, s.ffn_sib, s.ffn_plane_send, s.ffn_plane_recv, s.ffn_plane_sib
     )
-    run(steps_a[:2])
+    (a, a_plane), (f, f_plane) = go_a, go_f
+    a.own()
+    a_plane.own()
 
     def last():
         terms, spare = s.terms, s.spare
@@ -1364,19 +1394,50 @@
     lead_f.lines()
     lead_f.store(s.ffn_w)
     s.term_grads[...] = jnp.zeros(s.term_grads.shape, jnp.float32)
-    run(steps_a[2:5])
-    run(steps_f[:2])
-    run(steps_a[5:])
+    a.over_a(0)
+    a_plane.near()
+    a.line(1)
+    a.line(2)
+    a_plane.complete()
+    a.over_a(1)
+    a_plane.line(1)
+    a.over_a(2)
+    f_plane.own()
+    a.line(3)
+    a_plane.line(2)
+    a.over_a(3)
+    a.over_b(0)
+    f.own()
+    f_plane.near()
+    a.over_b(1)
+    f.line(1)
+    a.over_b(2)
+    a.over_b(3)
+    a_plane.line(3)
     sends.go(Spread(p, sends, s.terms, s.term_send, s.term_recv).run)
     for go in go_a:
         go.from_sibling()
     get_t.wait()
 
-    rest = steps_f[2:]
-    work.qkv(spaced(rest[:4], 0))
-    work.attend(spaced(rest[4:16], 0))
-    work.first_norm(spaced(rest[16:20], 0))
-    run(rest[20:])
+    on = functools.partial
+    work.qkv(((3, on(f.line, 2)), (3, on(f.over_a, 0))))
+    work.attend(
+        (
+            (0, f_plane.complete),
+            (3, on(f.line, 3)),
+            (5, on(f_plane.line, 1)),
+            (7, on(f.over_a, 1)),
+            (8, on(f.over_a, 2)),
+            (9, on(f_plane.line, 2)),
+            (9, on(f.over_b, 0)),
+            (9, on(f.over_a, 3)),
+        )
+    )
+    work.first_norm()
+    f.over_b(1)
+    f.over_b(2)
+    f_plane.line(3)
+    f.over_b(3)
     get_c = local(cot_in, s.tok, 2)
     for go in go_f:
         go.from_sibling()
@@ -1400,12 +1461,12 @@
     f_batches, o_batches, q_batches = batches(levels)
     everything = pl.ds(0, D)
     ffn_slots = lambda i, count: slots.at[i] if count == 1 else slots.at[pl.ds(i, count)]
-    add_f = Reduce(
-        p, 4, ffn.chips, f_batches, of(s.ffn_w, half_f), ffn_slots, s.ffn_extra,
+    add_f = Chain(
+        s.ffn_extra, s.f_line, p, 4, ffn.chips, f_batches, of(s.ffn_w, half_f), ffn_slots,
         lambda core: s.ffn_own.at[core], s.f_send, s.f_recv,
     )
     add_o = Reduce(
-        p, 3, att.chips, o_batches, of(s.att_w, half_a), att_slots(everything), s.att_extra,
+        p, 3, att.chips, o_batches, of(s.att_w, half_a), att_slots(everything),
         lambda core: s.att_own.at[core], s.o_send, s.o_recv,
     )
     add_q = []
@@ -1416,7 +1477,7 @@
         whole = (act.at[blocks, tile(1 - p.c, half_a), lanes], slope.at[pl.ds(0, 3 * att.split), :, lanes])
         add_q.append(
             Reduce(
-                p, 3, att.chips, q_batches, view, att_slots(lanes), s.att_extra.at[:, :, lanes],
+                p, 3, att.chips, q_batches, view, att_slots(lanes),
                 lambda core, lanes=lanes: s.att_own.at[core, :, :, lanes], s.q_send.at[group], s.q_recv.at[group], whole,
             )
         )
@@ -1424,132 +1485,114 @@
 
     def do(act, *at):
         return sums.later(functools.partial(act, *at))
-
-    def q(group, act, *at):
-        return functools.partial(act, add_q[group], *at, 0)
-
-    def f(act, *at):
-        return functools.partial(act, *at)
 
     work.hidden_back(0)
     work.down_grads(0)
     work.hidden_back(1)
     work.down_grads(1)
-    f(add_f.share, 2)()
+    add_f.share(2)
     put_o.wait()
     get_t = local(tok_in, s.tok, 2)
     work.hidden_back(2)
-    work.down_grads(2, ((0, f(add_f.over_b, 2)),))
+    work.down_grads(2, ((0, on(add_f.over_b, 2)),))
     work.hidden_back(3)
     work.down_grads(3)
-    f(add_f.share, 3)()
-    work.in_back(0, ((3, f(add_f.over_b, 3)),))
+    add_f.share(3)
+    work.in_back(0, ((1, on(add_f.over_b, 3)),))
     work.in_grads(0)
-    work.in_back(1, ((2, f(add_f.over_a, 2)),))
+    work.in_back(1, ((1, on(add_f.over_a, 2)),))
     work.in_grads(1)
     work.in_back(2)
     work.in_grads(2)
-    work.in_back(3, ((2, f(add_f.collect, 2)), (2, f(add_f.line, 2, 2))))
-    work.in_grads(3, ((1, f(add_f.over_a, 3)),))
-    f(add_f.share, 0)()
-    f(add_f.share, 1)()
-
-    def greet(device):
+    work.in_back(3, ((1, on(add_f.collect, 2)), (1, on(add_f.line, 2, 2))))
+    work.in_grads(3, ((1, on(add_f.over_a, 3)),))
+    add_f.share(0)
+    add_f.share(1)
+
+    line = [(p.turn(distance), p.c) for distance in range(1, levels)]
+    for device in (p.sibling, p.across_a, p.across_b, *line):
         pl.semaphore_signal(s.free, inc=1, device_id=device, device_id_type=MESH_ID)
-
-    for device in (p.sibling, p.across_a, p.across_b):
-        greet(device)
-    pl.when(p.has_up)(lambda: greet(p.up))
-    pl.when(p.has_down)(lambda: greet(p.down))
-
     get_t.wait()
-    work.first_back(((1, f(add_f.over_b, 0)),))
-    work.out_grads(((3, f(add_f.line, 1, 2)),))
-    pl.semaphore_wait(s.free, 3 + p.has_up.astype(jnp.int32) + p.has_down.astype(jnp.int32))
-    f(add_o.share, 0)()
+    work.first_back(((1, on(add_f.over_b, 0)),))
+    work.out_grads(((3, on(add_f.line, 1, 2)),))
+    pl.semaphore_wait(s.free, 2 + levels)
+    add_o.share(0)
     work.make_bias()
     work.attend_back(
         0,
         (
-            (0, f(add_f.over_b, 1)),
-            (1, f(add_f.collect, 3)),
-            (1, f(add_f.line, 3, 3)),
-            (2, f(add_f.over_a, 0)),
-            (3, f(add_o.over_b, 0)),
+            (0, on(add_f.over_b, 1)),
+            (1, on(add_f.collect, 3)),
+            (1, on(add_f.line, 3, 3)),
+            (2, on(add_f.over_a, 0)),
+            (3, on(add_o.over_b, 0)),
         ),
     )
     work.qkv_grads(0)
-    add_q[0].share(0)
+    q = add_q
+    q[0].share(0)
     work.attend_back(
         1,
         (
-            (0, q(0, Reduce.over_b)),
-            (1, f(add_f.line, 2, 3)),
-            (1, f(add_f.collect, 0)),
-            (1, f(add_f.line, 3, 0)),
-            (2, f(add_f.over_a, 1)),
-            (3, q(0, Reduce.over_a)),
-            (3, f(add_o.over_a, 0)),
+            (0, on(q[0].over_b, 0)),
+            (1, on(add_f.line, 2, 3)),
+            (1, on(add_f.collect, 0)),
+            (1, on(add_f.line, 3, 0)),
+            (2, on(add_f.over_a, 1)),
+            (3, on(q[0].over_a, 0)),
+            (3, on(add_o.over_a, 0)),
         ),
     )
     work.qkv_grads(1)
-    add_q[1].share(0)
+    q[1].share(0)
     work.attend_back(
         2,
         (
-            (0, f(add_f.line, 1, 3)),
-            (0, f(add_f.line, 2, 0)),
-            (0, f(add_f.collect, 1)),
-            (0, f(add_f.line, 2, 1)),
-            (0, q(1, Reduce.over_b)),
-            (1, q(0, Reduce.collect)),
-            (1, f(add_o.collect, 0)),
-            (1, f(add_o.line, 3, 0)),
-            (1, q(0, Reduce.line, 3)),
-            (2, q(0, Reduce.line, 2)),
-            (3, f(add_o.line, 2, 0)),
-            (3, q(1, Reduce.over_a)),
+            (0, on(add_f.line, 1, 3)),
+            (0, on(add_f.line, 2, 0)),
+            (0, on(add_f.collect, 1)),
+            (0, on(add_f.line, 2, 1)),
+            (0, on(q[1].over_b, 0)),
+            (1, on(q[0].collect, 0)),
+            (1, on(q[0].line, 0)),
+            (1, on(add_o.collect, 0)),
+            (1, on(add_o.line, 0)),
+            (3, on(q[1].over_a, 0)),
         ),
     )
     work.qkv_grads(2)
-    add_q[2].share(0)
+    q[2].share(0)
     for core in range(2):
         s.terms_sum[core] = s.term_grads[:, pl.ds(D // 2 * core, D // 2)]
     do(add_t.share)()
-    f(add_f.line, 1, 0)()
-    f(add_f.line, 1, 1)()
-    q(0, Reduce.line, 1)()
-    work.input_back(
-        (
-            (0, q(2, Reduce.over_b)),
-            (0, do(add_t.over_b)),
-            (0, f(add_o.line, 1, 0)),
-            (1, q(1, Reduce.collect)),
-            (1, q(1, Reduce.line, 3)),
-            (2, q(1, Reduce.line, 2)),
-            (2, do(add_t.over_a)),
-            (3, q(2, Reduce.over_a)),
-            (3, q(1, Reduce.line, 1)),
-        )
-    )
-    put_g = local(work.gin, gin_out, 4)
     trail_f = Trail(p, sums, ffn, s.ffn_own, s.ffn_line, s.ffn_long, s.ffn_back_send, s.ffn_back_recv)
     trail_a = Trail(p, sums, att, s.att_own, s.att_line, s.att_long, s.att_back_send, s.att_back_recv)
     given_f = lambda core: handed(p, s.ffn_own, core, s.ffn_own_send, s.ffn_own_recv)
     given_a = lambda core: handed(p, s.att_own, core, s.att_own_send, s.att_own_recv)
-    do(add_t.line, 3)()
+    add_f.line(1, 0)
+    add_f.line(1, 1)
+    work.input_back(
+        (
+            (0, on(q[2].over_b, 0)),
+            (0, do(add_t.over_b)),
+            (1, on(q[1].collect, 0)),
+            (1, on(q[1].line, 0)),
+            (2, do(add_t.over_a)),
+            (3, on(q[2].over_a, 0)),
+            (3, do(add_t.line)),
+        )
+    )
+    put_g = local(work.gin, gin_out, 4)
     add_f.keep()
     sums.go(lambda: sums.start(None, lambda: given_f(p.c)))
-    q(2, Reduce.collect)()
-    q(2, Reduce.line, 3)()
-    do(add_t.line, 2)()
+    add_o.keep()
+    q[0].keep()
+    q[2].collect(0)
+    q[2].line(0)
     given_f(1 - p.c).wait_recv()
     trail_f.lines()
-    q(2, Reduce.line, 2)()
-    do(add_t.line, 1)()
     sums.go(trail_f.pass_back)
-    q(2, Reduce.line, 1)()
-    do(add_t.line, 0)()
+    q[1].keep()
     do(add_t.hand_over)()
     final = p.d == att.chips - 1
 
@@ -1561,8 +1604,7 @@
     pl.when(final)(terms_here)
     trail_f.out()
     put_f = local(s.ffn_long.at[pl.ds(0, ffn.held), :], ffn_out, 1)
-    for who in (add_o, *add_q):
-        who.keep()
+    q[2].keep()
     sums.go(lambda: sums.start(None, lambda: given_a(p.c)))
     given_a(1 - p.c).wait_recv()
     trail_a.lines()
@@ -1570,7 +1612,7 @@
     trail_a.out()
     put_a = local(s.att_long.at[pl.ds(0, att.held), :], att_out, 0)
     sums.finish()
-    for who in (add_f, add_o, *add_q):
+    for who in (add_f, add_o, *q):
         who.finish()
     for copy in (put_g, put_f, put_a):
         copy.wait()
@@ -1582,7 +1624,6 @@
     seqs, length = segments.shape
     rows = tokens.shape[0]
     bf16, f32 = jnp.bfloat16, jnp.float32
-    live = jnp.broadcast_to((jnp.arange(seqs) < live_count[0]).astype(f32)[:, None], (seqs, 128))
     shape = jax.ShapeDtypeStruct
     scratch = scratch_shapes(levels, att, ffn, rows, seqs, length)
     return pl.pallas_call(
@@ -1593,14 +1634,14 @@
             shape((att.held, 128), f32),
             shape((ffn.held, 128), f32),
         ),
-        in_specs=[anywhere, anywhere, anywhere, anywhere, vmem, vmem, vmem],
+        in_specs=[anywhere, anywhere, anywhere, anywhere, vmem, pl.BlockSpec(memory_space=pltpu.SMEM)],
         out_specs=(anywhere, anywhere, anywhere, anywhere),
         scratch_shapes=list(scratch.values()),
         compiler_params=pltpu.CompilerParams(
             collective_id=1, has_side_effects=True, vmem_limit_bytes=64 * 2**20
         ),
         name="layer",
-    )(att_lines, ffn_lines, tokens, cotangent, segments, segments.T, live)
+    )(att_lines, ffn_lines, tokens, cotangent, segments, live_count)
 
 
 def as_lines(flat, vector):

time: 218 us -> 206 us (0.945)
  Pallas kernels: 201 us -> 192 us
    pallas_call x1, Pallas kernels: 201 us -> 192 us  [run_layer(): pl.pallas_call(functools.partial(layer_kernel, tuple(scratch), levels, at...]
    unnamed x17 -> x16, local copies, waits for them, and re-layouts: 4.91 us -> 3.38 us
where the time goes in v3:
time: 206 us; the launch traced here: 205 us
  Pallas kernels  192 us (93%)
  local copies, waits for them, and re-layouts  6.39 us (3%)
  other arithmetic  5.81 us (3%)
    pallas_call x1, Pallas kernels, run_layer(): pl.pallas_call(functools.partial(layer_kernel, tuple(scratch), levels, at...  192 us
    add x2, other arithmetic, adam_update(): return (first_new, second_new, update + decay * master)  5.81 us

profile of v3, /device:TPU:0, one launch (start us, length us, event | category | flops | bytes accessed | tf_op | source)
XLA Modules:
  0.0 205.5 jit_solution(6588423027841159307)
XLA Ops:
  0.6 0.0 copy-start
  1.4 1.9 pad_bitcast_fusion.1.att_in
  3.3 0.0 copy-done
  3.3 1.1 pad_bitcast_fusion.ffn_in
  4.4 191.8 %layer.1 = (bf16[1024,768]{1,0:T(8,128)(2,1)}, bf16[1024,768]{1,0:T(8,128)(2,1)}, f32[1160,128]{1,0:T(8,128)}, f32[2312,128]{1,0:T(8,128)}) custom-call(f32[1160,128]{1,0:T(8,128)} %pad_bitcast_fusion.1.att_in, f32[2312,128]{1,0:T(8,128)} %pad_bitcast_fusion.ffn_in, bf16[1024,768]{1,0:T(8,128)(2,1)} %tok_in.1, bf16[1024,768]{1,0:T(8,128)(2,1)} %cot_in.1, ...), custom_call_target="tpu_custom_call" | custom-call | tf_op jit(solution)/shard_map/layer/pallas_call | solution.py:1629
  196.2 0.0 copy-start.1
  196.3 0.0 copy-start.4
  196.3 0.0 copy-start.5
  196.3 0.0 copy-start.6
  196.3 3.3 %multiply_add_fusion.2 = (f32[147696]{0:T(1024)}, f32[147696]{0:T(1024)}, f32[147696]{0:T(1024)}, f32[147696]{0:T(1024)}) fusion(f32[147696]{0:T(1024)} %param.14, f32[147696]{0:T(1024)} %param.16, f32[147696]{0:T(1024)} %param.15, f32[148480]{0:T(1024)} %bitcast.7), kind=kLoop, calls=%fused_computation.7 | loop fusion | flops 1920048 | bytes 4726272 | tf_op jit(solution)/shard_map/add | solution.py:128
  199.6 0.0 copy-done.1
  199.6 0.0 copy-done.4
  199.6 0.0 copy-done.5
  199.6 0.2 copy-done.6
  199.8 0.0 copy-start.3
  199.8 2.5 %multiply_add_fusion = (f32[295248]{0:T(1024)}, f32[295248]{0:T(1024)}, f32[295248]{0:T(1024)}, f32[295248]{0:T(1024)}) fusion(f32[295248]{0:T(1024)S(1)} %copy-done.1, f32[295248]{0:T(1024)S(1)} %copy-done.4, f32[295248]{0:T(1024)S(1)} %copy-done.5, f32[295936]{0:T(1024)S(1)} %bitcast.6), kind=kLoop, calls=%fused_computation.2 | loop fusion | flops 3838224 | bytes 9447936 | tf_op jit(solution)/shard_map/add | solution.py:128
  202.3 0.0 copy-done.3
  202.3 0.0 copy-start.2
  202.3 1.1 copy.23
  203.5 0.8 copy-done.2
  204.3 1.1 copy.24
Async XLA Ops:
  0.6 2.7 %copy-start = (f32[295248]{0:T(1024)S(1)}, f32[295248]{0:T(1024)}, u32[]{:S(2)}) copy-start(f32[295248]{0:T(1024)} %param.17) | copy-start | bytes 3542980
  196.2 3.3 %copy-start.1 = (f32[295248]{0:T(1024)S(1)}, f32[295248]{0:T(1024)}, u32[]{:S(2)}) copy-start(f32[295248]{0:T(1024)} %param.17) | copy-start | bytes 3542980
  196.3 3.3 %copy-start.4 = (f32[295248]{0:T(1024)S(1)}, f32[295248]{0:T(1024)}, u32[]{:S(2)}) copy-start(f32[295248]{0:T(1024)} %param.19) | copy-start | bytes 3542980
  196.3 3.3 %copy-start.5 = (f32[295248]{0:T(1024)S(1)}, f32[295248]{0:T(1024)}, u32[]{:S(2)}) copy-start(f32[295248]{0:T(1024)} %param.18) | copy-start | bytes 3542980
  196.3 3.5 %copy-start.6 = (f32[2312,128]{1,0:T(8,128)S(1)}, f32[2312,128]{1,0:T(8,128)}, u32[]{:S(2)}) copy-start(f32[2312,128]{1,0:T(8,128)} %get-tuple-element.17) | copy-start | bytes 3551236
  199.8 2.5 %copy-start.3 = (bf16[1024,768]{1,0:T(8,128)(2,1)S(1)}, bf16[1024,768]{1,0:T(8,128)(2,1)}, u32[]{:S(2)}) copy-start(bf16[1024,768]{1,0:T(8,128)(2,1)} %get-tuple-element.36) | copy-start | bytes 4718596
  202.3 2.0 copy-start.2

commit v4 on v3

--- a/solution.py
+++ b/solution.py
@@ -1142,17 +1142,20 @@
     def down_grads(self, part, beside=()):
         deep = self.ffn_w.shape[2]
         first = self.ffn_split + 2 * part
-
-        def step(m):
-            grads = dot(self.down_t[tile(m, 2 * deep), :], self.whole(self.act, part)).astype(jnp.bfloat16)
-            for owner in range(2):
-                for block in range(6):
-                    at = 128 * (3 * owner + block % 3)
-                    self.ffn_w[first + owner, m, :, pl.ds(128 * block, 128)] = grads[
-                        deep * (block // 3) : deep * (block // 3 + 1), at : at + 128
+        count = self.act.shape[0] // 4
+
+        def step(n):
+            acts = self.act[pl.ds(count * part, count), :, tile(n, 256)].reshape(self.seqs * self.length, 256)
+            grads = dot(self.down_t[...], acts).astype(jnp.bfloat16)
+            for k in range(2):
+                block = 2 * n + k
+                for i in range(D // deep):
+                    lanes = tile(3 * (i % 2) + block % 3, 128)
+                    self.ffn_w[first + block // 3, i // 2, :, lanes] = grads[
+                        deep * i : deep * (i + 1), 128 * k : 128 * (k + 1)
                     ]
 
-        loop(4, step, beside)
+        loop(3, step, beside)
 
     def in_back(self, part, beside=()):
         def step(r):
@@ -1165,12 +1168,15 @@
 
     def in_grads(self, part, beside=()):
         deep = self.ffn_w.shape[2]
-
-        def step(m):
-            grads = dot(self.low_t[tile(m, 2 * deep), :], self.whole(self.slope, part)).astype(jnp.bfloat16)
-            self.ffn_w[pl.ds(2 * m, 2), part] = grads.reshape(2, deep, D)
-
-        loop(4, step, beside)
+        count = self.slope.shape[0] // 4
+
+        def step(n):
+            lanes = tile(n, 256)
+            inner = self.slope[pl.ds(count * part, count), :, lanes].reshape(self.seqs * self.length, 256)
+            grads = dot(self.low_t[...], inner).astype(jnp.bfloat16)
+            self.ffn_w[pl.ds(0, self.ffn_split), part, :, lanes] = grads.reshape(self.ffn_split, deep, 256)
+
+        loop(3, step, beside)
 
     def first_back(self, beside=()):
         def step(r):
@@ -1196,11 +1202,17 @@
         loop(self.tiles, step, beside)
 
     def out_grads(self, beside=()):
-        def step(m):
-            grads = dot(self.ctx_t[tile(m, 192), :], self.whole(self.act, 3)).astype(jnp.bfloat16)
-            self.att_w[self.att_split + m] = grads.reshape(self.att_w.shape[1:])
-
-        loop(4, step, beside)
+        count = self.act.shape[0] // 4
+
+        def step(n):
+            lanes = tile(n, 256)
+            proj = self.act[pl.ds(3 * count, count), :, lanes].reshape(self.seqs * self.length, 256)
+            grads = dot(self.ctx_t[...], proj).astype(jnp.bfloat16)
+            owners = self.att_w.shape[0] - self.att_split
+            shape = (owners, *self.att_w.shape[1:3], 256)
+            self.att_w[pl.ds(self.att_split, owners), :, :, lanes] = grads.reshape(shape)
+
+        loop(3, step, beside)
 
     def attend_back(self, group, beside=()):
         def step(i):
@@ -1263,7 +1275,8 @@
 
 
 def batches(levels):
-    return [(level,) for level in range(levels)], [(levels - 1,)], [tuple(range(levels - 1))]
+    half = levels // 2
+    return [(level,) for level in range(half, levels)], [tuple(range(half))], [(levels - 1,)], [tuple(range(levels - 1))]
 
 
 def scratch_shapes(levels, att, ffn, rows, seqs, length):
@@ -1271,7 +1284,7 @@
     vmem, dma = pltpu.VMEM, pltpu.SemaphoreType.DMA
     chips = att.chips
     turned = vmem((D, rows), bf16)
-    f_batches, o_batches, q_batches = batches(levels)
+    f_batches, i_batches, o_batches, q_batches = batches(levels)
     shapes = dict(
         att_w=vmem((chips, att.parts, att.deep, D), bf16),
         ffn_w=vmem((chips, ffn.parts, ffn.deep, D), bf16),
@@ -1303,6 +1316,9 @@
         ffn_extra=vmem((ffn.parts, ffn.deep // 2, D), bf16),
         f_send=dma((5,)),
         f_line=dma((2, levels)),
+        i_send=dma((2, 5)),
+        i_recv=dma((2, len(i_batches), 5)),
+        i_line=dma((2, 2, levels)),
         f_recv=dma((len(f_batches), 5)),
         o_send=dma((5,)),
         o_recv=dma((len(o_batches), 5)),
@@ -1333,7 +1349,7 @@
     return shapes
 
 
-def layer_kernel(names, levels, att, ffn, seqs, length, att_in, ffn_in, tok_in, cot_in, segs, live_count,
+def layer_kernel(names, levels, att, ffn, seqs, length, masters_in, tok_in, cot_in, segs, live_count,
                  out_out, gin_out, att_out, ffn_out, *scratch):
     s = types.SimpleNamespace(**dict(zip(names, scratch)))
     act_first = s.act.shape[0] // 4
@@ -1348,8 +1364,8 @@
         return copy
 
     p = Place(levels)
-    get_a = local(att_in, s.att_long.at[pl.ds(att.halo, att.held), :], 0)
-    get_f = local(ffn_in, s.ffn_long.at[pl.ds(ffn.halo, ffn.held), :], 1)
+    get_a = local(masters_in.at[pl.ds(0, att.held), :], s.att_long.at[pl.ds(att.halo, att.held), :], 0)
+    get_f = local(masters_in.at[pl.ds(att.held, ffn.held), :], s.ffn_long.at[pl.ds(ffn.halo, ffn.held), :], 1)
     get_t = local(tok_in, s.tok, 2)
     p.meet()
     sends = Sends()
@@ -1394,24 +1410,24 @@
     lead_f.lines()
     lead_f.store(s.ffn_w)
     s.term_grads[...] = jnp.zeros(s.term_grads.shape, jnp.float32)
+    a.line(1)
     a.over_a(0)
     a_plane.near()
-    a.line(1)
     a.line(2)
+    a.over_b(0)
     a_plane.complete()
     a.over_a(1)
+    a.line(3)
+    f_plane.own()
+    a.over_a(2)
+    f.own()
     a_plane.line(1)
-    a.over_a(2)
-    f_plane.own()
-    a.line(3)
+    a.over_b(1)
+    a.over_b(2)
+    a.over_a(3)
+    f_plane.near()
     a_plane.line(2)
-    a.over_a(3)
-    a.over_b(0)
-    f.own()
-    f_plane.near()
-    a.over_b(1)
     f.line(1)
-    a.over_b(2)
     a.over_b(3)
     a_plane.line(3)
     sends.go(Spread(p, sends, s.terms, s.term_send, s.term_recv).run)
@@ -1420,24 +1436,24 @@
     get_t.wait()
 
     on = functools.partial
-    work.qkv(((3, on(f.line, 2)), (3, on(f.over_a, 0))))
+    work.qkv(((2, on(f.over_a, 0)), (2, on(f.line, 2)), (2, f_plane.complete),))
     work.attend(
         (
-            (0, f_plane.complete),
+            (3, on(f.over_a, 1)),
             (3, on(f.line, 3)),
-            (5, on(f_plane.line, 1)),
-            (7, on(f.over_a, 1)),
+            (6, on(f_plane.line, 1)),
             (8, on(f.over_a, 2)),
-            (9, on(f_plane.line, 2)),
             (9, on(f.over_b, 0)),
-            (9, on(f.over_a, 3)),
+            (10, on(f_plane.line, 2)),
+            (10, on(f.over_b, 1)),
+            (10, on(f.over_a, 3)),
         )
     )
     work.first_norm()
-    f.over_b(1)
     f.over_b(2)
     f_plane.line(3)
     f.over_b(3)
+
     get_c = local(cot_in, s.tok, 2)
     for go in go_f:
         go.from_sibling()
@@ -1458,13 +1474,26 @@
     def att_slots(lanes):
         return lambda i, count: slope.at[pl.ds(3 * i, 3 * count), :, lanes]
 
-    f_batches, o_batches, q_batches = batches(levels)
+    f_batches, i_batches, o_batches, q_batches = batches(levels)
     everything = pl.ds(0, D)
     ffn_slots = lambda i, count: slots.at[i] if count == 1 else slots.at[pl.ds(i, count)]
     add_f = Chain(
         s.ffn_extra, s.f_line, p, 4, ffn.chips, f_batches, of(s.ffn_w, half_f), ffn_slots,
         lambda core: s.ffn_own.at[core], s.f_send, s.f_recv,
     )
+    add_i = []
+    for group in range(2):
+        parts = pl.ds(2 * group, 2)
+        own_chips = pl.ds(0, ffn.split)
+        whole = (s.ffn_w.at[own_chips, parts, tile(1 - p.c, half_f), :], slots.at[own_chips, parts])
+        add_i.append(
+            Chain(
+                s.ffn_extra.at[parts], s.i_line.at[group], p, 2, ffn.chips, i_batches,
+                lambda chip, core, parts=parts: s.ffn_w.at[chip, parts, tile(core, half_f), :],
+                lambda i, count, parts=parts: slots.at[i, parts] if count == 1 else slots.at[pl.ds(i, count), parts],
+                lambda core, parts=parts: s.ffn_own.at[core, parts], s.i_send.at[group], s.i_recv.at[group], whole,
+            )
+        )
     add_o = Reduce(
         p, 3, att.chips, o_batches, of(s.att_w, half_a), att_slots(everything),
         lambda core: s.att_own.at[core], s.o_send, s.o_recv,
@@ -1490,41 +1519,41 @@
     work.down_grads(0)
     work.hidden_back(1)
     work.down_grads(1)
-    add_f.share(2)
+    add_f.share(0)
     put_o.wait()
     get_t = local(tok_in, s.tok, 2)
     work.hidden_back(2)
-    work.down_grads(2, ((0, on(add_f.over_b, 2)),))
+    work.down_grads(2, ((0, on(add_f.over_b, 0)),))
     work.hidden_back(3)
     work.down_grads(3)
-    add_f.share(3)
-    work.in_back(0, ((1, on(add_f.over_b, 3)),))
+    add_f.share(1)
+    work.in_back(0, ((1, on(add_f.over_b, 1)),))
     work.in_grads(0)
-    work.in_back(1, ((1, on(add_f.over_a, 2)),))
-    work.in_grads(1)
-    work.in_back(2)
+    work.in_back(1)
+    work.in_grads(1, ((0, on(add_f.over_a, 0)),))
+    add_i[0].share(0)
+    work.in_back(2, ((1, on(add_i[0].over_b, 0)),))
     work.in_grads(2)
-    work.in_back(3, ((1, on(add_f.collect, 2)), (1, on(add_f.line, 2, 2))))
-    work.in_grads(3, ((1, on(add_f.over_a, 3)),))
-    add_f.share(0)
-    add_f.share(1)
+    work.in_back(3)
+    work.in_grads(3, ((0, on(add_f.collect, 0)), (0, on(add_f.line, 2, 0)), (2, on(add_f.over_a, 1))))
+    add_i[1].share(0)
 
     line = [(p.turn(distance), p.c) for distance in range(1, levels)]
     for device in (p.sibling, p.across_a, p.across_b, *line):
         pl.semaphore_signal(s.free, inc=1, device_id=device, device_id_type=MESH_ID)
     get_t.wait()
-    work.first_back(((1, on(add_f.over_b, 0)),))
-    work.out_grads(((3, on(add_f.line, 1, 2)),))
+    work.first_back(((1, on(add_i[1].over_b, 0)),))
+    work.out_grads()
     pl.semaphore_wait(s.free, 2 + levels)
     add_o.share(0)
     work.make_bias()
     work.attend_back(
         0,
         (
-            (0, on(add_f.over_b, 1)),
-            (1, on(add_f.collect, 3)),
-            (1, on(add_f.line, 3, 3)),
-            (2, on(add_f.over_a, 0)),
+            (0, on(add_f.collect, 1)),
+            (0, on(add_f.line, 3, 1)),
+            (1, on(add_f.line, 1, 0)),
+            (1, on(add_i[0].over_a, 0)),
             (3, on(add_o.over_b, 0)),
         ),
     )
@@ -1535,10 +1564,11 @@
         1,
         (
             (0, on(q[0].over_b, 0)),
-            (1, on(add_f.line, 2, 3)),
-            (1, on(add_f.collect, 0)),
-            (1, on(add_f.line, 3, 0)),
-            (2, on(add_f.over_a, 1)),
+            (0, on(add_f.line, 2, 1)),
+            (0, on(add_i[0].collect, 0)),
+            (0, on(add_i[0].line, 3, 0)),
+            (2, on(add_i[1].over_a, 0)),
+            (3, on(add_i[0].line, 2, 0)),
             (3, on(q[0].over_a, 0)),
             (3, on(add_o.over_a, 0)),
         ),
@@ -1548,15 +1578,16 @@
     work.attend_back(
         2,
         (
-            (0, on(add_f.line, 1, 3)),
-            (0, on(add_f.line, 2, 0)),
-            (0, on(add_f.collect, 1)),
-            (0, on(add_f.line, 2, 1)),
+            (0, on(add_f.line, 1, 1)),
             (0, on(q[1].over_b, 0)),
+            (0, on(add_i[1].collect, 0)),
+            (0, on(add_i[1].line, 3, 0)),
             (1, on(q[0].collect, 0)),
             (1, on(q[0].line, 0)),
             (1, on(add_o.collect, 0)),
             (1, on(add_o.line, 0)),
+            (1, on(add_i[0].line, 1, 0)),
+            (3, on(add_i[1].line, 2, 0)),
             (3, on(q[1].over_a, 0)),
         ),
     )
@@ -1569,11 +1600,10 @@
     trail_a = Trail(p, sums, att, s.att_own, s.att_line, s.att_long, s.att_back_send, s.att_back_recv)
     given_f = lambda core: handed(p, s.ffn_own, core, s.ffn_own_send, s.ffn_own_recv)
     given_a = lambda core: handed(p, s.att_own, core, s.att_own_send, s.att_own_recv)
-    add_f.line(1, 0)
-    add_f.line(1, 1)
     work.input_back(
         (
             (0, on(q[2].over_b, 0)),
+            (0, on(add_i[1].line, 1, 0)),
             (0, do(add_t.over_b)),
             (1, on(q[1].collect, 0)),
             (1, on(q[1].line, 0)),
@@ -1583,7 +1613,8 @@
         )
     )
     put_g = local(work.gin, gin_out, 4)
-    add_f.keep()
+    for who in (add_f, *add_i):
+        who.keep()
     sums.go(lambda: sums.start(None, lambda: given_f(p.c)))
     add_o.keep()
     q[0].keep()
@@ -1612,13 +1643,13 @@
     trail_a.out()
     put_a = local(s.att_long.at[pl.ds(0, att.held), :], att_out, 0)
     sums.finish()
-    for who in (add_f, add_o, *q):
+    for who in (add_f, *add_i, add_o, *q):
         who.finish()
     for copy in (put_g, put_f, put_a):
         copy.wait()
 
 
-def run_layer(levels, att, ffn, att_lines, ffn_lines, tokens, cotangent, segments, live_count):
+def run_layer(levels, att, ffn, masters, tokens, cotangent, segments, live_count):
     vmem = pl.BlockSpec(memory_space=pltpu.VMEM)
     anywhere = pl.BlockSpec(memory_space=pl.ANY)
     seqs, length = segments.shape
@@ -1634,14 +1665,14 @@
             shape((att.held, 128), f32),
             shape((ffn.held, 128), f32),
         ),
-        in_specs=[anywhere, anywhere, anywhere, anywhere, vmem, pl.BlockSpec(memory_space=pltpu.SMEM)],
+        in_specs=[anywhere, anywhere, anywhere, vmem, pl.BlockSpec(memory_space=pltpu.SMEM)],
         out_specs=(anywhere, anywhere, anywhere, anywhere),
         scratch_shapes=list(scratch.values()),
         compiler_params=pltpu.CompilerParams(
             collective_id=1, has_side_effects=True, vmem_limit_bytes=64 * 2**20
         ),
         name="layer",
-    )(att_lines, ffn_lines, tokens, cotangent, segments, live_count)
+    )(masters, tokens, cotangent, segments, live_count)
 
 
 def as_lines(flat, vector):
@@ -1668,8 +1699,7 @@
         levels,
         att,
         ffn,
-        as_lines(att, att_master),
-        as_lines(ffn, ffn_master),
+        jnp.concatenate([as_lines(att, att_master), as_lines(ffn, ffn_master)]),
         tokens,
         cotangent,
         segments,

time: 206 us -> 200 us (0.971)
  Pallas kernels: 192 us -> 187 us
    pallas_call x1, Pallas kernels: 192 us -> 187 us  [run_layer(): pl.pallas_call(functools.partial(layer_kernel, tuple(scratch), levels, at...]
where the time goes in v4:
time: 200 us
  Pallas kernels  187 us (94%)
  other arithmetic  7.16 us (4%)
  local copies, waits for them, and re-layouts  4.56 us (2%)
    pallas_call x1, Pallas kernels, run_layer(): pl.pallas_call(functools.partial(layer_kernel, tuple(scratch), levels, at...  187 us
    add x2, other arithmetic, adam_update(): return (first_new, second_new, update + decay * master)  5.81 us

profile of v4, /device:TPU:0, one launch (start us, length us, event | category | flops | bytes accessed | tf_op | source)
XLA Modules:
  0.0 199.9 jit_solution(14642278160342580615)
XLA Ops:
  0.6 0.0 copy-start
  1.4 1.1 pad_bitcast_fusion.1
  2.5 0.0 copy-done
  2.5 0.1 pad_bitcast_fusion
  2.6 1.3 pad_maximum_fusion.masters_in
  3.9 186.7 %layer.1 = (bf16[1024,768]{1,0:T(8,128)(2,1)}, bf16[1024,768]{1,0:T(8,128)(2,1)}, f32[1160,128]{1,0:T(8,128)}, f32[2312,128]{1,0:T(8,128)}) custom-call(f32[3472,128]{1,0:T(8,128)} %pad_maximum_fusion.masters_in, bf16[1024,768]{1,0:T(8,128)(2,1)} %tok_in.1, bf16[1024,768]{1,0:T(8,128)(2,1)} %cot_in.1, s32[2,512]{1,0:T(2,128)} %segs.1, s32[1]{0:T(128)S(6)} %copy.22.live_count), custom_call_target="tpu_custom_call" | custom-call | tf_op jit(solution)/shard_map/layer/pallas_call | solution.py:1660
  190.7 0.0 copy-start.1
  190.7 0.0 copy-start.4
  190.7 0.0 copy-start.5
  190.7 0.0 copy-start.6
  190.7 3.3 %multiply_add_fusion.2 = (f32[147696]{0:T(1024)}, f32[147696]{0:T(1024)}, f32[147696]{0:T(1024)}, f32[147696]{0:T(1024)}) fusion(f32[147696]{0:T(1024)} %param.14, f32[147696]{0:T(1024)} %param.16, f32[147696]{0:T(1024)} %param.15, f32[148480]{0:T(1024)} %bitcast.7), kind=kLoop, calls=%fused_computation.8 | loop fusion | flops 1920048 | bytes 4726272 | tf_op jit(solution)/shard_map/add | solution.py:128
  194.0 0.0 copy-done.1
  194.0 0.0 copy-done.4
  194.0 0.0 copy-done.5
  194.0 0.2 copy-done.6
  194.2 0.0 copy-start.3
  194.2 2.5 %multiply_add_fusion = (f32[295248]{0:T(1024)}, f32[295248]{0:T(1024)}, f32[295248]{0:T(1024)}, f32[295248]{0:T(1024)}) fusion(f32[295248]{0:T(1024)S(1)} %copy-done.1, f32[295248]{0:T(1024)S(1)} %copy-done.4, f32[295248]{0:T(1024)S(1)} %copy-done.5, f32[295936]{0:T(1024)S(1)} %bitcast.6), kind=kLoop, calls=%fused_computation.3 | loop fusion | flops 3838224 | bytes 9447936 | tf_op jit(solution)/shard_map/add | solution.py:128
  196.8 0.0 copy-done.3
  196.8 0.0 copy-start.2
  196.8 1.1 copy.23
  197.9 0.8 copy-done.2
  198.8 1.1 copy.24
Async XLA Ops:
  0.6 1.9 copy-start
  190.7 3.3 %copy-start.1 = (f32[295248]{0:T(1024)S(1)}, f32[295248]{0:T(1024)}, u32[]{:S(2)}) copy-start(f32[295248]{0:T(1024)} %param.17) | copy-start | bytes 3542980
  190.7 3.3 %copy-start.4 = (f32[295248]{0:T(1024)S(1)}, f32[295248]{0:T(1024)}, u32[]{:S(2)}) copy-start(f32[295248]{0:T(1024)} %param.19) | copy-start | bytes 3542980
  190.7 3.3 %copy-start.5 = (f32[295248]{0:T(1024)S(1)}, f32[295248]{0:T(1024)}, u32[]{:S(2)}) copy-start(f32[295248]{0:T(1024)} %param.18) | copy-start | bytes 3542980
  190.7 3.5 %copy-start.6 = (f32[2312,128]{1,0:T(8,128)S(1)}, f32[2312,128]{1,0:T(8,128)}, u32[]{:S(2)}) copy-start(f32[2312,128]{1,0:T(8,128)} %get-tuple-element.17) | copy-start | bytes 3551236
  194.2 2.5 %copy-start.3 = (bf16[1024,768]{1,0:T(8,128)(2,1)S(1)}, bf16[1024,768]{1,0:T(8,128)(2,1)}, u32[]{:S(2)}) copy-start(bf16[1024,768]{1,0:T(8,128)(2,1)} %get-tuple-element.36) | copy-start | bytes 4718596
  196.8 2.0 copy-start.2

commit v5 on v4

--- a/solution.py
+++ b/solution.py
@@ -389,7 +389,9 @@
         for distance in range(1, self.levels):
             greet((self.turn(distance), self.c))
             count += 1
-        edges = [((self.d + 1, self.c), self.d < 4 * self.levels - 1), ((self.d - 1, self.c), self.d > 0)]
+        after, before = self.d < 4 * self.levels - 1, self.d > 0
+        edges = [((self.d + 1, self.c), after), ((self.d - 1, self.c), before)]
+        edges += [((self.d + 1, 0), after & (self.c == 1)), ((self.d - 1, 1), before & (self.c == 0))]
         for device, there in edges:
             pl.when(there)(functools.partial(greet, device))
             count = count + there.astype(jnp.int32)
@@ -910,34 +912,49 @@
 
 
 class Trail:
-    def __init__(self, place, sends, flat, own_ref, line_ref, out_ref, send_sem, recv_sem):
+    def __init__(self, place, sends, flat, own_ref, line_ref, out_ref, send_sem, recv_sem, more_sem=None):
         self.place, self.sends, self.flat = place, sends, flat
         self.own_ref, self.line_ref, self.out_ref = own_ref, line_ref, out_ref
-        self.send_sem, self.recv_sem = send_sem, recv_sem
-
-    def copy(self):
+        self.send_sem, self.recv_sem, self.more_sem = send_sem, recv_sem, more_sem
+
+    def copy(self, send_sem=None, device=None):
         f, p = self.flat, self.place
         return remote(
             self.line_ref.at[pl.ds(0, f.halo), :],
             self.line_ref.at[pl.ds(f.lines, f.halo), :],
-            self.send_sem,
+            self.send_sem if send_sem is None else send_sem,
             self.recv_sem,
-            (p.d - 1, p.c),
-        )
+            (p.d - 1, p.c) if device is None else device,
+        )
+
+    def put(self, split, core):
+        f = self.flat
+        half = f.deep // 2
+        for part in range(f.parts):
+            for block in range(D // 128):
+                first, stride = f.place_of(part, block, split)
+                first = first + stride * half * core
+                self.line_ref[pl.ds(first, half, stride=stride), :] = self.own_ref[
+                    core, part, :, pl.ds(128 * block, 128)
+                ]
+
+    def half_lines(self, core, cond):
+        p, f = self.place, self.flat
+        pl.when(cond & (p.d < f.split))(lambda: self.put(True, core))
+        pl.when(cond & (p.d >= f.split))(lambda: self.put(False, core))
+
+    def early_back(self):
+        p, f = self.place, self.flat
+        for core, send_sem in ((0, self.send_sem), (1, self.more_sem)):
+            make = lambda core=core, send_sem=send_sem: self.copy(send_sem, (p.d - 1, core))
+            self.sends.start((p.c == 0) & (p.d > 0), make)
 
     def lines(self):
         p, f = self.place, self.flat
-        half = f.deep // 2
 
         def put(split):
             for core in range(2):
-                for part in range(f.parts):
-                    for block in range(D // 128):
-                        first, stride = f.place_of(part, block, split)
-                        first = first + stride * half * core
-                        self.line_ref[pl.ds(first, half, stride=stride), :] = self.own_ref[
-                            core, part, :, pl.ds(128 * block, 128)
-                        ]
+                self.put(split, core)
 
         def put_turned():
             for j in range(f.rows // 128):
@@ -1312,6 +1329,7 @@
         term_recv=dma,
         sum_send=dma((5,)),
         sum_recv=dma((5,)),
+        more_send=dma,
         free=pltpu.SemaphoreType.REGULAR,
         ffn_extra=vmem((ffn.parts, ffn.deep // 2, D), bf16),
         f_send=dma((5,)),
@@ -1515,6 +1533,7 @@
     def do(act, *at):
         return sums.later(functools.partial(act, *at))
 
+    q = add_q
     work.hidden_back(0)
     work.down_grads(0)
     work.hidden_back(1)
@@ -1523,108 +1542,119 @@
     put_o.wait()
     get_t = local(tok_in, s.tok, 2)
     work.hidden_back(2)
-    work.down_grads(2, ((0, on(add_f.over_b, 0)),))
+    work.down_grads(2, (
+            (2, on(add_f.over_b, 0)),
+        ))
     work.hidden_back(3)
     work.down_grads(3)
     add_f.share(1)
-    work.in_back(0, ((1, on(add_f.over_b, 1)),))
-    work.in_grads(0)
+    work.in_back(0)
+    work.in_grads(0, (
+            (2, on(add_f.over_b, 1)),
+        ))
     work.in_back(1)
-    work.in_grads(1, ((0, on(add_f.over_a, 0)),))
+    work.in_grads(1)
     add_i[0].share(0)
-    work.in_back(2, ((1, on(add_i[0].over_b, 0)),))
-    work.in_grads(2)
-    work.in_back(3)
-    work.in_grads(3, ((0, on(add_f.collect, 0)), (0, on(add_f.line, 2, 0)), (2, on(add_f.over_a, 1))))
+    work.in_back(2)
+    work.in_grads(2, (
+            (1, on(add_f.over_a, 0)),
+        ))
+    work.in_back(3, (
+            (0, on(add_f.over_a, 1)),
+        ))
+    work.in_grads(3)
     add_i[1].share(0)
 
     line = [(p.turn(distance), p.c) for distance in range(1, levels)]
     for device in (p.sibling, p.across_a, p.across_b, *line):
         pl.semaphore_signal(s.free, inc=1, device_id=device, device_id_type=MESH_ID)
     get_t.wait()
-    work.first_back(((1, on(add_i[1].over_b, 0)),))
-    work.out_grads()
+    work.first_back((
+            (0, on(add_i[0].over_b, 0)),
+            (3, on(add_f.collect, 1)),
+        ))
+    work.out_grads((
+            (1, on(add_i[1].over_b, 0)),
+            (2, on(add_f.line, 3, 1)),
+        ))
     pl.semaphore_wait(s.free, 2 + levels)
     add_o.share(0)
     work.make_bias()
-    work.attend_back(
-        0,
-        (
-            (0, on(add_f.collect, 1)),
-            (0, on(add_f.line, 3, 1)),
-            (1, on(add_f.line, 1, 0)),
-            (1, on(add_i[0].over_a, 0)),
+    work.attend_back(0, (
+            (1, on(add_f.collect, 0)),
+            (2, on(add_f.line, 2, 0)),
+            (2, on(add_i[0].over_a, 0)),
+        ))
+    work.qkv_grads(0)
+    q[0].share(0)
+    work.attend_back(1, (
+            (0, on(add_f.line, 2, 1)),
+            (0, on(add_f.line, 1, 0)),
+            (0, on(add_i[1].over_a, 0)),
+            (2, on(q[0].over_b, 0)),
+            (3, on(add_i[0].collect, 0)),
             (3, on(add_o.over_b, 0)),
-        ),
-    )
-    work.qkv_grads(0)
-    q = add_q
-    q[0].share(0)
-    work.attend_back(
-        1,
-        (
-            (0, on(q[0].over_b, 0)),
-            (0, on(add_f.line, 2, 1)),
-            (0, on(add_i[0].collect, 0)),
-            (0, on(add_i[0].line, 3, 0)),
-            (2, on(add_i[1].over_a, 0)),
-            (3, on(add_i[0].line, 2, 0)),
-            (3, on(q[0].over_a, 0)),
-            (3, on(add_o.over_a, 0)),
-        ),
-    )
+            (3, on(add_i[0].line, 3, 0)),
+        ))
     work.qkv_grads(1)
     q[1].share(0)
-    work.attend_back(
-        2,
-        (
-            (0, on(add_f.line, 1, 1)),
-            (0, on(q[1].over_b, 0)),
-            (0, on(add_i[1].collect, 0)),
-            (0, on(add_i[1].line, 3, 0)),
-            (1, on(q[0].collect, 0)),
-            (1, on(q[0].line, 0)),
-            (1, on(add_o.collect, 0)),
-            (1, on(add_o.line, 0)),
+    q[1].over_b(0)
+    add_i[1].collect(0)
+    add_i[0].line(2, 0)
+    q[0].over_a(0)
+    work.attend_back(2, (
+            (1, on(add_o.over_a, 0)),
+            (1, on(add_i[1].line, 3, 0)),
             (1, on(add_i[0].line, 1, 0)),
-            (3, on(add_i[1].line, 2, 0)),
-            (3, on(q[1].over_a, 0)),
-        ),
-    )
+            (2, on(q[0].collect, 0)),
+            (2, on(q[0].line, 0)),
+            (3, on(add_f.line, 1, 1)),
+        ))
     work.qkv_grads(2)
     q[2].share(0)
     for core in range(2):
         s.terms_sum[core] = s.term_grads[:, pl.ds(D // 2 * core, D // 2)]
     do(add_t.share)()
     trail_f = Trail(p, sums, ffn, s.ffn_own, s.ffn_line, s.ffn_long, s.ffn_back_send, s.ffn_back_recv)
-    trail_a = Trail(p, sums, att, s.att_own, s.att_line, s.att_long, s.att_back_send, s.att_back_recv)
+    trail_a = Trail(p, sums, att, s.att_own, s.att_line, s.att_long, s.att_back_send, s.att_back_recv, s.more_send)
     given_f = lambda core: handed(p, s.ffn_own, core, s.ffn_own_send, s.ffn_own_recv)
     given_a = lambda core: handed(p, s.att_own, core, s.att_own_send, s.att_own_recv)
-    work.input_back(
-        (
+    add_o.collect(0)
+    add_i[1].line(2, 0)
+    add_o.line(0)
+    q[1].over_a(0)
+    work.input_back((
             (0, on(q[2].over_b, 0)),
             (0, on(add_i[1].line, 1, 0)),
+            (0, on(q[1].collect, 0)),
             (0, do(add_t.over_b)),
-            (1, on(q[1].collect, 0)),
-            (1, on(q[1].line, 0)),
+            (2, on(q[2].over_a, 0)),
+            (2, on(q[1].line, 0)),
             (2, do(add_t.over_a)),
-            (3, on(q[2].over_a, 0)),
+            (3, on(q[2].collect, 0)),
             (3, do(add_t.line)),
-        )
-    )
+        ))
     put_g = local(work.gin, gin_out, 4)
-    for who in (add_f, *add_i):
-        who.keep()
+    add_f.keep()
+    q[0].keep()
+    add_i[0].keep()
+    q[2].line(0)
+    add_i[1].keep()
     sums.go(lambda: sums.start(None, lambda: given_f(p.c)))
     add_o.keep()
-    q[0].keep()
-    q[2].collect(0)
-    q[2].line(0)
+    q[1].keep()
     given_f(1 - p.c).wait_recv()
     trail_f.lines()
     sums.go(trail_f.pass_back)
-    q[1].keep()
+    q[2].keep()
+    sums.go(lambda: sums.start(None, lambda: given_a(p.c)))
+    trail_a.half_lines(0, p.c == 0)
+    sums.go(trail_a.early_back)
+    trail_a.half_lines(1, p.c == 1)
     do(add_t.hand_over)()
+    given_a(1 - p.c).wait_recv()
+    trail_a.half_lines(1, p.c == 0)
+    trail_a.half_lines(0, p.c == 1)
     final = p.d == att.chips - 1
 
     def terms_here():
@@ -1635,11 +1665,6 @@
     pl.when(final)(terms_here)
     trail_f.out()
     put_f = local(s.ffn_long.at[pl.ds(0, ffn.held), :], ffn_out, 1)
-    q[2].keep()
-    sums.go(lambda: sums.start(None, lambda: given_a(p.c)))
-    given_a(1 - p.c).wait_recv()
-    trail_a.lines()
-    sums.go(trail_a.pass_back)
     trail_a.out()
     put_a = local(s.att_long.at[pl.ds(0, att.held), :], att_out, 0)
     sums.finish()

time: 200 us -> 197 us (0.985)
  Pallas kernels: 187 us -> 184 us
    pallas_call x1, Pallas kernels: 187 us -> 184 us  [run_layer(): pl.pallas_call(functools.partial(layer_kernel, tuple(scratch), levels, at...]
where the time goes in v5:
time: 197 us
  Pallas kernels  184 us (93%)
  other arithmetic  7.16 us (4%)
  local copies, waits for them, and re-layouts  4.56 us (2%)
    pallas_call x1, Pallas kernels, run_layer(): pl.pallas_call(functools.partial(layer_kernel, tuple(scratch), levels, at...  184 us
    add x2, other arithmetic, adam_update(): return (first_new, second_new, update + decay * master)  5.81 us

profile of v5, /device:TPU:0, one launch (start us, length us, event | category | flops | bytes accessed | tf_op | source)
XLA Modules:
  0.0 196.8 jit_solution(11500673080952836753)
XLA Ops:
  0.6 0.0 copy-start
  1.4 1.1 pad_bitcast_fusion.1
  2.5 0.0 copy-done
  2.5 0.1 pad_bitcast_fusion
  2.6 1.3 pad_maximum_fusion.masters_in
  3.9 183.6 %layer.1 = (bf16[1024,768]{1,0:T(8,128)(2,1)}, bf16[1024,768]{1,0:T(8,128)(2,1)}, f32[1160,128]{1,0:T(8,128)}, f32[2312,128]{1,0:T(8,128)}) custom-call(f32[3472,128]{1,0:T(8,128)} %pad_maximum_fusion.masters_in, bf16[1024,768]{1,0:T(8,128)(2,1)} %tok_in.1, bf16[1024,768]{1,0:T(8,128)(2,1)} %cot_in.1, s32[2,512]{1,0:T(2,128)} %segs.1, s32[1]{0:T(128)S(6)} %copy.22.live_count), custom_call_target="tpu_custom_call" | custom-call | tf_op jit(solution)/shard_map/layer/pallas_call | solution.py:1685
  187.6 0.0 copy-start.1
  187.6 0.0 copy-start.4
  187.6 0.0 copy-start.5
  187.6 0.0 copy-start.6
  187.6 3.3 %multiply_add_fusion.2 = (f32[147696]{0:T(1024)}, f32[147696]{0:T(1024)}, f32[147696]{0:T(1024)}, f32[147696]{0:T(1024)}) fusion(f32[147696]{0:T(1024)} %param.14, f32[147696]{0:T(1024)} %param.16, f32[147696]{0:T(1024)} %param.15, f32[148480]{0:T(1024)} %bitcast.7), kind=kLoop, calls=%fused_computation.8 | loop fusion | flops 1920048 | bytes 4726272 | tf_op jit(solution)/shard_map/add | solution.py:128
  190.9 0.0 copy-done.1
  190.9 0.0 copy-done.4
  190.9 0.0 copy-done.5
  190.9 0.2 copy-done.6
  191.1 0.0 copy-start.3
  191.1 2.5 %multiply_add_fusion = (f32[295248]{0:T(1024)}, f32[295248]{0:T(1024)}, f32[295248]{0:T(1024)}, f32[295248]{0:T(1024)}) fusion(f32[295248]{0:T(1024)S(1)} %copy-done.1, f32[295248]{0:T(1024)S(1)} %copy-done.4, f32[295248]{0:T(1024)S(1)} %copy-done.5, f32[295936]{0:T(1024)S(1)} %bitcast.6), kind=kLoop, calls=%fused_computation.3 | loop fusion | flops 3838224 | bytes 9447936 | tf_op jit(solution)/shard_map/add | solution.py:128
  193.7 0.0 copy-done.3
  193.7 0.0 copy-start.2
  193.7 1.1 copy.23
  194.8 0.8 copy-done.2
  195.7 1.1 copy.24
Async XLA Ops:
  0.6 1.9 copy-start
  187.6 3.3 %copy-start.1 = (f32[295248]{0:T(1024)S(1)}, f32[295248]{0:T(1024)}, u32[]{:S(2)}) copy-start(f32[295248]{0:T(1024)} %param.17) | copy-start | bytes 3542980
  187.6 3.3 %copy-start.4 = (f32[295248]{0:T(1024)S(1)}, f32[295248]{0:T(1024)}, u32[]{:S(2)}) copy-start(f32[295248]{0:T(1024)} %param.19) | copy-start | bytes 3542980
  187.6 3.3 %copy-start.5 = (f32[295248]{0:T(1024)S(1)}, f32[295248]{0:T(1024)}, u32[]{:S(2)}) copy-start(f32[295248]{0:T(1024)} %param.18) | copy-start | bytes 3542980
  187.6 3.5 %copy-start.6 = (f32[2312,128]{1,0:T(8,128)S(1)}, f32[2312,128]{1,0:T(8,128)}, u32[]{:S(2)}) copy-start(f32[2312,128]{1,0:T(8,128)} %get-tuple-element.17) | copy-start | bytes 3551236
  191.1 2.5 %copy-start.3 = (bf16[1024,768]{1,0:T(8,128)(2,1)S(1)}, bf16[1024,768]{1,0:T(8,128)(2,1)}, u32[]{:S(2)}) copy-start(bf16[1024,768]{1,0:T(8,128)(2,1)} %get-tuple-element.36) | copy-start | bytes 4718596
  193.7 2.0 %copy-start.2 = (bf16[1024,768]{1,0:T(8,128)(2,1)S(1)}, bf16[1024,768]{1,0:T(8,128)(2,1)}, u32[]{:S(2)}) copy-start(bf16[1024,768]{1,0:T(8,128)(2,1)} %get-tuple-element.37) | copy-start | bytes 4718596

commit v6 on v5

--- a/solution.py
+++ b/solution.py
@@ -643,6 +643,10 @@
         p, f = self.place, self.flat
         slip = f.slip * p.d
         self.line_ref[pl.ds(0, f.lines), :] = shifted(self.long_ref, f.halo * 128 - slip, f.lines)
+
+    def join(self):
+        p, f = self.place, self.flat
+        slip = f.slip * p.d
 
         def mend():
             self.copy().wait_recv()
@@ -1394,6 +1398,8 @@
     get_f.wait()
     sends.go(lead_f.begin)
     lead_a.lines()
+    lead_f.lines()
+    lead_a.join()
     lead_a.store(s.att_w)
     def gathers(ref, cut, *sems):
         parts, lanes = ref.shape[1], pl.ds(0, D)
@@ -1425,7 +1431,7 @@
                 terms[pl.ds(at, count), pl.ds(128 * block, 128)] = spare[pl.ds(block, count, stride=6), :]
 
     pl.when(p.d == att.chips - 1)(last)
-    lead_f.lines()
+    lead_f.join()
     lead_f.store(s.ffn_w)
     s.term_grads[...] = jnp.zeros(s.term_grads.shape, jnp.float32)
     a.line(1)

time: 197 us -> 197 us (level)
  no operation moved by 1% of the time
where the time goes in v6:
time: 197 us
  Pallas kernels  184 us (93%)
  other arithmetic  7.16 us (4%)
  local copies, waits for them, and re-layouts  4.56 us (2%)
    pallas_call x1, Pallas kernels, run_layer(): pl.pallas_call(functools.partial(layer_kernel, tuple(scratch), levels, at...  184 us
    add x2, other arithmetic, adam_update(): return (first_new, second_new, update + decay * master)  5.81 us

profile of v6, /device:TPU:0, one launch (start us, length us, event | category | flops | bytes accessed | tf_op | source)
XLA Modules:
  0.0 196.8 jit_solution(15583043934955150956)
XLA Ops:
  0.6 0.0 copy-start
  1.4 1.1 pad_bitcast_fusion.1
  2.5 0.0 copy-done
  2.5 0.1 pad_bitcast_fusion
  2.6 1.3 pad_maximum_fusion.masters_in
  3.9 183.6 %layer.1 = (bf16[1024,768]{1,0:T(8,128)(2,1)}, bf16[1024,768]{1,0:T(8,128)(2,1)}, f32[1160,128]{1,0:T(8,128)}, f32[2312,128]{1,0:T(8,128)}) custom-call(f32[3472,128]{1,0:T(8,128)} %pad_maximum_fusion.masters_in, bf16[1024,768]{1,0:T(8,128)(2,1)} %tok_in.1, bf16[1024,768]{1,0:T(8,128)(2,1)} %cot_in.1, s32[2,512]{1,0:T(2,128)} %segs.1, s32[1]{0:T(128)S(6)} %copy.22.live_count), custom_call_target="tpu_custom_call" | custom-call | tf_op jit(solution)/shard_map/layer/pallas_call | solution.py:1691
  187.6 0.0 copy-start.1
  187.6 0.0 copy-start.4
  187.6 0.0 copy-start.5
  187.6 0.0 copy-start.6
  187.6 3.3 %multiply_add_fusion.2 = (f32[147696]{0:T(1024)}, f32[147696]{0:T(1024)}, f32[147696]{0:T(1024)}, f32[147696]{0:T(1024)}) fusion(f32[147696]{0:T(1024)} %param.14, f32[147696]{0:T(1024)} %param.16, f32[147696]{0:T(1024)} %param.15, f32[148480]{0:T(1024)} %bitcast.7), kind=kLoop, calls=%fused_computation.8 | loop fusion | flops 1920048 | bytes 4726272 | tf_op jit(solution)/shard_map/add | solution.py:128
  190.9 0.0 copy-done.1
  190.9 0.0 copy-done.4
  190.9 0.0 copy-done.5
  190.9 0.2 copy-done.6
  191.1 0.0 copy-start.3
  191.1 2.5 %multiply_add_fusion = (f32[295248]{0:T(1024)}, f32[295248]{0:T(1024)}, f32[295248]{0:T(1024)}, f32[295248]{0:T(1024)}) fusion(f32[295248]{0:T(1024)S(1)} %copy-done.1, f32[295248]{0:T(1024)S(1)} %copy-done.4, f32[295248]{0:T(1024)S(1)} %copy-done.5, f32[295936]{0:T(1024)S(1)} %bitcast.6), kind=kLoop, calls=%fused_computation.3 | loop fusion | flops 3838224 | bytes 9447936 | tf_op jit(solution)/shard_map/add | solution.py:128
  193.7 0.0 copy-done.3
  193.7 0.0 copy-start.2
  193.7 1.1 copy.23
  194.8 0.8 copy-done.2
  195.6 1.1 copy.24
Async XLA Ops:
  0.6 1.9 copy-start
  187.6 3.3 %copy-start.1 = (f32[295248]{0:T(1024)S(1)}, f32[295248]{0:T(1024)}, u32[]{:S(2)}) copy-start(f32[295248]{0:T(1024)} %param.17) | copy-start | bytes 3542980
  187.6 3.3 %copy-start.4 = (f32[295248]{0:T(1024)S(1)}, f32[295248]{0:T(1024)}, u32[]{:S(2)}) copy-start(f32[295248]{0:T(1024)} %param.19) | copy-start | bytes 3542980
  187.6 3.3 %copy-start.5 = (f32[295248]{0:T(1024)S(1)}, f32[295248]{0:T(1024)}, u32[]{:S(2)}) copy-start(f32[295248]{0:T(1024)} %param.18) | copy-start | bytes 3542980
  187.6 3.5 %copy-start.6 = (f32[2312,128]{1,0:T(8,128)S(1)}, f32[2312,128]{1,0:T(8,128)}, u32[]{:S(2)}) copy-start(f32[2312,128]{1,0:T(8,128)} %get-tuple-element.17) | copy-start | bytes 3551236
  191.1 2.5 %copy-start.3 = (bf16[1024,768]{1,0:T(8,128)(2,1)S(1)}, bf16[1024,768]{1,0:T(8,128)(2,1)}, u32[]{:S(2)}) copy-start(bf16[1024,768]{1,0:T(8,128)(2,1)} %get-tuple-element.36) | copy-start | bytes 4718596
  193.7 2.0 %copy-start.2 = (bf16[1024,768]{1,0:T(8,128)(2,1)S(1)}, bf16[1024,768]{1,0:T(8,128)(2,1)}, u32[]{:S(2)}) copy-start(bf16[1024,768]{1,0:T(8,128)(2,1)} %get-tuple-element.37) | copy-start | bytes 4718596
